TPU v7x, 32 devices: a whole 2x2x4 slice. The times are simulated.
32 devices in a mesh: member: 4 (over z), region: 8 (over y, x, core).
Axes of the slice: x: 2, y: 2, z: 4, core: 2. Of those that a mesh axis runs over, the one named last changes fastest.
Arguments:
- grid_input: bfloat16 [16, 4096, 1024], P('member', 'region'), may hold values from -6 to 6
- w_hidden: bfloat16 [1024, 1024], replicated, may hold values from -0.1875 to 0.1875
- b_hidden: float32 [1024], replicated, may hold values from -3 to 3
- w_out: bfloat16 [1024, 96], replicated, may hold values from -0.1875 to 0.1875
- b_out: float32 [96], replicated, may hold values from -3 to 3
- target: float32 [96, 4096], P(None, 'region'), may hold values from -6 to 6
- channel_weight: float32 [96], replicated, may hold values from 0.5 to 5
- interp_weight: bfloat16 [32, 3, 128, 128], P('region'), may hold values from -0.5 to 0.5
- block_index: int32 [32, 3], P('region'), may hold values from 0 to 15, as said below
Outputs:
- grad_w_hidden: float32 [1024, 1024], P(('member', 'region'))
- grad_w_out: float32 [1024, 96], P(('member', 'region'))
- grad_mesh: float32 [16, 2048, 1024], P('member', 'region')
Inputs may be any that keep to these rules, and one draw needn't show every extreme that they name: `block_index`: grid block b lies in region b // 4; its mesh blocks belong to that region or to one of its two neighbours along the region index, cyclically, a block j belonging to region j // 2. For k = 0 the mesh block is the region's own block number (b % 4) % 2.
All inputs are finite; a program needn't handle non-finite values.
Results may differ from a plain program's by a relative error of at most 0.0095.
Values may be sent and summed in bfloat16 or wider, within the bound.
No kernel may reach another device: no remote copies, remote signals or barrier semaphores. Data moves between devices by JAX's collectives and lax.ppermute only.
A program may use at most 128 MiB of HBM per device.

v0:
```python
import jax
import jax.numpy as jnp
from jax import lax
from jax.sharding import PartitionSpec as P

GB = 128
MB = 128
K = 3
GBLK_REG = 4
MBLK_REG = 2


ALPHA = 0.95
SMOOTH = 0.25


def shifted(block, axis, distance):
    devices = range(lax.axis_size(axis))
    route = [((i - distance) % len(devices), i) for i in devices]
    return lax.ppermute(block, axis, route)


def smooth_slope(diff):
    return diff / jnp.sqrt(diff * diff + SMOOTH * SMOOTH)


def ensemble_adjoint(own, every, target_cells, channel_weight):
    members = every.shape[0]
    kappa = ALPHA / (2.0 * members * (members - 1)) + (1.0 - ALPHA) / (2.0 * members * members)
    skill = smooth_slope(own - target_cells[None]) / members
    spread = jnp.sum(smooth_slope(own[:, None] - every[None, :]), axis=1)
    return channel_weight[None, :, None] * (skill - 2.0 * kappa * spread)


def body(
    grid_input, w_hidden, b_hidden, w_out, b_out, target, channel_weight, interp_weight, block_index
):
    members_here = grid_input.shape[0]
    cells_here = grid_input.shape[1]
    width = grid_input.shape[2]
    channels = w_out.shape[1]
    flat_input = grid_input.reshape(members_here * cells_here, width)
    pre_act = jnp.dot(flat_input, w_hidden, preferred_element_type=jnp.float32) + b_hidden
    activated = jax.nn.silu(pre_act).astype(jnp.bfloat16)
    predicted = jnp.dot(activated, w_out, preferred_element_type=jnp.float32) + b_out
    pred_cols = predicted.reshape(members_here, cells_here, channels).transpose(0, 2, 1)
    cell_slices = lax.all_to_all(pred_cols, "member", split_axis=2, concat_axis=0, tiled=True)
    slice_len = cell_slices.shape[2]
    slice_start = lax.axis_index("member") * slice_len
    target_slice = lax.dynamic_slice_in_dim(target, slice_start, slice_len, 1)
    adjoint = ensemble_adjoint(cell_slices, cell_slices, target_slice, channel_weight).astype(
        jnp.bfloat16
    )
    adjoint_cols = lax.all_to_all(adjoint, "member", split_axis=0, concat_axis=2, tiled=True)
    dpred = adjoint_cols.transpose(0, 2, 1).reshape(members_here * cells_here, channels)
    dact = jnp.dot(dpred, w_out.T, preferred_element_type=jnp.float32)
    logistic = jax.nn.sigmoid(pre_act)
    dpre = (dact * logistic * (1.0 + pre_act * (1.0 - logistic))).astype(jnp.bfloat16)
    hidden_term = lax.dot_general(
        flat_input, dpre, (((0,), (0,)), ((), ())), preferred_element_type=jnp.float32
    )
    output_term = lax.dot_general(
        activated, dpred, (((0,), (0,)), ((), ())), preferred_element_type=jnp.float32
    )
    partial_sums = lax.psum_scatter(
        jnp.concatenate([hidden_term, output_term], axis=1).astype(jnp.bfloat16),
        "member",
        scatter_dimension=0,
        tiled=True,
    )
    summed = lax.psum_scatter(partial_sums, "region", scatter_dimension=0, tiled=True).astype(
        jnp.float32
    )
    grad_w_hidden = summed[:, :width]
    grad_w_out = summed[:, width:]
    dinput = jnp.dot(dpre, w_hidden.T, preferred_element_type=jnp.float32).astype(jnp.bfloat16)
    dinput_blocks = dinput.reshape(members_here, GBLK_REG, GB, width)
    region_now = lax.axis_index("region")
    region_count = lax.axis_size("region")
    owner = block_index // MBLK_REG
    relative = (owner - region_now + 1 + region_count) % region_count
    target_slots = (relative * MBLK_REG + block_index % MBLK_REG).reshape(-1)
    buffer = jnp.zeros((members_here, 3 * MBLK_REG, MB, width), jnp.float32)

    def add_block(pair_pos, accum):
        block_pos = pair_pos // K
        source_pos = pair_pos % K
        weight_tile = lax.dynamic_index_in_dim(
            lax.dynamic_index_in_dim(interp_weight, block_pos, 0, False), source_pos, 0, False
        )
        block_rows = lax.dynamic_index_in_dim(dinput_blocks, block_pos, 1, False)
        contrib = jnp.einsum(
            "gn,mgh->mnh", weight_tile, block_rows, preferred_element_type=jnp.float32
        )
        target_slot = lax.dynamic_index_in_dim(target_slots, pair_pos, 0, False)
        current = lax.dynamic_index_in_dim(accum, target_slot, 1, False)
        return lax.dynamic_update_index_in_dim(accum, current + contrib, target_slot, 1)

    buffer = lax.fori_loop(0, GBLK_REG * K, add_block, buffer)
    from_above = shifted(buffer[:, :MBLK_REG], "region", -1)
    from_below = shifted(buffer[:, 2 * MBLK_REG :].astype(jnp.bfloat16), "region", 1).astype(
        jnp.float32
    )
    own_terms = buffer[:, MBLK_REG : 2 * MBLK_REG] + from_above + from_below
    grad_mesh = own_terms.reshape(members_here, MBLK_REG * MB, width)
    return (grad_w_hidden, grad_w_out, grad_mesh)


def solution(mesh):
    placed = (
        P("member", "region", None),
        P(),
        P(),
        P(),
        P(),
        P(None, "region"),
        P(),
        P("region", None, None, None),
        P("region", None),
    )
    return jax.shard_map(
        body,
        mesh=mesh,
        in_specs=placed,
        out_specs=(
            P(("member", "region"), None),
            P(("member", "region"), None),
            P("member", "region", None),
        ),
        check_vma=False,
    )
```

profile of v0, /device:TPU:3, one launch (start us, length us, event | category | flops | bytes accessed | tf_op | source)
XLA Modules:
  0.0 294.6 jit_solution(8047896098288263430)
XLA Ops:
  7.2 1.6 copy-done
  8.8 10.3 %multiply_convert_fusion.1 = (bf16[2048,1024]{1,0:T(8,128)(2,1)S(1)}, f32[2048,1024]{1,0:T(8,128)}) fusion(f32[1024]{0:T(1024)} %param.13, bf16[2048,1024]{1,0:T(8,128)(2,1)} %bitcast.74, bf16[1024,1024]{1,0:T(8,128)(2,1)S(1)} %copy-done), kind=kOutput, calls=%fused_computation.14 | convolution fusion | flops 4307550208 | bytes 18878464 | tf_op jit(solution)/shard_map/dot_general | solution.py:43
  19.1 2.0 copy-done.2
  23.9 2.3 copy.39
  26.2 4.6 %all-to-all-start = ((f32[4,96,512]{1,0,2:T(4,128)}), f32[4,96,512]{1,0,2:T(4,128)S(1)}, u32[]{:S(2)}, u32[]{:S(2)}) async-start(f32[4,96,512]{1,0,2:T(4,128)} %bitcast.66), calls=%async_computation | async-start | bytes 2097152 | tf_op jit(solution)/shard_map/all_to_all | solution.py:47
  31.6 24.4 %all-to-all-done = f32[4,96,512]{1,0,2:T(4,128)S(1)} async-done(((f32[4,96,512]{1,0,2:T(4,128)}), f32[4,96,512]{1,0,2:T(4,128)S(1)}, u32[]{:S(2)}, u32[]{:S(2)}) %all-to-all-start) | async-done | bytes 786464 | tf_op jit(solution)/shard_map/all_to_all | solution.py:47
  57.3 4.0 %fusion.7 = f32[16,96,128]{2,1,0:T(8,128)S(1)} fusion(f32[16,96,128]{2,1,0:T(8,128)} %bitcast.68), kind=kLoop, calls=%fused_computation.12 | loop fusion | flops 15532032 | bytes 1572864 | tf_op jit(solution)/shard_map/reduce_sum | solution.py:31
  62.4 3.6 %all-to-all-start.1 = ((bf16[16,96,128]{2,1,0:T(8,128)(2,1)}), bf16[16,96,128]{2,1,0:T(8,128)(2,1)S(1)}, u32[]{:S(2)}, u32[]{:S(2)}) async-start(bf16[16,96,128]{2,1,0:T(8,128)(2,1)} %multiply_convert_fusion.2), calls=%async_computation.1 | async-start | bytes 786432 | tf_op jit(solution)/shard_map/all_to_all | solution.py:54
  66.4 9.4 %all-to-all-done.1 = bf16[16,96,128]{2,1,0:T(8,128)(2,1)S(1)} async-done(((bf16[16,96,128]{2,1,0:T(8,128)(2,1)}), bf16[16,96,128]{2,1,0:T(8,128)(2,1)S(1)}, u32[]{:S(2)}, u32[]{:S(2)}) %all-to-all-start.1) | async-done | bytes 393248 | tf_op jit(solution)/shard_map/all_to_all | solution.py:54
  76.3 3.0 %convolution_convert_fusion.1 = bf16[1024,96]{0,1:T(8,128)(2,1)S(1)} fusion(bf16[2048,96]{0,1:T(8,128)(2,1)S(1)} %bitcast.70, bf16[2048,1024]{1,0:T(8,128)(2,1)} %copy-done.2), kind=kOutput, calls=%fused_computation.22 | convolution fusion | flops 402751488 | bytes 4784128 | tf_op jit(solution)/shard_map/dot_general | solution.py:62
  79.4 6.0 %multiply_convert_fusion = bf16[2048,1024]{1,0:T(8,128)(2,1)S(1)} fusion(f32[2048,1024]{1,0:T(8,128)} %get-tuple-element.215, bf16[2048,96]{0,1:T(8,128)(2,1)S(1)} %bitcast.71, bf16[1024,96]{0,1:T(8,128)(2,1)S(1)} %copy-done.4, f32[1024]{0:T(1024)S(1)} %copy-done.9), kind=kOutput, calls=%fused_computation.13 | convolution fusion | flops 423624704 | bytes 13176832 | tf_op jit(solution)/shard_map/dot_general | solution.py:56
  85.4 4.8 %convert_bitcast_fusion = bf16[1024,1024]{0,1:T(8,128)(2,1)S(1)} fusion(bf16[2048,1024]{1,0:T(8,128)(2,1)S(1)} %multiply_convert_fusion, bf16[2048,1024]{1,0:T(8,128)(2,1)S(1)} %bitcast.75), kind=kOutput, calls=%fused_computation.21 | convolution fusion | flops 4296015872 | bytes 10485760 | tf_op jit(solution)/shard_map/dot_general | solution.py:59
  90.2 6.3 %convolution_convert_fusion = bf16[2048,1024]{1,0:T(8,128)(2,1)} fusion(bf16[2048,1024]{1,0:T(8,128)(2,1)S(1)} %multiply_convert_fusion, bf16[1024,1024]{1,0:T(8,128)(2,1)S(1)} %copy-done), kind=kOutput, calls=%fused_computation.18 | convolution fusion | flops 4297064448 | bytes 10485760 | tf_op jit(solution)/shard_map/dot_general | solution.py:76
  96.4 1.6 pad_maximum_fusion
  98.1 5.9 %broadcast_in_dim.21 = f32[4,6,128,1024]{2,3,0,1:T(8,128)} broadcast(f32[]{:T(128)} %constant.224.clone.1), dimensions={} | broadcast | bytes 12582916 | tf_op jit(solution)/shard_map/broadcast_in_dim | solution.py:83
  104.0 88.5 %while.16 = (s32[]{:T(128)}, f32[4,6,128,1024]{2,3,0,1:T(8,128)}, s32[12]{0:T(128)S(1)}, bf16[4,4,128,1024]{3,2,1,0:T(8,128)(2,1)}, bf16[4,3,128,128]{3,2,1,0:T(...) while((s32[]{:T(128)}, f32[4,6,128,1024]{2,3,0,1:T(8,128)}, ...), condition=%wide.region_4.5_spmd, body=%wide.region_3.4_spmd.sunk | while | flops 134742048 | bytes 9470358 | solution.py:99
  106.6 1.7 constant_dynamic-slice_fusion.3
  108.4 3.1 %bitcast_dynamic-update-slice_fusion.2 = f32[4,6,128,1024]{2,3,0,1:T(8,128)} fusion(f32[4,6,128,1024]{2,3,0,1:T(8,128)} %get-tuple-element.260, s32[]{:T(128)S(6)} %select_n.135, f32[4,1,128,1024]{2,3,0,1:T(8,128)S(1)} %constant_dynamic-slice_fusion.3, bf16[4,4,128,1024]{3,2,1,0:T(8,128)(2,1)} %get-tuple-element.274, s32[]{:T(128)S(6)} %select_n.137, ...), kind=kOutput, calls=%fused_computation.clone.1 | convolution fusion | flops 134742016 | bytes 5275664 | tf_op jit(solution)/shard_map/while/body/eval_jaxpr/gn,mgh->mnh/dot_general | solution.py:92
  113.9 1.7 constant_dynamic-slice_fusion.3
  115.7 3.1 %bitcast_dynamic-update-slice_fusion.2 = f32[4,6,128,1024]{2,3,0,1:T(8,128)} fusion(f32[4,6,128,1024]{2,3,0,1:T(8,128)} %get-tuple-element.260, s32[]{:T(128)S(6)} %select_n.135, f32[4,1,128,1024]{2,3,0,1:T(8,128)S(1)} %constant_dynamic-slice_fusion.3, bf16[4,4,128,1024]{3,2,1,0:T(8,128)(2,1)} %get-tuple-element.274, s32[]{:T(128)S(6)} %select_n.137, ...), kind=kOutput, calls=%fused_computation.clone.1 | convolution fusion | flops 134742016 | bytes 5275664 | tf_op jit(solution)/shard_map/while/body/eval_jaxpr/gn,mgh->mnh/dot_general | solution.py:92
  121.3 1.8 constant_dynamic-slice_fusion.3
  123.1 3.0 %bitcast_dynamic-update-slice_fusion.2 = f32[4,6,128,1024]{2,3,0,1:T(8,128)} fusion(f32[4,6,128,1024]{2,3,0,1:T(8,128)} %get-tuple-element.260, s32[]{:T(128)S(6)} %select_n.135, f32[4,1,128,1024]{2,3,0,1:T(8,128)S(1)} %constant_dynamic-slice_fusion.3, bf16[4,4,128,1024]{3,2,1,0:T(8,128)(2,1)} %get-tuple-element.274, s32[]{:T(128)S(6)} %select_n.137, ...), kind=kOutput, calls=%fused_computation.clone.1 | convolution fusion | flops 134742016 | bytes 5275664 | tf_op jit(solution)/shard_map/while/body/eval_jaxpr/gn,mgh->mnh/dot_general | solution.py:92
  128.7 1.7 constant_dynamic-slice_fusion.3
  130.5 3.1 %bitcast_dynamic-update-slice_fusion.2 = f32[4,6,128,1024]{2,3,0,1:T(8,128)} fusion(f32[4,6,128,1024]{2,3,0,1:T(8,128)} %get-tuple-element.260, s32[]{:T(128)S(6)} %select_n.135, f32[4,1,128,1024]{2,3,0,1:T(8,128)S(1)} %constant_dynamic-slice_fusion.3, bf16[4,4,128,1024]{3,2,1,0:T(8,128)(2,1)} %get-tuple-element.274, s32[]{:T(128)S(6)} %select_n.137, ...), kind=kOutput, calls=%fused_computation.clone.1 | convolution fusion | flops 134742016 | bytes 5275664 | tf_op jit(solution)/shard_map/while/body/eval_jaxpr/gn,mgh->mnh/dot_general | solution.py:92
  136.1 1.8 constant_dynamic-slice_fusion.3
  137.9 3.0 %bitcast_dynamic-update-slice_fusion.2 = f32[4,6,128,1024]{2,3,0,1:T(8,128)} fusion(f32[4,6,128,1024]{2,3,0,1:T(8,128)} %get-tuple-element.260, s32[]{:T(128)S(6)} %select_n.135, f32[4,1,128,1024]{2,3,0,1:T(8,128)S(1)} %constant_dynamic-slice_fusion.3, bf16[4,4,128,1024]{3,2,1,0:T(8,128)(2,1)} %get-tuple-element.274, s32[]{:T(128)S(6)} %select_n.137, ...), kind=kOutput, calls=%fused_computation.clone.1 | convolution fusion | flops 134742016 | bytes 5275664 | tf_op jit(solution)/shard_map/while/body/eval_jaxpr/gn,mgh->mnh/dot_general | solution.py:92
  143.5 1.7 constant_dynamic-slice_fusion.3
  145.3 3.1 %bitcast_dynamic-update-slice_fusion.2 = f32[4,6,128,1024]{2,3,0,1:T(8,128)} fusion(f32[4,6,128,1024]{2,3,0,1:T(8,128)} %get-tuple-element.260, s32[]{:T(128)S(6)} %select_n.135, f32[4,1,128,1024]{2,3,0,1:T(8,128)S(1)} %constant_dynamic-slice_fusion.3, bf16[4,4,128,1024]{3,2,1,0:T(8,128)(2,1)} %get-tuple-element.274, s32[]{:T(128)S(6)} %select_n.137, ...), kind=kOutput, calls=%fused_computation.clone.1 | convolution fusion | flops 134742016 | bytes 5275664 | tf_op jit(solution)/shard_map/while/body/eval_jaxpr/gn,mgh->mnh/dot_general | solution.py:92
  150.9 1.7 constant_dynamic-slice_fusion.3
  152.7 3.1 %bitcast_dynamic-update-slice_fusion.2 = f32[4,6,128,1024]{2,3,0,1:T(8,128)} fusion(f32[4,6,128,1024]{2,3,0,1:T(8,128)} %get-tuple-element.260, s32[]{:T(128)S(6)} %select_n.135, f32[4,1,128,1024]{2,3,0,1:T(8,128)S(1)} %constant_dynamic-slice_fusion.3, bf16[4,4,128,1024]{3,2,1,0:T(8,128)(2,1)} %get-tuple-element.274, s32[]{:T(128)S(6)} %select_n.137, ...), kind=kOutput, calls=%fused_computation.clone.1 | convolution fusion | flops 134742016 | bytes 5275664 | tf_op jit(solution)/shard_map/while/body/eval_jaxpr/gn,mgh->mnh/dot_general | solution.py:92
  158.3 1.7 constant_dynamic-slice_fusion.3
  160.0 3.0 %bitcast_dynamic-update-slice_fusion.2 = f32[4,6,128,1024]{2,3,0,1:T(8,128)} fusion(f32[4,6,128,1024]{2,3,0,1:T(8,128)} %get-tuple-element.260, s32[]{:T(128)S(6)} %select_n.135, f32[4,1,128,1024]{2,3,0,1:T(8,128)S(1)} %constant_dynamic-slice_fusion.3, bf16[4,4,128,1024]{3,2,1,0:T(8,128)(2,1)} %get-tuple-element.274, s32[]{:T(128)S(6)} %select_n.137, ...), kind=kOutput, calls=%fused_computation.clone.1 | convolution fusion | flops 134742016 | bytes 5275664 | tf_op jit(solution)/shard_map/while/body/eval_jaxpr/gn,mgh->mnh/dot_general | solution.py:92
  165.6 1.7 constant_dynamic-slice_fusion.3
  167.4 3.0 %bitcast_dynamic-update-slice_fusion.2 = f32[4,6,128,1024]{2,3,0,1:T(8,128)} fusion(f32[4,6,128,1024]{2,3,0,1:T(8,128)} %get-tuple-element.260, s32[]{:T(128)S(6)} %select_n.135, f32[4,1,128,1024]{2,3,0,1:T(8,128)S(1)} %constant_dynamic-slice_fusion.3, bf16[4,4,128,1024]{3,2,1,0:T(8,128)(2,1)} %get-tuple-element.274, s32[]{:T(128)S(6)} %select_n.137, ...), kind=kOutput, calls=%fused_computation.clone.1 | convolution fusion | flops 134742016 | bytes 5275664 | tf_op jit(solution)/shard_map/while/body/eval_jaxpr/gn,mgh->mnh/dot_general | solution.py:92
  172.9 1.7 constant_dynamic-slice_fusion.3
  174.7 3.1 %bitcast_dynamic-update-slice_fusion.2 = f32[4,6,128,1024]{2,3,0,1:T(8,128)} fusion(f32[4,6,128,1024]{2,3,0,1:T(8,128)} %get-tuple-element.260, s32[]{:T(128)S(6)} %select_n.135, f32[4,1,128,1024]{2,3,0,1:T(8,128)S(1)} %constant_dynamic-slice_fusion.3, bf16[4,4,128,1024]{3,2,1,0:T(8,128)(2,1)} %get-tuple-element.274, s32[]{:T(128)S(6)} %select_n.137, ...), kind=kOutput, calls=%fused_computation.clone.1 | convolution fusion | flops 134742016 | bytes 5275664 | tf_op jit(solution)/shard_map/while/body/eval_jaxpr/gn,mgh->mnh/dot_general | solution.py:92
  180.3 1.7 constant_dynamic-slice_fusion.3
  182.1 3.0 %bitcast_dynamic-update-slice_fusion.2 = f32[4,6,128,1024]{2,3,0,1:T(8,128)} fusion(f32[4,6,128,1024]{2,3,0,1:T(8,128)} %get-tuple-element.260, s32[]{:T(128)S(6)} %select_n.135, f32[4,1,128,1024]{2,3,0,1:T(8,128)S(1)} %constant_dynamic-slice_fusion.3, bf16[4,4,128,1024]{3,2,1,0:T(8,128)(2,1)} %get-tuple-element.274, s32[]{:T(128)S(6)} %select_n.137, ...), kind=kOutput, calls=%fused_computation.clone.1 | convolution fusion | flops 134742016 | bytes 5275664 | tf_op jit(solution)/shard_map/while/body/eval_jaxpr/gn,mgh->mnh/dot_general | solution.py:92
  187.7 1.7 constant_dynamic-slice_fusion.3
  189.4 3.0 %bitcast_dynamic-update-slice_fusion.2 = f32[4,6,128,1024]{2,3,0,1:T(8,128)} fusion(f32[4,6,128,1024]{2,3,0,1:T(8,128)} %get-tuple-element.260, s32[]{:T(128)S(6)} %select_n.135, f32[4,1,128,1024]{2,3,0,1:T(8,128)S(1)} %constant_dynamic-slice_fusion.3, bf16[4,4,128,1024]{3,2,1,0:T(8,128)(2,1)} %get-tuple-element.274, s32[]{:T(128)S(6)} %select_n.137, ...), kind=kOutput, calls=%fused_computation.clone.1 | convolution fusion | flops 134742016 | bytes 5275664 | tf_op jit(solution)/shard_map/while/body/eval_jaxpr/gn,mgh->mnh/dot_general | solution.py:92
  192.5 4.5 %slice.19 = f32[4,2,128,1024]{2,3,0,1:T(8,128)} slice(f32[4,6,128,1024]{2,3,0,1:T(8,128)} %get-tuple-element.163), slice={[0:4], [0:2], [0:128], [0:1024]} | slice | bytes 8388608 | tf_op jit(solution)/shard_map/slice | solution.py:100
  197.0 2.8 collective-permute-start
  199.8 2.5 slice.26
  203.7 2.1 copy.50
  205.8 45.7 %collective-permute-done.1 = bf16[4,2,128,1024]{2,3,0,1:T(8,128)(2,1)} collective-permute-done((bf16[4,2,128,1024]{2,3,0,1:T(8,128)(2,1)S(1)}, bf16[4,2,128,1024]{2,3,0,1:T(8,128)(2,1)}, u32[]{:S(2)}, u32[]{:S(2)}) %collective-permute-start.1) | collective-permute-done | bytes 2097184 | tf_op jit(solution)/shard_map/ppermute | solution.py:20
  251.5 20.9 %collective-permute-done = f32[4,2,128,1024]{2,3,0,1:T(8,128)} collective-permute-done((f32[4,2,128,1024]{2,3,0,1:T(8,128)}, f32[4,2,128,1024]{2,3,0,1:T(8,128)}, u32[]{:S(2)}, u32[]{:S(2)}) %collective-permute-start) | collective-permute-done | bytes 4194336 | tf_op jit(solution)/shard_map/ppermute | solution.py:20
  272.4 6.7 %convert_add_fusion = f32[4,2,128,1024]{2,3,0,1:T(8,128)} fusion(bf16[4,2,128,1024]{2,3,0,1:T(8,128)(2,1)} %collective-permute-done.1, f32[4,2,128,1024]{2,3,0,1:T(8,128)} %collective-permute-done, f32[4,6,128,1024]{2,3,0,1:T(8,128)} %get-tuple-element.163), kind=kLoop, calls=%fused_computation.17 | loop fusion | flops 3145728 | bytes 14680064 | tf_op jit(solution)/shard_map/add | solution.py:104
  279.1 5.3 %copy.45 = f32[4,2,128,1024]{3,2,1,0:T(8,128)} copy(f32[4,2,128,1024]{2,3,0,1:T(8,128)} %convert_add_fusion) | data formatting | bytes 8388608 | tf_op jit(solution)/shard_map/add | solution.py:104
  (53 shorter events, 18.6 us)
Async XLA Ops:
  7.2 1.6 copy-start
  8.8 12.3 %copy-start.4 = (bf16[1024,96]{0,1:T(8,128)(2,1)S(1)}, bf16[1024,96]{0,1:T(8,128)(2,1)}, u32[]{:S(2)}) copy-start(bf16[1024,96]{0,1:T(8,128)(2,1)} %param.14) | copy-start | bytes 589828
  8.8 12.3 %copy-start.6 = (f32[96]{0:T(128)S(1)}, f32[96]{0:T(128)}, u32[]{:S(2)}) copy-start(f32[96]{0:T(128)} %param.15) | copy-start | bytes 1156
  19.1 2.0 copy-start.2
  26.2 29.8 %all-to-all-start = ((f32[4,96,512]{1,0,2:T(4,128)}), f32[4,96,512]{1,0,2:T(4,128)S(1)}, u32[]{:S(2)}, u32[]{:S(2)}) async-start(f32[4,96,512]{1,0,2:T(4,128)} %bitcast.66), calls=%async_computation | async-start | bytes 2097152 | tf_op jit(solution)/shard_map/all_to_all | solution.py:47
  30.8 30.6 %copy-start.7 = (f32[96]{0:T(128)S(1)}, f32[96]{0:T(128)}, u32[]{:S(2)}) copy-start(f32[96]{0:T(128)} %param.17) | copy-start | bytes 1156
  57.3 4.0 %copy-start.3 = (f32[4,4,96,128]{3,2,1,0:T(8,128)S(1)}, f32[4,4,96,128]{3,2,1,0:T(8,128)}, u32[]{:S(2)}) copy-start(f32[4,4,96,128]{3,2,1,0:T(8,128)} %copy.41) | copy-start | bytes 2359300
  57.3 8.9 %copy-start.5 = (s32[4,3]{1,0:T(4,128)S(1)}, s32[4,3]{1,0:T(4,128)}, u32[]{:S(2)}) copy-start(s32[4,3]{1,0:T(4,128)} %param.19) | copy-start | bytes 148
  62.4 16.9 %copy-start.9 = (f32[1024]{0:T(1024)S(1)}, f32[1024]{0:T(1024)}, u32[]{:S(2)}) copy-start(f32[1024]{0:T(1024)} %param.13) | copy-start | bytes 12292
  62.4 13.4 %all-to-all-start.1 = ((bf16[16,96,128]{2,1,0:T(8,128)(2,1)}), bf16[16,96,128]{2,1,0:T(8,128)(2,1)S(1)}, u32[]{:S(2)}, u32[]{:S(2)}) async-start(bf16[16,96,128]{2,1,0:T(8,128)(2,1)} %multiply_convert_fusion.2), calls=%async_computation.1 | async-start | bytes 786432 | tf_op jit(solution)/shard_map/all_to_all | solution.py:54
  66.0 137.6 %reduce-scatter.5.cloned.1.call-start = ((), (), s32[]{:S(2)}) async-start(), calls=%async_computation.4 | async-start | bytes 2867200 | tf_op jit(solution)/shard_map/reduce_scatter | solution.py:65
  79.4 6.0 %copy-start.8 = (bf16[4,512,1024]{2,1,0:T(8,128)(2,1)S(1)}, bf16[4,512,1024]{2,1,0:T(8,128)(2,1)}, u32[]{:S(2)}) copy-start(bf16[4,512,1024]{2,1,0:T(8,128)(2,1)} %param.11) | copy-start | bytes 12582916
  98.0 186.4 %reduce-scatter.7.cloned.1.call-start = ((), (), s32[]{:S(2)}) async-start(), calls=%async_computation.5 | async-start | bytes 663552
  197.0 75.4 %collective-permute-start = (f32[4,2,128,1024]{2,3,0,1:T(8,128)}, f32[4,2,128,1024]{2,3,0,1:T(8,128)}, u32[]{:S(2)}, u32[]{:S(2)}) collective-permute-start(f32[4,2,128,1024]{2,3,0,1:T(8,128)} %slice.19), channel_id=1, source_target_pairs={{1,0},{2,1},{3,2},{4,3},{5,4},{6,5},{7,6},{0,7},{9,8},{10,9},{11,1... | collective-permute-start | bytes 12582920 | tf_op jit(solution)/shard_map/ppermute | solution.py:20
  202.4 49.2 %collective-permute-start.1 = (bf16[4,2,128,1024]{2,3,0,1:T(8,128)(2,1)S(1)}, bf16[4,2,128,1024]{2,3,0,1:T(8,128)(2,1)}, u32[]{:S(2)}, u32[]{:S(2)}) collective-permute-start(bf16[4,2,128,1024]{2,3,0,1:T(8,128)(2,1)S(1)} %slice.26), channel_id=1, source_target_pairs={{7,0},{0,1},{1,2},{2,3},{3,4},{4,5},{5,6},{6,7},{15,8},{8,9},{9,10... | collective-permute-start | bytes 6291464 | tf_op jit(solution)/shard_map/ppermute | solution.py:20
  272.4 15.4 %copy-start.1 = (bf16[1024,1024]{1,0:T(8,128)(2,1)S(1)}, bf16[1024,1024]{1,0:T(8,128)(2,1)}, u32[]{:S(2)}) copy-start(bf16[1024,1024]{1,0:T(8,128)(2,1)} %param.12) | copy-start | bytes 6291460
Sparse Core Ops, SparseCore 0:
  98.1 48.0 reduce-scatter.4
  205.9 34.1 reduce-scatter.6
where the time goes:
time: 297 us; the launch traced here: 295 us
  waiting for transfers between devices  101 us (34%)
  matrix products  68.4 us (23%)
  local copies, waits for them, and re-layouts  61.7 us (21%)
  loops' own time  23.9 us (8%)
  between operations  14.2 us (5%)
  other arithmetic  13.3 us (4%)
  starting transfers between devices  12.6 us (4%)
    ppermute x2, waiting for transfers between devices, shifted(): return lax.ppermute(block, axis, route)  66.6 us
    dot_general x12, matrix products, add_block(): jnp.einsum('gn,mgh->mnh', weight_tile, block_rows, preferred_element_type...  36.7 us
    all_to_all x1, waiting for transfers between devices, body(): lax.all_to_all(pred_cols, 'member', split_axis=2, concat_axis=0, tiled=True)  24.4 us
    another operation x1, loops' own time, body(): buffer = lax.fori_loop(0, GBLK_REG * K, add_block, buffer)  23.9 us
    dynamic_slice x12, local copies, waits for them, and re-layouts, add_block(): current = lax.dynamic_index_in_dim(accum, target_slot, 1, False)  20.9 us
    dot_general x1, matrix products, body(): jnp.dot(flat_input, w_hidden, preferred_element_type=jnp.float32) + b_hidden  10.3 us
    all_to_all x1, waiting for transfers between devices, body(): lax.all_to_all(adjoint, 'member', split_axis=0, concat_axis=2, tiled=True)  9.45 us
    unnamed x25, local copies, waits for them, and re-layouts  7.55 us
  transfers between devices with their start and end apart: 6, of which 4 were waited for; matrix products, arithmetic and copies ran while one was open for 31% of the time, Pallas kernels for 0%

commit v1 on v0

v1 whole, which is shorter than its diff:
```python
import functools

import jax
import jax.numpy as jnp
from jax import lax
from jax.experimental import pallas as pl
from jax.experimental.pallas import tpu as pltpu
from jax.sharding import PartitionSpec as P

ALPHA = 0.95
SMOOTH = 0.25
MBLK_REG = 2
PER = 1
SCOPED = 16 * 1024 * 1024
F32 = jnp.float32
BF16 = jnp.bfloat16
ON_VMEM = pl.BlockSpec(memory_space=pltpu.VMEM)
ON_HBM = pl.BlockSpec(memory_space=pltpu.HBM)
ON_SMEM = pl.BlockSpec(memory_space=pltpu.SMEM)
ANYWHERE = pl.BlockSpec(memory_space=pl.ANY)


def shifted(block, axis, distance):
    count = lax.axis_size(axis)
    return lax.ppermute(block, axis, [((i - distance) % count, i) for i in range(count)])


def exchanged(block, axis, bit):
    count = lax.axis_size(axis)
    return lax.ppermute(block, axis, [(i, i ^ bit) for i in range(count)])


def smooth_slope(diff):
    return diff * lax.rsqrt(diff * diff + SMOOTH * SMOOTH)


def params():
    return pltpu.CompilerParams(vmem_limit_bytes=SCOPED)


def cost(flops, moved):
    return pl.CostEstimate(flops=int(flops), bytes_accessed=int(moved), transcendentals=0)


def forward_kernel(
    pieces, place, x_hbm, w_hbm, b_ref, wout_ref, x_ref, w_ref, act_ref, slope_ref, *rest
):
    sends, line, base, x_sems, w_sems = rest[:pieces], *rest[pieces:]
    members, _, width = x_ref.shape
    length = sends[0].shape[2]
    step = width // w_sems.shape[0]
    w_parts = [slice(lo, lo + step) for lo in range(0, width, step)]
    w_copies = [
        pltpu.make_async_copy(w_hbm.at[:, cols], w_ref.at[:, cols], w_sems.at[i])
        for i, cols in enumerate(w_parts)
    ]
    x_copies = [pltpu.make_async_copy(x_hbm.at[m], x_ref.at[m], x_sems.at[m]) for m in range(members)]
    x_copies[0].start()
    for copy in w_copies + x_copies[1:]:
        copy.start()
    for m in range(members):
        x_copies[m].wait()
        row = None
        for i, cols in enumerate(w_parts):
            if m == 0:
                w_copies[i].wait()
            pre = jnp.dot(x_ref[m], w_ref[:, cols], preferred_element_type=F32) + b_ref[:, cols]
            logistic = 0.5 * jnp.tanh(0.5 * pre) + 0.5
            act = pre * logistic
            slope_ref[m, :, cols] = (logistic + act * (1.0 - logistic)).astype(BF16)
            act = act.astype(BF16)
            act_ref[m, :, cols] = act
            part = lax.dot_general(
                wout_ref[:, cols], act, (((1,), (1,)), ((), ())), preferred_element_type=F32
            )
            row = part if row is None else row + part
        if m == 0:
            base[...] = row.astype(BF16).astype(F32)
        line[m] = row - base[...]
    for s in range(pieces):
        at = lax.rem(place[0] + s, pieces) * length
        lanes = pl.ds(pl.multiple_of(at, length), length)
        sends[s][0] = base[:, lanes].astype(BF16)
        for m in range(members):
            sends[s][1 + m] = line[m, :, lanes].astype(BF16)


def forward(grid_input, w_hidden, b_hidden, w_out_t, place, pieces):
    members, cells, width = grid_input.shape
    channels = w_out_t.shape[0]
    length = cells // pieces
    return pl.pallas_call(
        functools.partial(forward_kernel, pieces),
        in_specs=[ON_SMEM, ON_HBM, ON_HBM, ON_VMEM, ON_VMEM],
        out_specs=[ON_VMEM] * (4 + pieces),
        out_shape=[
            pltpu.VMEM(grid_input.shape, BF16),
            pltpu.VMEM(w_hidden.shape, BF16),
            pltpu.VMEM(grid_input.shape, BF16),
            pltpu.VMEM(grid_input.shape, BF16),
        ]
        + [pltpu.VMEM((members + 1, channels, length), BF16)] * pieces,
        scratch_shapes=[
            pltpu.VMEM((members, channels, cells), F32),
            pltpu.VMEM((channels, cells), F32),
            pltpu.SemaphoreType.DMA((members,)),
            pltpu.SemaphoreType.DMA((2,)),
        ],
        compiler_params=params(),
        cost_estimate=cost(2 * members * cells * width * (width + 256), 14 << 20),
        name="forward",
    )(place, grid_input, w_hidden, b_hidden.reshape(1, width), w_out_t)


def score_kernel(pieces, place, target_ref, bias_ref, weight_ref, *refs):
    given, out, (bias, weights_of) = refs[:pieces], refs[pieces : 2 * pieces], refs[2 * pieces :]
    per, channels, length = out[0].shape
    members = per * pieces
    kappa = ALPHA / (2.0 * members * (members - 1)) + (1.0 - ALPHA) / (2.0 * members * members)
    start = pl.multiple_of(place[0] * length, length)
    bias[...] = jnp.broadcast_to(bias_ref[...], (8, channels)).T
    weights_of[...] = jnp.broadcast_to(weight_ref[...], (8, channels)).T

    def rows_step(i, carry):
        rows = pl.ds(pl.multiple_of(i * 16, 16), 16)
        own = []
        for s in range(pieces):
            base = given[s][0, rows, :].astype(F32)
            own += [base + given[s][1 + m, rows, :].astype(F32) for m in range(per)]
        aim = target_ref[rows, pl.ds(start, length)] - bias[rows, :1]
        weight = weights_of[rows, :1]
        spread = [None] * members
        for j in range(members):
            for k in range(j + 1, members):
                slope = smooth_slope(own[j] - own[k])
                spread[j] = slope if spread[j] is None else spread[j] + slope
                spread[k] = -slope if spread[k] is None else spread[k] - slope
        for j in range(members):
            skill = smooth_slope(own[j] - aim) * (1.0 / members)
            value = weight * (skill - (2.0 * kappa) * spread[j])
            out[j // per][j % per, rows, :] = value.astype(BF16)
        return carry

    lax.fori_loop(0, channels // 16, rows_step, 0)


def score(given, target, b_out, channel_weight, place):
    pieces = len(given)
    extra, channels, length = given[0].shape
    shape = (extra - 1, channels, length)
    return pl.pallas_call(
        functools.partial(score_kernel, pieces),
        in_specs=[ON_SMEM] + [ON_VMEM] * (3 + pieces),
        out_specs=[ON_VMEM] * pieces,
        out_shape=[pltpu.VMEM(shape, BF16)] * pieces,
        scratch_shapes=[pltpu.VMEM((channels, 8), F32)] * 2,
        compiler_params=params(),
        cost_estimate=cost(40_000_000, 1 << 20),
        name="score",
    )(place, target, b_out.reshape(1, channels), channel_weight.reshape(1, channels), *given)


def tiles_kernel(per_region, regions, place, index_ref, tile_ref, out_ref, total):
    blocks, sources, cells, nodes = tile_ref.shape
    total[...] = jnp.zeros_like(total)
    for b in range(blocks):
        for k in range(sources):
            number = index_ref[b, k]
            relative = lax.rem(number // per_region - place[1] + 1 + regions, regions)
            slot = relative * per_region + lax.rem(number, per_region)
            total[slot, b] += tile_ref[b, k].astype(F32).T
    for s in range(total.shape[0]):
        for b in range(blocks):
            out_ref[s * nodes : (s + 1) * nodes, b * cells : (b + 1) * cells] = total[s, b].astype(BF16)


def tiles_matrix(interp_weight, block_index, place, per_region, regions):
    blocks, _, cells, nodes = interp_weight.shape
    slots = 3 * per_region
    return pl.pallas_call(
        functools.partial(tiles_kernel, per_region, regions),
        in_specs=[ON_SMEM, ON_SMEM, ON_VMEM],
        out_specs=ON_VMEM,
        out_shape=pltpu.VMEM((slots * nodes, blocks * cells), BF16),
        scratch_shapes=[pltpu.VMEM((slots, blocks, nodes, cells), F32)],
        compiler_params=params(),
        cost_estimate=cost(4_000_000, 2 << 20),
        name="tiles",
    )(place, block_index, interp_weight)


def backward_kernel(first, pieces, place, wout_ref, slope_ref, tiles_ref, *refs):
    given = refs[:pieces]
    dpred_ref, dpre_ref, below_ref, own_ref, above_ref = refs[pieces:]
    length = given[0].shape[2]
    members, nodes, width = own_ref.shape
    step = 512
    for m in range(members):
        for s in range(pieces):
            at = lax.rem(place[0] + s, pieces) * length
            rows = pl.ds(pl.multiple_of(at, length), length)
            dpred_ref[m, rows, :] = given[s][first + m].astype(F32).T.astype(BF16)
        for lo in range(0, width, step):
            cols = slice(lo, lo + step)
            dact = jnp.dot(dpred_ref[m], wout_ref[:, cols], preferred_element_type=F32)
            dpre = (dact * slope_ref[first + m, :, cols].astype(F32)).astype(BF16)
            dpre_ref[m, :, cols] = dpre
            terms = jnp.dot(tiles_ref[...], dpre, preferred_element_type=F32)
            below_ref[m, :, cols] = terms[:nodes].astype(BF16)
            own_ref[m, :, cols] = terms[nodes : 2 * nodes].astype(BF16)
            above_ref[m, :, cols] = terms[2 * nodes :].astype(BF16)


def backward(first, members, given, w_out_t, slope, tiles, place):
    pieces = len(given)
    _, cells, width = slope.shape
    channels = w_out_t.shape[0]
    nodes = tiles.shape[0] // 3
    return pl.pallas_call(
        functools.partial(backward_kernel, first, pieces),
        in_specs=[ON_SMEM] + [ON_VMEM] * (3 + pieces),
        out_specs=[ON_VMEM] * 5,
        out_shape=[
            pltpu.VMEM((members, cells, channels), BF16),
            pltpu.VMEM((members, cells, width), BF16),
            pltpu.VMEM((members, nodes, width), BF16),
            pltpu.VMEM((members, nodes, width), BF16),
            pltpu.VMEM((members, nodes, width), BF16),
        ],
        compiler_params=params(),
        cost_estimate=cost(2 * members * cells * width * (256 + 3 * nodes), 5 << 20),
        name="backward",
    )(place, w_out_t, slope, tiles, *given)


def weights_kernel(parts, cores, place, x_ref, act_ref, *refs):
    dpre, dpred = refs[:parts], refs[parts : 2 * parts]
    per, _, width = dpre[0].shape
    across = (((0,), (0,)), ((), ()))
    step = 256
    total = refs[-1]
    count, rows = total.shape[1:3]
    for lo in range(0, width, step):
        cols = slice(lo, lo + step)
        hidden = output = None
        for m in range(parts * per):
            part = lax.dot_general(
                x_ref[m, :, cols], dpre[m // per][m % per], across, preferred_element_type=F32
            )
            hidden = part if hidden is None else hidden + part
            part = lax.dot_general(
                act_ref[m, :, cols], dpred[m // per][m % per], across, preferred_element_type=F32
            )
            output = part if output is None else output + part
        hidden, output = hidden.astype(BF16), output.astype(BF16)
        for i in range(step // rows):
            block = lo // rows + i
            total[block % cores, block // cores, :, :width] = hidden[i * rows : (i + 1) * rows]
            total[block % cores, block // cores, :, width:] = output[i * rows : (i + 1) * rows]
    if cores == 1:
        refs[2 * parts][...] = total[0]
    else:
        mine = lax.rem(place[1], cores)
        refs[2 * parts][...] = total[1 - mine]
        refs[2 * parts + 1][...] = total[mine]


def weights(x, act, dpre, dpred, place, blocks, cores):
    members, cells, width = x.shape
    columns = width + dpred[0].shape[2]
    parts = len(dpre)
    rows = width // blocks
    return pl.pallas_call(
        functools.partial(weights_kernel, parts, cores),
        in_specs=[ON_SMEM] + [ON_VMEM] * (2 + 2 * parts),
        out_specs=[ON_VMEM] * cores,
        out_shape=[pltpu.VMEM((blocks // cores, rows, columns), BF16)] * cores,
        scratch_shapes=[pltpu.VMEM((cores, blocks // cores, rows, columns), BF16)],
        compiler_params=params(),
        cost_estimate=cost(1000, 1000),
        name="weights",
    )(place, x, act, *dpre, *dpred)


def halve_kernel(which, bit, after, place, kept_ref, came_ref, away_ref, mine_ref):
    count = away_ref.shape[0]
    mine = lax.rem(place[which] // bit, 2)
    for ref, side in ((away_ref, 1 - mine), (mine_ref, mine)):
        for i in range(count):
            at = (2 * (i // after) + side) * after + i % after
            ref[i] = (kept_ref[at].astype(F32) + came_ref[at].astype(F32)).astype(BF16)


def halve(kept, came, place, which, bit, after):
    blocks, rows, columns = kept.shape
    half = pltpu.VMEM((blocks // 2, rows, columns), BF16)
    return pl.pallas_call(
        functools.partial(halve_kernel, which, bit, after),
        in_specs=[ON_SMEM, ON_VMEM, ON_VMEM],
        out_specs=[ON_VMEM] * 2,
        out_shape=[half, half],
        compiler_params=params(),
        cost_estimate=cost(1000, 1000),
        name="halve",
    )(place, kept, came)


def total_kernel(kept_ref, came_ref, hidden_ref, output_ref):
    total = kept_ref[0].astype(F32) + came_ref[0].astype(F32)
    width = hidden_ref.shape[1]
    hidden_ref[...] = total[:, :width]
    output_ref[...] = total[:, width:]


def last_total(kept, came, width):
    _, rows, columns = kept.shape
    return pl.pallas_call(
        total_kernel,
        in_specs=[ON_VMEM] * 2,
        out_specs=[ON_VMEM] * 2,
        out_shape=[
            jax.ShapeDtypeStruct((rows, width), F32),
            jax.ShapeDtypeStruct((rows, columns - width), F32),
        ],
        compiler_params=params(),
        cost_estimate=cost(1000, 1000),
        name="total",
    )(kept, came)


def bits_of(count):
    return [1 << i for i in range(count.bit_length() - 1)]


def weight_gradients(x, act, dpre, dpred, place, after):
    groups, regions = lax.axis_size("member"), lax.axis_size("region")
    blocks, width = groups * regions, x.shape[2]
    if regions < 2 or blocks & (blocks - 1) or (width // blocks) % 16:
        (part,) = weights(x, act, dpre, dpred, place, blocks, 1)
        part = part.reshape(width, -1)
        part = lax.psum_scatter(part, "member", scatter_dimension=0, tiled=True)
        part = lax.psum_scatter(part, "region", scatter_dimension=0, tiled=True).astype(F32)
        return part[:, :width], part[:, width:]
    near, *far = [(1, b) for b in bits_of(regions)]
    line = [(0, b) for b in bits_of(groups)]
    order = far[::-1][:1] + line + far[::-1][1:]
    names = line[::-1] + far[::-1]
    axes = ("member", "region")
    away, kept = weights(x, act, dpre, dpred, place, blocks, 2)
    (away, kept), _ = lax.optimization_barrier(((away, kept), after))
    came = exchanged(away, "region", 1)
    for which, bit in order:
        at = names.index((which, bit))
        names.pop(at)
        away, kept = halve(kept, came, place, which, bit, 1 << (len(names) - at))
        came = exchanged(away, axes[which], bit)
    return last_total(kept, came, width)


def finish_kernel(own_ref, up_ref, down_ref, w_ref, *refs):
    out_ref = refs[-1]
    total = own_ref[0].astype(F32) + up_ref[0].astype(F32) + down_ref[0].astype(F32)
    out_ref[0] = lax.dot_general(
        total.astype(BF16), w_ref[...], (((1,), (1,)), ((), ())), preferred_element_type=F32
    )


def finish(first, members, own, up, down, w_hidden, held):
    here, nodes, width = own.shape
    step = 128
    rows = pl.BlockSpec((1, step, width), lambda m, j: (m, j, 0))
    extra = [] if held is None else [held]
    return pl.pallas_call(
        finish_kernel,
        grid=(here, nodes // step),
        in_specs=[rows, rows, rows, pl.BlockSpec((width, width), lambda m, j: (0, 0))]
        + [ANYWHERE] * len(extra),
        out_specs=pl.BlockSpec((1, step, width), lambda m, j: (first + m, j, 0)),
        out_shape=jax.ShapeDtypeStruct((members, nodes, width), F32),
        input_output_aliases={4: 0} if extra else {},
        compiler_params=params(),
        cost_estimate=cost(1000, 1000),
        name="finish",
    )(own, up, down, w_hidden, *extra)


def body(
    grid_input, w_hidden, b_hidden, w_out, b_out, target, channel_weight, interp_weight, block_index
):
    members, cells, width = grid_input.shape
    groups, regions = lax.axis_size("member"), lax.axis_size("region")
    per_region = MBLK_REG
    place = jnp.stack([lax.axis_index("member"), lax.axis_index("region")]).astype(jnp.int32)
    w_out_t = w_out.T
    tiles = tiles_matrix(interp_weight, block_index, place, per_region, regions)
    x, w_hidden, act, slope, *sends = forward(grid_input, w_hidden, b_hidden, w_out_t, place, groups)
    given = [sends[0]] + [shifted(sends[s], "member", s) for s in range(1, groups)]
    adjoint = score(given, target, b_out, channel_weight, place)
    back = [adjoint[0]] + [shifted(adjoint[s], "member", -s) for s in range(1, groups)]
    dpred, dpre, own, up, down = [], [], [], [], []
    per = PER
    for first in range(0, members, per):
        one = backward(first, per, back, w_out_t, slope, tiles, place)
        dpred.append(one[0])
        dpre.append(one[1])
        own.append(one[3])
        down.append(shifted(one[2], "region", -1))
        up.append(shifted(one[4], "region", 1))
    hidden, output = weight_gradients(x, act, dpre, dpred, place, (up[0], down[0]))
    out = None
    for i, first in enumerate(range(0, members, per)):
        out = finish(first, members, own[i], up[i], down[i], w_hidden, out)
    return hidden, output, out


def solution(mesh):
    placed = (
        P("member", "region", None),
        P(),
        P(),
        P(),
        P(),
        P(None, "region"),
        P(),
        P("region", None, None, None),
        P("region", None),
    )
    return jax.shard_map(
        body,
        mesh=mesh,
        in_specs=placed,
        out_specs=(
            P(("member", "region"), None),
            P(("member", "region"), None),
            P("member", "region", None),
        ),
        check_vma=False,
    )
```

time: 297 us -> 132 us (0.44)
  matrix products: 68.4 us -> 0 us
  local copies, waits for them, and re-layouts: 61.7 us -> 5.42 us
  waiting for transfers between devices: 101 us -> 58 us
  Pallas kernels: 0 us -> 41 us
  loops' own time: 23.9 us -> 0 us
  starting transfers between devices: 12.6 us -> 26.5 us
  between operations: 14.2 us -> 0.8 us
  other arithmetic: 13.3 us -> 0.08 us
    dot_general x18 -> x0, matrix products: 68.4 us -> none  [the longest x12 36.7 us: add_block(): jnp.einsum('gn,mgh->mnh', weight_tile, block_rows, preferred_element_type...]
    pallas_call x0 -> x17, Pallas kernels: none -> 41 us  [the longest x4 9.87 us: finish(): pl.pallas_call(finish_kernel, grid=(here, nodes // step), in_specs=[rows,...]
    all_to_all x2 -> x0, waiting for transfers between devices: 33.9 us -> none  [the longest x1 24.4 us: body(): lax.all_to_all(pred_cols, 'member', split_axis=2, concat_axis=0, tiled=True)]
    dynamic_slice x25 -> x0, local copies, waits for them, and re-layouts: 28.7 us -> none  [the longest x12 20.9 us: add_block(): current = lax.dynamic_index_in_dim(accum, target_slot, 1, False)]
    another operation x1 -> x0, loops' own time: 23.9 us -> none  [body(): buffer = lax.fori_loop(0, GBLK_REG * K, add_block, buffer)]
    ppermute x2 -> x19, starting transfers between devices: 4.14 us -> 26.5 us  [the longest x14 24.9 us: shifted(): lax.ppermute(block, axis, [((i - distance) % count, i) for i in range(cou...]
    ppermute x2 -> x19, waiting for transfers between devices: 66.6 us -> 58 us  [the longest x14 35.4 us: shifted(): lax.ppermute(block, axis, [((i - distance) % count, i) for i in range(cou...]
    slice x4 -> x0, local copies, waits for them, and re-layouts: 8.57 us -> none  [the longest x1 4.5 us: body(): from_above = shifted(buffer[:, :MBLK_REG], 'region', -1)]
  transfers between devices with their start and end apart: 6 -> 19, of which waited for: 4 -> 11; matrix products, arithmetic and copies ran while one was open for 31% -> 0% of each run, Pallas kernels for 0% -> 19%
where the time goes in v1:
time: 132 us
  waiting for transfers between devices  58 us (44%)
  Pallas kernels  41 us (31%)
  starting transfers between devices  26.5 us (20%)
  local copies, waits for them, and re-layouts  5.42 us (4%)
    ppermute x14, waiting for transfers between devices, shifted(): lax.ppermute(block, axis, [((i - distance) % count, i) for i in range(cou...  35.4 us
    ppermute x14, starting transfers between devices, shifted(): lax.ppermute(block, axis, [((i - distance) % count, i) for i in range(cou...  24.9 us
    ppermute x5, waiting for transfers between devices, exchanged(): return lax.ppermute(block, axis, [(i, i ^ bit) for i in range(count)])  22.6 us
    pallas_call x4, Pallas kernels, finish(): pl.pallas_call(finish_kernel, grid=(here, nodes // step), in_specs=[rows,...  9.87 us
    pallas_call x1, Pallas kernels, forward(): pl.pallas_call(functools.partial(forward_kernel, pieces), in_specs=[ON_SM...  9.77 us
    pallas_call x4, Pallas kernels, backward(): pl.pallas_call(functools.partial(backward_kernel, first, pieces), in_spec...  8.01 us
    pallas_call x1, Pallas kernels, weights(): pl.pallas_call(functools.partial(weights_kernel, parts, cores), in_specs=...  6.67 us
    unnamed x20, local copies, waits for them, and re-layouts  5.42 us
  transfers between devices with their start and end apart: 19, of which 11 were waited for; matrix products, arithmetic and copies ran while one was open for 0% of the time, Pallas kernels for 19%

profile of v1, /device:TPU:3, one launch (start us, length us, event | category | flops | bytes accessed | tf_op | source)
XLA Modules:
  0.0 131.8 jit_solution(8283289199876224650)
XLA Ops:
  0.6 0.1 pad_add_fusion.place
  0.7 0.9 copy-done
  1.6 2.2 %copy-done.7 = bf16[4,512,1024]{2,1,0:T(8,128)(2,1)S(1)} copy-done((bf16[4,512,1024]{2,1,0:T(8,128)(2,1)S(1)}, bf16[4,512,1024]{2,1,0:T(8,128)(2,1)}, u32[]{:S(2)}) %copy-start.7) | copy-done | bytes 4194328
  3.8 1.6 %copy-done.8 = bf16[1024,1024]{1,0:T(8,128)(2,1)S(1)} copy-done((bf16[1024,1024]{1,0:T(8,128)(2,1)S(1)}, bf16[1024,1024]{1,0:T(8,128)(2,1)}, u32[]{:S(2)}) %copy-start.8) | copy-done | bytes 2097176
  5.4 0.7 copy-done.9
  6.1 0.0 copy-start.4
  6.1 9.8 %forward.1 = (bf16[4,512,1024]{2,1,0:T(8,128)(2,1)S(1)}, bf16[1024,1024]{1,0:T(8,128)(2,1)S(1)}, bf16[4,512,1024]{2,1,0:T(8,128)(2,1)S(1)}, bf16[4,512,1024]{2,1...) custom-call(s32[2]{0:T(128)S(1)} %pad_add_fusion.place, ...), custom_call_target="tpu_custom_call" | custom-call | flops 5368709120 | bytes 14680064 | tf_op jit(solution)/shard_map/forward/pallas_call | solution.py:92
  15.9 1.3 %collective-permute-start = (bf16[5,96,128]{2,1,0:T(8,128)(2,1)S(1)}, bf16[5,96,128]{2,1,0:T(8,128)(2,1)S(1)}, u32[]{:S(2)}, u32[]{:S(2)}) collective-permute-start(bf16[5,96,128]{2,1,0:T(8,128)(2,1)S(1)} %get-tuple-element.53), channel_id=1, source_target_pairs={{24,0},{0,8},{8,16},{16,24},{25,1},{1,9},{9,17},{17,25},{26,2},{2,... | collective-permute-start | bytes 368648 | tf_op jit(solution)/shard_map/ppermute | solution.py:25
  17.3 2.3 %collective-permute-start.1 = (bf16[5,96,128]{2,1,0:T(8,128)(2,1)S(1)}, bf16[5,96,128]{2,1,0:T(8,128)(2,1)S(1)}, u32[]{:S(2)}, u32[]{:S(2)}) collective-permute-start(bf16[5,96,128]{2,1,0:T(8,128)(2,1)S(1)} %get-tuple-element.54), channel_id=1, source_target_pairs={{16,0},{24,8},{0,16},{8,24},{17,1},{25,9},{1,17},{9,25},{18,2},{26... | collective-permute-start | bytes 368648 | tf_op jit(solution)/shard_map/ppermute | solution.py:25
  19.6 1.1 collective-permute-start.2
  20.6 1.4 %collective-permute-done.refs_1_ = bf16[5,96,128]{2,1,0:T(8,128)(2,1)S(1)} collective-permute-done((bf16[5,96,128]{2,1,0:T(8,128)(2,1)S(1)}, bf16[5,96,128]{2,1,0:T(8,128)(2,1)S(1)}, u32[]{:S(2)}, u32[]{:S(2)}) %collective-permute-start) | collective-permute-done | bytes 122912 | tf_op jit(solution)/shard_map/ppermute | solution.py:25
  22.1 6.3 %collective-permute-done.1.refs_2_ = bf16[5,96,128]{2,1,0:T(8,128)(2,1)S(1)} collective-permute-done((bf16[5,96,128]{2,1,0:T(8,128)(2,1)S(1)}, bf16[5,96,128]{2,1,0:T(8,128)(2,1)S(1)}, u32[]{:S(2)}, u32[]{:S(2)}) %collective-permute-start.1) | collective-permute-done | bytes 122912 | tf_op jit(solution)/shard_map/ppermute | solution.py:25
  28.4 2.4 %score.1 = (bf16[4,96,128]{2,1,0:T(8,128)(2,1)S(1)}, bf16[4,96,128]{2,1,0:T(8,128)(2,1)S(1)}, bf16[4,96,128]{2,1,0:T(8,128)(2,1)S(1)}, bf16[4,96,128]{2,1,0:T(8,128)(2,1)S(1)}) custom-call(s32[2]{0:T(128)S(1)} %pad_add_fusion.place, f32[96,512]{1,0:T(8,128)S(1)} %copy-done.3, f32[1,96]{1,0:T(1,128)S(1)} %bitcast.11, f32[1,96]{1,0:T(1,128)S(1)} %bitcast.12, ...), custom_call_target="tpu_custom_call" | custom-call | flops 40000000 | bytes 1048576 | tf_op jit(solution)/shard_map/score/pallas_call | solution.py:151
  30.7 3.0 %collective-permute-start.3 = (bf16[4,96,128]{2,1,0:T(8,128)(2,1)S(1)}, bf16[4,96,128]{2,1,0:T(8,128)(2,1)S(1)}, u32[]{:S(2)}, u32[]{:S(2)}) collective-permute-start(bf16[4,96,128]{2,1,0:T(8,128)(2,1)S(1)} %get-tuple-element.57), channel_id=1, source_target_pairs={{8,0},{16,8},{24,16},{0,24},{9,1},{17,9},{25,17},{1,25},{10,2},{18... | collective-permute-start | bytes 294920 | tf_op jit(solution)/shard_map/ppermute | solution.py:25
  33.7 1.2 collective-permute-start.4
  34.9 0.9 tiles.1.tiles_ref
  35.8 0.6 collective-permute-done.3.refs_1_
  36.4 7.2 %collective-permute-done.4.refs_2_ = bf16[4,96,128]{2,1,0:T(8,128)(2,1)S(1)} collective-permute-done((bf16[4,96,128]{2,1,0:T(8,128)(2,1)S(1)}, bf16[4,96,128]{2,1,0:T(8,128)(2,1)S(1)}, u32[]{:S(2)}, u32[]{:S(2)}) %collective-permute-start.4) | collective-permute-done | bytes 98336 | tf_op jit(solution)/shard_map/ppermute | solution.py:25
  43.6 2.0 %backward.4 = (bf16[1,512,96]{2,1,0:T(8,128)(2,1)S(1)}, bf16[1,512,1024]{2,1,0:T(8,128)(2,1)S(1)}, bf16[1,256,1024]{2,1,0:T(8,128)(2,1)S(1)}, bf16[1,256,1024]{2,1,0:T(8,128)(2,1)S(1)}, bf16[1,256,1024]{2,1,0:T(8,128)(2,1)S(1)}) custom-call(s32[2]{0:T(128)S(1)} %pad_add_fusion.place, bf16[96,1024]{1,0:T(8,128)(2,1)S(1)} %bitcast.7, ...), custom_call_target="tpu_custom_call" | custom-call | flops 1073741824 | bytes 5242880 | tf_op jit(solution)/shard_map/backward/pallas_call | solution.py:219
  45.6 2.5 %collective-permute-start.6 = (bf16[1,256,1024]{2,1,0:T(8,128)(2,1)S(1)}, bf16[1,256,1024]{2,1,0:T(8,128)(2,1)S(1)}, u32[]{:S(2)}, u32[]{:S(2)}) collective-permute-start(bf16[1,256,1024]{2,1,0:T(8,128)(2,1)S(1)} %get-tuple-element.70), channel_id=1, source_target_pairs={{7,0},{0,1},{1,2},{2,3},{3,4},{4,5},{5,6},{6,7},{15,8},{8,9},{9,10... | collective-permute-start | bytes 1572872 | tf_op jit(solution)/shard_map/ppermute | solution.py:25
  48.1 2.0 %backward.7 = (bf16[1,512,96]{2,1,0:T(8,128)(2,1)S(1)}, bf16[1,512,1024]{2,1,0:T(8,128)(2,1)S(1)}, bf16[1,256,1024]{2,1,0:T(8,128)(2,1)S(1)}, bf16[1,256,1024]{2,1,0:T(8,128)(2,1)S(1)}, bf16[1,256,1024]{2,1,0:T(8,128)(2,1)S(1)}) custom-call(s32[2]{0:T(128)S(1)} %pad_add_fusion.place, bf16[96,1024]{1,0:T(8,128)(2,1)S(1)} %bitcast.8, ...), custom_call_target="tpu_custom_call" | custom-call | flops 1073741824 | bytes 5242880 | tf_op jit(solution)/shard_map/backward/pallas_call | solution.py:219
  50.1 2.0 %backward.6 = (bf16[1,512,96]{2,1,0:T(8,128)(2,1)S(1)}, bf16[1,512,1024]{2,1,0:T(8,128)(2,1)S(1)}, bf16[1,256,1024]{2,1,0:T(8,128)(2,1)S(1)}, bf16[1,256,1024]{2,1,0:T(8,128)(2,1)S(1)}, bf16[1,256,1024]{2,1,0:T(8,128)(2,1)S(1)}) custom-call(s32[2]{0:T(128)S(1)} %pad_add_fusion.place, bf16[96,1024]{1,0:T(8,128)(2,1)S(1)} %bitcast.9, ...), custom_call_target="tpu_custom_call" | custom-call | flops 1073741824 | bytes 5242880 | tf_op jit(solution)/shard_map/backward/pallas_call | solution.py:219
  52.2 2.0 %backward.5 = (bf16[1,512,96]{2,1,0:T(8,128)(2,1)S(1)}, bf16[1,512,1024]{2,1,0:T(8,128)(2,1)S(1)}, bf16[1,256,1024]{2,1,0:T(8,128)(2,1)S(1)}, bf16[1,256,1024]{2,1,0:T(8,128)(2,1)S(1)}, bf16[1,256,1024]{2,1,0:T(8,128)(2,1)S(1)}) custom-call(s32[2]{0:T(128)S(1)} %pad_add_fusion.place, bf16[96,1024]{1,0:T(8,128)(2,1)S(1)} %bitcast.10, ...), custom_call_target="tpu_custom_call" | custom-call | flops 1073741824 | bytes 5242880 | tf_op jit(solution)/shard_map/backward/pallas_call | solution.py:219
  54.2 6.7 %weights.1 = (bf16[16,32,1120]{2,1,0:T(8,128)(2,1)S(1)}, bf16[16,32,1120]{2,1,0:T(8,128)(2,1)S(1)}) custom-call(s32[2]{0:T(128)S(1)} %pad_add_fusion.place, bf16[4,512,1024]{2,1,0:T(8,128)(2,1)S(1)} %get-tuple-element.49.x_ref, bf16[4,512,1024]{2,1,0:T(8,128)(2,1)S(1)} %get-tuple-element.50.act_ref, bf16[1,512,1024]{2,1,0:T(8,128)(2,1)S(1)} %get-tuple-element.60.refs_0_, ...), custom_call_target="tpu_custom_call" | custom-call | flops 1000 | bytes 1000 | tf_op jit(solution)/shard_map/weights/pallas_call | solution.py:273
  60.8 0.7 collective-permute-done.7.down_ref
  61.5 0.0 collective-permute-start.8
  61.5 2.8 %collective-permute-done.8.came_ref = bf16[16,32,1120]{2,1,0:T(8,128)(2,1)S(1)} collective-permute-done((bf16[16,32,1120]{2,1,0:T(8,128)(2,1)S(1)}, bf16[16,32,1120]{2,1,0:T(8,128)(2,1)S(1)}, u32[]{:S(2)}, u32[]{:S(2)}) %collective-permute-start.8) | collective-permute-done | bytes 1146912 | tf_op jit(solution)/shard_map/ppermute | solution.py:30
  64.4 0.8 halve.4
  65.2 1.0 collective-permute-start.9
  66.2 1.6 %collective-permute-start.17 = (bf16[1,256,1024]{2,1,0:T(8,128)(2,1)S(1)}, bf16[1,256,1024]{2,1,0:T(8,128)(2,1)S(1)}, u32[]{:S(2)}, u32[]{:S(2)}) collective-permute-start(bf16[1,256,1024]{2,1,0:T(8,128)(2,1)S(1)} %get-tuple-element.92), channel_id=1, source_target_pairs={{7,0},{0,1},{1,2},{2,3},{3,4},{4,5},{5,6},{6,7},{15,8},{8,9},{9,10... | collective-permute-start | bytes 1572872 | tf_op jit(solution)/shard_map/ppermute | solution.py:25
  67.8 12.2 %collective-permute-done.9.came_ref = bf16[8,32,1120]{2,1,0:T(8,128)(2,1)S(1)} collective-permute-done((bf16[8,32,1120]{2,1,0:T(8,128)(2,1)S(1)}, bf16[8,32,1120]{2,1,0:T(8,128)(2,1)S(1)}, u32[]{:S(2)}, u32[]{:S(2)}) %collective-permute-start.9) | collective-permute-done | bytes 573472 | tf_op jit(solution)/shard_map/ppermute | solution.py:30
  80.0 0.7 halve.5
  80.7 0.1 collective-permute-start.10
  80.8 7.5 %collective-permute-done.10.came_ref = bf16[4,32,1120]{2,1,0:T(8,128)(2,1)S(1)} collective-permute-done((bf16[4,32,1120]{2,1,0:T(8,128)(2,1)S(1)}, bf16[4,32,1120]{2,1,0:T(8,128)(2,1)S(1)}, u32[]{:S(2)}, u32[]{:S(2)}) %collective-permute-start.10) | collective-permute-done | bytes 286752 | tf_op jit(solution)/shard_map/ppermute | solution.py:30
  88.4 0.6 halve.6
  89.0 0.5 collective-permute-start.11
  89.5 2.1 %collective-permute-start.18 = (bf16[1,256,1024]{2,1,0:T(8,128)(2,1)S(1)}, bf16[1,256,1024]{2,1,0:T(8,128)(2,1)S(1)}, u32[]{:S(2)}, u32[]{:S(2)}) collective-permute-start(bf16[1,256,1024]{2,1,0:T(8,128)(2,1)S(1)} %get-tuple-element.93), channel_id=1, source_target_pairs={{1,0},{2,1},{3,2},{4,3},{5,4},{6,5},{7,6},{0,7},{9,8},{10,9},{11,1... | collective-permute-start | bytes 1572872 | tf_op jit(solution)/shard_map/ppermute | solution.py:25
  91.6 7.1 %collective-permute-start.15 = (bf16[1,256,1024]{2,1,0:T(8,128)(2,1)S(1)}, bf16[1,256,1024]{2,1,0:T(8,128)(2,1)S(1)}, u32[]{:S(2)}, u32[]{:S(2)}) collective-permute-start(bf16[1,256,1024]{2,1,0:T(8,128)(2,1)S(1)} %get-tuple-element.89), channel_id=1, source_target_pairs={{7,0},{0,1},{1,2},{2,3},{3,4},{4,5},{5,6},{6,7},{15,8},{8,9},{9,10... | collective-permute-start | bytes 1572872 | tf_op jit(solution)/shard_map/ppermute | solution.py:25
  98.7 2.6 %collective-permute-start.13 = (bf16[1,256,1024]{2,1,0:T(8,128)(2,1)S(1)}, bf16[1,256,1024]{2,1,0:T(8,128)(2,1)S(1)}, u32[]{:S(2)}, u32[]{:S(2)}) collective-permute-start(bf16[1,256,1024]{2,1,0:T(8,128)(2,1)S(1)} %get-tuple-element.85), channel_id=1, source_target_pairs={{7,0},{0,1},{1,2},{2,3},{3,4},{4,5},{5,6},{6,7},{15,8},{8,9},{9,10... | collective-permute-start | bytes 1572872 | tf_op jit(solution)/shard_map/ppermute | solution.py:25
  101.4 0.6 halve.7
  102.0 9.2 %collective-permute-done.18.down_ref = bf16[1,256,1024]{2,1,0:T(8,128)(2,1)S(1)} collective-permute-done((bf16[1,256,1024]{2,1,0:T(8,128)(2,1)S(1)}, bf16[1,256,1024]{2,1,0:T(8,128)(2,1)S(1)}, u32[]{:S(2)}, u32[]{:S(2)}) %collective-permute-start.18) | collective-permute-done | bytes 524320 | tf_op jit(solution)/shard_map/ppermute | solution.py:25
  111.2 2.5 %finish.4.refs_0_ = f32[4,256,1024]{2,1,0:T(8,128)} custom-call(bf16[1,256,1024]{2,1,0:T(8,128)(2,1)S(1)} %get-tuple-element.94.own_ref, bf16[1,256,1024]{2,1,0:T(8,128)(2,1)S(1)} %collective-permute-done.6.up_ref, bf16[1,256,1024]{2,1,0:T(8,128)(2,1)S(1)} %collective-permute-done.7.down_ref, bf16[1024,1024]{1,0:T(8,128)(2,1)S(1)} %get-tuple-element.87.w_ref), custom_call_target="tpu_custom_call" | custom-call | flops 1000 | bytes 1000 | tf_op jit(solution)/shard_map/finish/pallas_call | solution.py:373
  113.6 2.5 %finish.5.refs_0_ = f32[4,256,1024]{2,1,0:T(8,128)} custom-call(bf16[1,256,1024]{2,1,0:T(8,128)(2,1)S(1)} %get-tuple-element.91.own_ref, bf16[1,256,1024]{2,1,0:T(8,128)(2,1)S(1)} %collective-permute-done.17.up_ref, bf16[1,256,1024]{2,1,0:T(8,128)(2,1)S(1)} %collective-permute-done.18.down_ref, ...), custom_call_target="tpu_custom_call", output_to_operand_aliasing={{}: (4, {})} | custom-call | flops 1000 | bytes 1000 | tf_op jit(solution)/shard_map/finish/pallas_call | solution.py:373
  116.1 6.3 %collective-permute-done.16.down_ref = bf16[1,256,1024]{2,1,0:T(8,128)(2,1)S(1)} collective-permute-done((bf16[1,256,1024]{2,1,0:T(8,128)(2,1)S(1)}, bf16[1,256,1024]{2,1,0:T(8,128)(2,1)S(1)}, u32[]{:S(2)}, u32[]{:S(2)}) %collective-permute-start.16) | collective-permute-done | bytes 524320 | tf_op jit(solution)/shard_map/ppermute | solution.py:25
  122.4 2.5 %finish.6.refs_0_ = f32[4,256,1024]{2,1,0:T(8,128)} custom-call(bf16[1,256,1024]{2,1,0:T(8,128)(2,1)S(1)} %get-tuple-element.88.own_ref, bf16[1,256,1024]{2,1,0:T(8,128)(2,1)S(1)} %collective-permute-done.15.up_ref, bf16[1,256,1024]{2,1,0:T(8,128)(2,1)S(1)} %collective-permute-done.16.down_ref, ...), custom_call_target="tpu_custom_call", output_to_operand_aliasing={{}: (4, {})} | custom-call | flops 1000 | bytes 1000 | tf_op jit(solution)/shard_map/finish/pallas_call | solution.py:373
  124.9 3.8 %collective-permute-done.14.down_ref = bf16[1,256,1024]{2,1,0:T(8,128)(2,1)S(1)} collective-permute-done((bf16[1,256,1024]{2,1,0:T(8,128)(2,1)S(1)}, bf16[1,256,1024]{2,1,0:T(8,128)(2,1)S(1)}, u32[]{:S(2)}, u32[]{:S(2)}) %collective-permute-start.14) | collective-permute-done | bytes 524320 | tf_op jit(solution)/shard_map/ppermute | solution.py:25
  128.6 2.5 %finish.7 = f32[4,256,1024]{2,1,0:T(8,128)} custom-call(bf16[1,256,1024]{2,1,0:T(8,128)(2,1)S(1)} %get-tuple-element.84.own_ref, bf16[1,256,1024]{2,1,0:T(8,128)(2,1)S(1)} %collective-permute-done.13.up_ref, bf16[1,256,1024]{2,1,0:T(8,128)(2,1)S(1)} %collective-permute-done.14.down_ref, ...), custom_call_target="tpu_custom_call", output_to_operand_aliasing={{}: (4, {})} | custom-call | flops 1000 | bytes 1000 | tf_op jit(solution)/shard_map/finish/pallas_call | solution.py:373
  131.1 0.7 total.1
  (28 shorter events, 0.1 us)
Async XLA Ops:
  0.7 0.9 copy-start
  1.6 2.2 %copy-start.7 = (bf16[4,512,1024]{2,1,0:T(8,128)(2,1)S(1)}, bf16[4,512,1024]{2,1,0:T(8,128)(2,1)}, u32[]{:S(2)}) copy-start(bf16[4,512,1024]{2,1,0:T(8,128)(2,1)} %x_hbm.1) | copy-start | bytes 12582916
  3.8 1.6 %copy-start.8 = (bf16[1024,1024]{1,0:T(8,128)(2,1)S(1)}, bf16[1024,1024]{1,0:T(8,128)(2,1)}, u32[]{:S(2)}) copy-start(bf16[1024,1024]{1,0:T(8,128)(2,1)} %w_hbm.1) | copy-start | bytes 6291460
  5.4 0.7 copy-start.9
  6.1 22.2 %copy-start.3 = (f32[96,512]{1,0:T(8,128)S(1)}, f32[96,512]{1,0:T(8,128)}, u32[]{:S(2)}) copy-start(f32[96,512]{1,0:T(8,128)} %target_ref.1) | copy-start | bytes 589828
  6.1 22.2 %copy-start.5 = (f32[96]{0:T(128)S(1)}, f32[96]{0:T(128)}, u32[]{:S(2)}) copy-start(f32[96]{0:T(128)} %param.13) | copy-start | bytes 1156
  6.1 22.2 %copy-start.6 = (f32[96]{0:T(128)S(1)}, f32[96]{0:T(128)}, u32[]{:S(2)}) copy-start(f32[96]{0:T(128)} %param.15) | copy-start | bytes 1156
  6.1 28.8 %copy-start.2 = (bf16[4,3,128,128]{3,2,1,0:T(8,128)(2,1)S(1)}, bf16[4,3,128,128]{3,2,1,0:T(8,128)(2,1)}, u32[]{:S(2)}) copy-start(bf16[4,3,128,128]{3,2,1,0:T(8,128)(2,1)} %tile_ref.1) | copy-start | bytes 1179652
  6.1 28.8 %copy-start.4 = (s32[4,3]{1,0:T(4,128)S(1)}, s32[4,3]{1,0:T(4,128)}, u32[]{:S(2)}) copy-start(s32[4,3]{1,0:T(4,128)} %index_ref.1) | copy-start | bytes 148
  6.1 37.5 %copy-start.1 = (bf16[1024,96]{0,1:T(8,128)(2,1)S(1)}, bf16[1024,96]{0,1:T(8,128)(2,1)}, u32[]{:S(2)}) copy-start(bf16[1024,96]{0,1:T(8,128)(2,1)} %param.12) | copy-start | bytes 589828
  15.9 6.2 %collective-permute-start = (bf16[5,96,128]{2,1,0:T(8,128)(2,1)S(1)}, bf16[5,96,128]{2,1,0:T(8,128)(2,1)S(1)}, u32[]{:S(2)}, u32[]{:S(2)}) collective-permute-start(bf16[5,96,128]{2,1,0:T(8,128)(2,1)S(1)} %get-tuple-element.53), channel_id=1, source_target_pairs={{24,0},{0,8},{8,16},{16,24},{25,1},{1,9},{9,17},{17,25},{26,2},{2,... | collective-permute-start | bytes 368648 | tf_op jit(solution)/shard_map/ppermute | solution.py:25
  17.3 11.1 %collective-permute-start.1 = (bf16[5,96,128]{2,1,0:T(8,128)(2,1)S(1)}, bf16[5,96,128]{2,1,0:T(8,128)(2,1)S(1)}, u32[]{:S(2)}, u32[]{:S(2)}) collective-permute-start(bf16[5,96,128]{2,1,0:T(8,128)(2,1)S(1)} %get-tuple-element.54), channel_id=1, source_target_pairs={{16,0},{24,8},{0,16},{8,24},{17,1},{25,9},{1,17},{9,25},{18,2},{26... | collective-permute-start | bytes 368648 | tf_op jit(solution)/shard_map/ppermute | solution.py:25
  19.6 8.8 %collective-permute-start.2 = (bf16[5,96,128]{2,1,0:T(8,128)(2,1)S(1)}, bf16[5,96,128]{2,1,0:T(8,128)(2,1)S(1)}, u32[]{:S(2)}, u32[]{:S(2)}) collective-permute-start(bf16[5,96,128]{2,1,0:T(8,128)(2,1)S(1)} %get-tuple-element.55), channel_id=1, source_target_pairs={{8,0},{16,8},{24,16},{0,24},{9,1},{17,9},{25,17},{1,25},{10,2},{18... | collective-permute-start | bytes 368648 | tf_op jit(solution)/shard_map/ppermute | solution.py:25
  30.7 5.7 %collective-permute-start.3 = (bf16[4,96,128]{2,1,0:T(8,128)(2,1)S(1)}, bf16[4,96,128]{2,1,0:T(8,128)(2,1)S(1)}, u32[]{:S(2)}, u32[]{:S(2)}) collective-permute-start(bf16[4,96,128]{2,1,0:T(8,128)(2,1)S(1)} %get-tuple-element.57), channel_id=1, source_target_pairs={{8,0},{16,8},{24,16},{0,24},{9,1},{17,9},{25,17},{1,25},{10,2},{18... | collective-permute-start | bytes 294920 | tf_op jit(solution)/shard_map/ppermute | solution.py:25
  33.7 9.9 %collective-permute-start.4 = (bf16[4,96,128]{2,1,0:T(8,128)(2,1)S(1)}, bf16[4,96,128]{2,1,0:T(8,128)(2,1)S(1)}, u32[]{:S(2)}, u32[]{:S(2)}) collective-permute-start(bf16[4,96,128]{2,1,0:T(8,128)(2,1)S(1)} %get-tuple-element.58), channel_id=1, source_target_pairs={{16,0},{24,8},{0,16},{8,24},{17,1},{25,9},{1,17},{9,25},{18,2},{26... | collective-permute-start | bytes 294920 | tf_op jit(solution)/shard_map/ppermute | solution.py:25
  34.9 8.7 %collective-permute-start.5 = (bf16[4,96,128]{2,1,0:T(8,128)(2,1)S(1)}, bf16[4,96,128]{2,1,0:T(8,128)(2,1)S(1)}, u32[]{:S(2)}, u32[]{:S(2)}) collective-permute-start(bf16[4,96,128]{2,1,0:T(8,128)(2,1)S(1)} %get-tuple-element.59), channel_id=1, source_target_pairs={{24,0},{0,8},{8,16},{16,24},{25,1},{1,9},{9,17},{17,25},{26,2},{2,... | collective-permute-start | bytes 294920 | tf_op jit(solution)/shard_map/ppermute | solution.py:25
  45.6 15.2 %collective-permute-start.6 = (bf16[1,256,1024]{2,1,0:T(8,128)(2,1)S(1)}, bf16[1,256,1024]{2,1,0:T(8,128)(2,1)S(1)}, u32[]{:S(2)}, u32[]{:S(2)}) collective-permute-start(bf16[1,256,1024]{2,1,0:T(8,128)(2,1)S(1)} %get-tuple-element.70), channel_id=1, source_target_pairs={{7,0},{0,1},{1,2},{2,3},{3,4},{4,5},{5,6},{6,7},{15,8},{8,9},{9,10... | collective-permute-start | bytes 1572872 | tf_op jit(solution)/shard_map/ppermute | solution.py:25
  48.1 13.4 %collective-permute-start.7 = (bf16[1,256,1024]{2,1,0:T(8,128)(2,1)S(1)}, bf16[1,256,1024]{2,1,0:T(8,128)(2,1)S(1)}, u32[]{:S(2)}, u32[]{:S(2)}) collective-permute-start(bf16[1,256,1024]{2,1,0:T(8,128)(2,1)S(1)} %get-tuple-element.71), channel_id=1, source_target_pairs={{1,0},{2,1},{3,2},{4,3},{5,4},{6,5},{7,6},{0,7},{9,8},{10,9},{11,1... | collective-permute-start | bytes 1572872 | tf_op jit(solution)/shard_map/ppermute | solution.py:25
  61.5 2.8 %collective-permute-start.8 = (bf16[16,32,1120]{2,1,0:T(8,128)(2,1)S(1)}, bf16[16,32,1120]{2,1,0:T(8,128)(2,1)S(1)}, u32[]{:S(2)}, u32[]{:S(2)}) collective-permute-start(bf16[16,32,1120]{2,1,0:T(8,128)(2,1)S(1)} %get-tuple-element.73), channel_id=1, source_target_pairs={{0,1},{1,0},{2,3},{3,2},{4,5},{5,4},{6,7},{7,6},{8,9},{9,8},{10,11... | collective-permute-start | bytes 3440648 | tf_op jit(solution)/shard_map/ppermute | solution.py:30
  65.2 14.9 %collective-permute-start.9 = (bf16[8,32,1120]{2,1,0:T(8,128)(2,1)S(1)}, bf16[8,32,1120]{2,1,0:T(8,128)(2,1)S(1)}, u32[]{:S(2)}, u32[]{:S(2)}) collective-permute-start(bf16[8,32,1120]{2,1,0:T(8,128)(2,1)S(1)} %get-tuple-element.75), channel_id=1, source_target_pairs={{0,4},{1,5},{2,6},{3,7},{4,0},{5,1},{6,2},{7,3},{8,12},{9,13},{10,... | collective-permute-start | bytes 1720328 | tf_op jit(solution)/shard_map/ppermute | solution.py:30
  66.2 32.5 %collective-permute-start.17 = (bf16[1,256,1024]{2,1,0:T(8,128)(2,1)S(1)}, bf16[1,256,1024]{2,1,0:T(8,128)(2,1)S(1)}, u32[]{:S(2)}, u32[]{:S(2)}) collective-permute-start(bf16[1,256,1024]{2,1,0:T(8,128)(2,1)S(1)} %get-tuple-element.92), channel_id=1, source_target_pairs={{7,0},{0,1},{1,2},{2,3},{3,4},{4,5},{5,6},{6,7},{15,8},{8,9},{9,10... | collective-permute-start | bytes 1572872 | tf_op jit(solution)/shard_map/ppermute | solution.py:25
  80.7 7.6 %collective-permute-start.10 = (bf16[4,32,1120]{2,1,0:T(8,128)(2,1)S(1)}, bf16[4,32,1120]{2,1,0:T(8,128)(2,1)S(1)}, u32[]{:S(2)}, u32[]{:S(2)}) collective-permute-start(bf16[4,32,1120]{2,1,0:T(8,128)(2,1)S(1)} %get-tuple-element.77), channel_id=1, source_target_pairs={{0,8},{8,0},{16,24},{24,16},{1,9},{9,1},{17,25},{25,17},{2,10},{10... | collective-permute-start | bytes 860168 | tf_op jit(solution)/shard_map/ppermute | solution.py:30
  89.0 12.4 %collective-permute-start.11 = (bf16[2,32,1120]{2,1,0:T(8,128)(2,1)S(1)}, bf16[2,32,1120]{2,1,0:T(8,128)(2,1)S(1)}, u32[]{:S(2)}, u32[]{:S(2)}) collective-permute-start(bf16[2,32,1120]{2,1,0:T(8,128)(2,1)S(1)} %get-tuple-element.79), channel_id=1, source_target_pairs={{0,16},{8,24},{16,0},{24,8},{1,17},{9,25},{17,1},{25,9},{2,18},{10... | collective-permute-start | bytes 430088 | tf_op jit(solution)/shard_map/ppermute | solution.py:30
  89.5 21.7 %collective-permute-start.18 = (bf16[1,256,1024]{2,1,0:T(8,128)(2,1)S(1)}, bf16[1,256,1024]{2,1,0:T(8,128)(2,1)S(1)}, u32[]{:S(2)}, u32[]{:S(2)}) collective-permute-start(bf16[1,256,1024]{2,1,0:T(8,128)(2,1)S(1)} %get-tuple-element.93), channel_id=1, source_target_pairs={{1,0},{2,1},{3,2},{4,3},{5,4},{6,5},{7,6},{0,7},{9,8},{10,9},{11,1... | collective-permute-start | bytes 1572872 | tf_op jit(solution)/shard_map/ppermute | solution.py:25
  91.6 24.5 %collective-permute-start.15 = (bf16[1,256,1024]{2,1,0:T(8,128)(2,1)S(1)}, bf16[1,256,1024]{2,1,0:T(8,128)(2,1)S(1)}, u32[]{:S(2)}, u32[]{:S(2)}) collective-permute-start(bf16[1,256,1024]{2,1,0:T(8,128)(2,1)S(1)} %get-tuple-element.89), channel_id=1, source_target_pairs={{7,0},{0,1},{1,2},{2,3},{3,4},{4,5},{5,6},{6,7},{15,8},{8,9},{9,10... | collective-permute-start | bytes 1572872 | tf_op jit(solution)/shard_map/ppermute | solution.py:25
  98.7 23.7 %collective-permute-start.16 = (bf16[1,256,1024]{2,1,0:T(8,128)(2,1)S(1)}, bf16[1,256,1024]{2,1,0:T(8,128)(2,1)S(1)}, u32[]{:S(2)}, u32[]{:S(2)}) collective-permute-start(bf16[1,256,1024]{2,1,0:T(8,128)(2,1)S(1)} %get-tuple-element.90), channel_id=1, source_target_pairs={{1,0},{2,1},{3,2},{4,3},{5,4},{6,5},{7,6},{0,7},{9,8},{10,9},{11,1... | collective-permute-start | bytes 1572872 | tf_op jit(solution)/shard_map/ppermute | solution.py:25
  98.7 26.2 %collective-permute-start.13 = (bf16[1,256,1024]{2,1,0:T(8,128)(2,1)S(1)}, bf16[1,256,1024]{2,1,0:T(8,128)(2,1)S(1)}, u32[]{:S(2)}, u32[]{:S(2)}) collective-permute-start(bf16[1,256,1024]{2,1,0:T(8,128)(2,1)S(1)} %get-tuple-element.85), channel_id=1, source_target_pairs={{7,0},{0,1},{1,2},{2,3},{3,4},{4,5},{5,6},{6,7},{15,8},{8,9},{9,10... | collective-permute-start | bytes 1572872 | tf_op jit(solution)/shard_map/ppermute | solution.py:25
  101.4 27.3 %collective-permute-start.14 = (bf16[1,256,1024]{2,1,0:T(8,128)(2,1)S(1)}, bf16[1,256,1024]{2,1,0:T(8,128)(2,1)S(1)}, u32[]{:S(2)}, u32[]{:S(2)}) collective-permute-start(bf16[1,256,1024]{2,1,0:T(8,128)(2,1)S(1)} %get-tuple-element.86), channel_id=1, source_target_pairs={{1,0},{2,1},{3,2},{4,3},{5,4},{6,5},{7,6},{0,7},{9,8},{10,9},{11,1... | collective-permute-start | bytes 1572872 | tf_op jit(solution)/shard_map/ppermute | solution.py:25
  111.2 19.9 %collective-permute-start.12 = (bf16[1,32,1120]{2,1,0:T(8,128)(2,1)S(1)}, bf16[1,32,1120]{2,1,0:T(8,128)(2,1)S(1)}, u32[]{:S(2)}, u32[]{:S(2)}) collective-permute-start(bf16[1,32,1120]{2,1,0:T(8,128)(2,1)S(1)} %get-tuple-element.81), channel_id=1, source_target_pairs={{0,2},{1,3},{2,0},{3,1},{4,6},{5,7},{6,4},{7,5},{8,10},{9,11},{10,... | collective-permute-start | bytes 215048 | tf_op jit(solution)/shard_map/ppermute | solution.py:30

commit v2 on v1

v2 whole, which is shorter than its diff:
```python
import functools

import jax
import jax.numpy as jnp
from jax import lax
from jax.experimental import pallas as pl
from jax.experimental.pallas import tpu as pltpu
from jax.sharding import PartitionSpec as P

ALPHA = 0.95
SMOOTH = 0.25
MBLK_REG = 2
SCOPED = 16 * 1024 * 1024
F32 = jnp.float32
BF16 = jnp.bfloat16
ON_VMEM = pl.BlockSpec(memory_space=pltpu.VMEM)
ON_HBM = pl.BlockSpec(memory_space=pltpu.HBM)
ON_SMEM = pl.BlockSpec(memory_space=pltpu.SMEM)
ANYWHERE = pl.BlockSpec(memory_space=pl.ANY)


def shifted(block, axis, distance):
    count = lax.axis_size(axis)
    return lax.ppermute(block, axis, [((i - distance) % count, i) for i in range(count)])


def exchanged(block, axis, bit):
    count = lax.axis_size(axis)
    return lax.ppermute(block, axis, [(i, i ^ bit) for i in range(count)])


def smooth_slope(diff):
    return diff * lax.rsqrt(diff * diff + SMOOTH * SMOOTH)


def params():
    return pltpu.CompilerParams(vmem_limit_bytes=SCOPED)


def in_hbm(array):
    return pltpu.with_memory_space_constraint(array, pltpu.HBM)


def cost(flops, moved):
    return pl.CostEstimate(flops=int(flops), bytes_accessed=int(moved), transcendentals=0)


def forward_kernel(
    pieces, place, x_hbm, w_hbm, b_ref, wout_ref, x_ref, w_ref, act_ref, slope_ref, *rest
):
    sends, line, base, x_sems, w_sem = rest[:pieces], *rest[pieces:]
    members, cells, _ = x_ref.shape
    length = sends[0].shape[2]
    w_copy = pltpu.make_async_copy(w_hbm, w_ref, w_sem)
    x_copies = [pltpu.make_async_copy(x_hbm.at[m], x_ref.at[m], x_sems.at[m]) for m in range(members)]
    w_copy.start()
    x_copies[0].start()
    w_copy.wait()
    for copy in x_copies[1:]:
        copy.start()
    step = cells // 2
    for m in range(members):
        x_copies[m].wait()
        for lo in range(0, cells, step):
            rows = slice(lo, lo + step)
            pre = jnp.dot(x_ref[m, rows, :], w_ref[...], preferred_element_type=F32) + b_ref[...]
            logistic = 0.5 * jnp.tanh(0.5 * pre) + 0.5
            act = pre * logistic
            slope_ref[m, rows, :] = (logistic + act * (1.0 - logistic)).astype(BF16)
            act = act.astype(BF16)
            act_ref[m, rows, :] = act
            part = lax.dot_general(
                wout_ref[...], act, (((1,), (1,)), ((), ())), preferred_element_type=F32
            )
            if m == 0:
                base[:, rows] = part.astype(BF16).astype(F32)
            line[m, :, rows] = part - base[:, rows]
    for s in range(pieces):
        at = lax.rem(place[0] + s, pieces) * length
        lanes = pl.ds(pl.multiple_of(at, length), length)
        sends[s][0] = base[:, lanes].astype(BF16)
        for m in range(members):
            sends[s][1 + m] = line[m, :, lanes].astype(BF16)


def forward(grid_input, w_hidden, b_hidden, w_out_t, place, pieces):
    members, cells, width = grid_input.shape
    channels = w_out_t.shape[0]
    length = cells // pieces
    return pl.pallas_call(
        functools.partial(forward_kernel, pieces),
        in_specs=[ON_SMEM, ON_HBM, ON_HBM, ON_VMEM, ON_VMEM],
        out_specs=[ON_VMEM] * (4 + pieces),
        out_shape=[
            pltpu.VMEM(grid_input.shape, BF16),
            pltpu.VMEM(w_hidden.shape, BF16),
            pltpu.VMEM(grid_input.shape, BF16),
            pltpu.VMEM(grid_input.shape, BF16),
        ]
        + [pltpu.VMEM((members + 1, channels, length), BF16)] * pieces,
        scratch_shapes=[
            pltpu.VMEM((members, channels, cells), F32),
            pltpu.VMEM((channels, cells), F32),
            pltpu.SemaphoreType.DMA((members,)),
            pltpu.SemaphoreType.DMA,
        ],
        compiler_params=params(),
        cost_estimate=cost(2 * members * cells * width * (width + 256), 14 << 20),
        name="forward",
    )(place, in_hbm(grid_input), in_hbm(w_hidden), b_hidden.reshape(1, width), w_out_t)


def score_kernel(pieces, place, target_ref, bias_ref, weight_ref, *refs):
    given, out, (bias, weights_of) = refs[:pieces], refs[pieces:-2], refs[-2:]
    extra, channels, length = given[0].shape
    per = extra - 1
    members = per * pieces
    kappa = ALPHA / (2.0 * members * (members - 1)) + (1.0 - ALPHA) / (2.0 * members * members)
    start = pl.multiple_of(place[0] * length, length)
    bias[...] = jnp.broadcast_to(bias_ref[...], (8, channels)).T
    weights_of[...] = jnp.broadcast_to(weight_ref[...], (8, channels)).T

    def rows_step(i, carry):
        rows = pl.ds(pl.multiple_of(i * 16, 16), 16)
        own = []
        for s in range(pieces):
            base = given[s][0, rows, :].astype(F32)
            own += [base + given[s][1 + m, rows, :].astype(F32) for m in range(per)]
        aim = target_ref[rows, pl.ds(start, length)] - bias[rows, :1]
        weight = weights_of[rows, :1]
        spread = [None] * members
        for j in range(members):
            for k in range(j + 1, members):
                slope = smooth_slope(own[j] - own[k])
                spread[j] = slope if spread[j] is None else spread[j] + slope
                spread[k] = -slope if spread[k] is None else spread[k] - slope
        for j in range(members):
            skill = smooth_slope(own[j] - aim) * (1.0 / members)
            value = weight * (skill - (2.0 * kappa) * spread[j])
            part = j % per
            at = j // per
            while part >= out[at].shape[0]:
                part -= out[at].shape[0]
                at += pieces
            out[at][part, rows, :] = value.astype(BF16)
        return carry

    lax.fori_loop(0, channels // 16, rows_step, 0)


def score(given, target, b_out, channel_weight, place, parts):
    pieces = len(given)
    extra, channels, length = given[0].shape
    shapes = [pltpu.VMEM((part, channels, length), BF16) for part in parts for _ in given]
    return pl.pallas_call(
        functools.partial(score_kernel, pieces),
        in_specs=[ON_SMEM] + [ON_VMEM] * (3 + pieces),
        out_specs=[ON_VMEM] * len(shapes),
        out_shape=shapes,
        scratch_shapes=[pltpu.VMEM((channels, 8), F32)] * 2,
        compiler_params=params(),
        cost_estimate=cost(40_000_000, 1 << 20),
        name="score",
    )(place, target, b_out.reshape(1, channels), channel_weight.reshape(1, channels), *given)


def tiles_kernel(per_region, regions, place, index_ref, tile_ref, w_ref, out_ref, w_t_ref, total):
    blocks, sources, cells, nodes = tile_ref.shape
    total[...] = jnp.zeros_like(total)
    for b in range(blocks):
        for k in range(sources):
            number = index_ref[b, k]
            relative = lax.rem(number // per_region - place[1] + 1 + regions, regions)
            slot = relative * per_region + lax.rem(number, per_region)
            total[slot, b] += tile_ref[b, k].astype(F32).T
    for s in range(total.shape[0]):
        for b in range(blocks):
            out_ref[s * nodes : (s + 1) * nodes, b * cells : (b + 1) * cells] = total[s, b].astype(BF16)
    step = 256
    for lo in range(0, w_ref.shape[0], step):
        w_t_ref[:, lo : lo + step] = w_ref[lo : lo + step, :].T


def tiles_matrix(interp_weight, block_index, w_hidden, place, per_region, regions):
    blocks, _, cells, nodes = interp_weight.shape
    slots = 3 * per_region
    return pl.pallas_call(
        functools.partial(tiles_kernel, per_region, regions),
        in_specs=[ON_SMEM, ON_SMEM, ON_VMEM, ON_VMEM],
        out_specs=[ON_VMEM] * 2,
        out_shape=[
            pltpu.VMEM((slots * nodes, blocks * cells), BF16),
            pltpu.VMEM(w_hidden.shape, BF16),
        ],
        scratch_shapes=[pltpu.VMEM((slots, blocks, nodes, cells), F32)],
        compiler_params=params(),
        cost_estimate=cost(4_000_000, 2 << 20),
        name="tiles",
    )(place, block_index, interp_weight, w_hidden)


def backward_kernel(first, pieces, place, wout_ref, slope_ref, tiles_ref, *refs):
    given = refs[:pieces]
    dpred_ref, dpre_ref, below_ref, own_ref, above_ref = refs[pieces:]
    length = given[0].shape[2]
    members, nodes, width = own_ref.shape
    step = 512
    for m in range(members):
        for s in range(pieces):
            at = lax.rem(place[0] + s, pieces) * length
            rows = pl.ds(pl.multiple_of(at, length), length)
            dpred_ref[m, rows, :] = given[s][m].astype(F32).T.astype(BF16)
        for lo in range(0, width, step):
            cols = slice(lo, lo + step)
            dact = jnp.dot(dpred_ref[m], wout_ref[:, cols], preferred_element_type=F32)
            dpre = (dact * slope_ref[first + m, :, cols].astype(F32)).astype(BF16)
            dpre_ref[m, :, cols] = dpre
            terms = jnp.dot(tiles_ref[...], dpre, preferred_element_type=F32)
            below_ref[m, :, cols] = terms[:nodes].astype(BF16)
            own_ref[m, :, cols] = terms[nodes : 2 * nodes].astype(BF16)
            above_ref[m, :, cols] = terms[2 * nodes :].astype(BF16)


def backward(first, members, given, w_out_t, slope, tiles, place):
    pieces = len(given)
    _, cells, width = slope.shape
    channels = w_out_t.shape[0]
    nodes = tiles.shape[0] // 3
    return pl.pallas_call(
        functools.partial(backward_kernel, first, pieces),
        in_specs=[ON_SMEM] + [ON_VMEM] * (3 + pieces),
        out_specs=[ON_VMEM] * 5,
        out_shape=[
            pltpu.VMEM((members, cells, channels), BF16),
            pltpu.VMEM((members, cells, width), BF16),
            pltpu.VMEM((members, nodes, width), BF16),
            pltpu.VMEM((members, nodes, width), BF16),
            pltpu.VMEM((members, nodes, width), BF16),
        ],
        compiler_params=params(),
        cost_estimate=cost(2 * members * cells * width * (256 + 3 * nodes), 5 << 20),
        name="backward",
    )(place, w_out_t, slope, tiles, *given)


def weights_kernel(turns, groups, cores, place, x_ref, act_ref, *refs):
    parts = (len(refs) - cores) // 2
    dpre = [(ref, m) for ref in refs[:parts] for m in range(ref.shape[0])]
    dpred = [(ref, m) for ref in refs[parts : 2 * parts] for m in range(ref.shape[0])]
    out = refs[2 * parts :]
    width = dpre[0][0].shape[2]
    step = width // groups
    count, rows, _ = out[0].shape
    count //= len(turns)
    across = (((0,), (0,)), ((), ()))
    mine = lax.rem(place[1], cores)
    for i, turn in enumerate(turns):
        at = lax.rem(place[0] + turn, groups) * step
        cols = pl.ds(pl.multiple_of(at, step), step)
        for values, others, wide in (
            (x_ref, dpre, slice(0, width)),
            (act_ref, dpred, slice(width, None)),
        ):
            total = None
            for m, (ref, k) in enumerate(others):
                part = lax.dot_general(values[m, :, cols], ref[k], across, preferred_element_type=F32)
                total = part if total is None else total + part
            total = total.astype(BF16).reshape(count, cores, rows, total.shape[1])
            for b in range(count):
                block = [total[b, c] for c in range(cores)]
                if cores == 1:
                    out[0][i * count + b, :, wide] = block[0]
                else:
                    low = mine == 0
                    out[0][i * count + b, :, wide] = jnp.where(low, block[1], block[0])
                    out[1][i * count + b, :, wide] = jnp.where(low, block[0], block[1])


def weights(x, act, dpre, dpred, place, blocks, groups, cores, turns):
    width = x.shape[2]
    columns = width + dpred[0].shape[2]
    rows = width // blocks
    count = len(turns) * blocks // (groups * cores)
    parts = len(dpre)
    return pl.pallas_call(
        functools.partial(weights_kernel, turns, groups, cores),
        in_specs=[ON_SMEM] + [ON_VMEM] * (2 + 2 * parts),
        out_specs=[ON_VMEM] * cores,
        out_shape=[pltpu.VMEM((count, rows, columns), BF16)] * cores,
        compiler_params=params(),
        cost_estimate=cost(1000, 1000),
        name="weights",
    )(place, x, act, *dpre, *dpred)


def add_kernel(kept_ref, came_ref, *out):
    count = out[0].shape[0]
    for s, ref in enumerate(out):
        for i in range(count):
            at = s * count + i
            ref[i] = (kept_ref[at].astype(F32) + came_ref[at].astype(F32)).astype(BF16)


def add(kept, came, parts):
    blocks, rows, columns = kept.shape
    return pl.pallas_call(
        add_kernel,
        in_specs=[ON_VMEM] * 2,
        out_specs=[ON_VMEM] * parts,
        out_shape=[pltpu.VMEM((blocks // parts, rows, columns), BF16)] * parts,
        compiler_params=params(),
        cost_estimate=cost(1000, 1000),
        name="add",
    )(kept, came)


def split_kernel(which, unit, parts, place, *refs):
    given, out = refs[:-parts], refs[-parts:]
    count = out[0].shape[0]
    mine = lax.rem(place[which] // unit, parts)
    for s in range(parts):
        first = lax.rem(mine + s, parts) * count
        for i in range(count):
            total = given[0][first + i].astype(F32)
            for ref in given[1:]:
                total = total + ref[first + i].astype(F32)
            out[s][i] = total.astype(BF16)


def split(given, place, which, unit, parts):
    blocks, rows, columns = given[0].shape
    return pl.pallas_call(
        functools.partial(split_kernel, which, unit, parts),
        in_specs=[ON_SMEM] + [ON_VMEM] * len(given),
        out_specs=[ON_VMEM] * parts,
        out_shape=[pltpu.VMEM((blocks // parts, rows, columns), BF16)] * parts,
        compiler_params=params(),
        cost_estimate=cost(1000, 1000),
        name="split",
    )(place, *given)


def total_kernel(*refs):
    given, (hidden_ref, output_ref) = refs[:-2], refs[-2:]
    width = hidden_ref.shape[1]
    for ref, cols in ((hidden_ref, slice(0, width)), (output_ref, slice(width, None))):
        total = given[0][0, :, cols].astype(F32)
        for other in given[1:]:
            total = total + other[0, :, cols].astype(F32)
        ref[...] = total


def last_total(given, width):
    _, rows, columns = given[0].shape
    return pl.pallas_call(
        total_kernel,
        in_specs=[ON_VMEM] * len(given),
        out_specs=[ON_VMEM] * 2,
        out_shape=[
            jax.ShapeDtypeStruct((rows, width), F32),
            jax.ShapeDtypeStruct((rows, columns - width), F32),
        ],
        compiler_params=params(),
        cost_estimate=cost(1000, 1000),
        name="total",
    )(*given)


def weight_gradients(x, act, dpre, dpred, place, after):
    groups, regions = lax.axis_size("member"), lax.axis_size("region")
    blocks, width = groups * regions, x.shape[2]
    if regions % 2 or width % (blocks * 16):
        turns = list(range(groups))
        (part,) = weights(x, act, dpre, dpred, place * 0, blocks, groups, 1, turns)
        part = part.reshape(width, -1)
        part = lax.psum_scatter(part, "member", scatter_dimension=0, tiled=True)
        part = lax.psum_scatter(part, "region", scatter_dimension=0, tiled=True).astype(F32)
        return part[:, :width], part[:, width:]
    given = [None] * groups
    for turns in turn_sets(groups):
        away, kept = weights(x, act, dpre, dpred, place, blocks, groups, 2, turns)
        if after is not None:
            (away, kept), _ = lax.optimization_barrier(((away, kept), after))
            after = None
        came = lax.ppermute(away, "region", [(i, i ^ 1) for i in range(regions)])
        for s, part in zip(turns, add(kept, came, len(turns))):
            given[s] = shifted(part, "member", s) if s else part
    chips = regions // 2
    parts = split(given, place, 1, 2, chips)
    given = [parts[0]]
    for s in range(1, chips):
        route = [(i, (i + 2 * s) % regions) for i in range(regions)]
        given.append(lax.ppermute(parts[s], "region", route))
    return last_total(given, width)


def finish_kernel(first, own_ref, up_ref, down_ref, w_ref, *refs):
    out_ref, slots, sems = refs[-3:]
    copies = []
    for m in range(own_ref.shape[0]):
        total = own_ref[m].astype(F32) + up_ref[m].astype(F32) + down_ref[m].astype(F32)
        slots[m] = jnp.dot(total.astype(BF16), w_ref[...], preferred_element_type=F32)
        copies.append(pltpu.make_async_copy(slots.at[m], out_ref.at[first + m], sems.at[m]))
        copies[m].start()
    for copy in copies:
        copy.wait()


def finish(first, members, own, up, down, w_hidden_t, held):
    here, nodes, width = own.shape
    extra = [] if held is None else [held]
    return pl.pallas_call(
        functools.partial(finish_kernel, first),
        in_specs=[ON_VMEM] * 4 + [ANYWHERE] * len(extra),
        out_specs=ANYWHERE,
        out_shape=jax.ShapeDtypeStruct((members, nodes, width), F32),
        scratch_shapes=[pltpu.VMEM(own.shape, F32), pltpu.SemaphoreType.DMA((here,))],
        input_output_aliases={4: 0} if extra else {},
        compiler_params=params(),
        cost_estimate=cost(1000, 1000),
        name="finish",
    )(own, up, down, w_hidden_t, *extra)


def body(
    grid_input, w_hidden, b_hidden, w_out, b_out, target, channel_weight, interp_weight, block_index
):
    members, cells, width = grid_input.shape
    groups, regions = lax.axis_size("member"), lax.axis_size("region")
    per_region = MBLK_REG
    place = jnp.stack([lax.axis_index("member"), lax.axis_index("region")]).astype(jnp.int32)
    w_out_t = w_out.T
    x, w_hidden, act, slope, *sends = forward(grid_input, w_hidden, b_hidden, w_out_t, place, groups)
    tiles, w_hidden_t = tiles_matrix(
        interp_weight, block_index, w_hidden, place, per_region, regions
    )
    given = [sends[0]] + [shifted(sends[s], "member", s) for s in range(1, groups)]
    parts = shares(members)
    adjoint = score(given, target, b_out, channel_weight, place, parts)
    dpred, dpre, own, up, down = [], [], [], [], []
    first = 0
    for i, per in enumerate(parts):
        mine = adjoint[i * groups : (i + 1) * groups]
        back = [mine[0]] + [shifted(mine[s], "member", -s) for s in range(1, groups)]
        one = backward(first, per, back, w_out_t, slope, tiles, place)
        first += per
        dpred.append(one[0])
        dpre.append(one[1])
        own.append(one[3])
        down.append(shifted(one[2], "region", -1))
        up.append(shifted(one[4], "region", 1))
    hidden, output = weight_gradients(x, act, dpre, dpred, place, (up[0], down[0]))
    out = None
    first = 0
    for i, per in enumerate(parts):
        out = finish(first, members, own[i], up[i], down[i], w_hidden_t, out)
        first += per
    return hidden, output, out


def turn_sets(groups):
    return [list(range(groups - 1, 0, -1)), [0]]


def shares(members):
    return [1, 3]


def solution(mesh):
    placed = (
        P("member", "region", None),
        P(),
        P(),
        P(),
        P(),
        P(None, "region"),
        P(),
        P("region", None, None, None),
        P("region", None),
    )
    return jax.shard_map(
        body,
        mesh=mesh,
        in_specs=placed,
        out_specs=(
            P(("member", "region"), None),
            P(("member", "region"), None),
            P("member", "region", None),
        ),
        check_vma=False,
    )
```

time: 132 us -> 99.4 us (0.75)
  the two profiles are of different devices: /device:TPU:3 before, /device:TPU:8 now
where the time goes in v2:
time: 99.4 us; the launch traced here: 99.2 us
  Pallas kernels  34.2 us (34%)
  waiting for transfers between devices  34.1 us (34%)
  starting transfers between devices  28.3 us (28%)
  local copies, waits for them, and re-layouts  1.64 us (2%)
    ppermute x16, waiting for transfers between devices, shifted(): lax.ppermute(block, axis, [((i - distance) % count, i) for i in range(cou...  34 us
    ppermute x16, starting transfers between devices, shifted(): lax.ppermute(block, axis, [((i - distance) % count, i) for i in range(cou...  22.6 us
    pallas_call x1, Pallas kernels, forward(): pl.pallas_call(functools.partial(forward_kernel, pieces), in_specs=[ON_SM...  10.6 us
    pallas_call x2, Pallas kernels, weights(): pl.pallas_call(functools.partial(weights_kernel, turns, groups, cores), i...  7.06 us
    pallas_call x2, Pallas kernels, backward(): pl.pallas_call(functools.partial(backward_kernel, first, pieces), in_spec...  6.47 us
    pallas_call x2, Pallas kernels, finish(): pl.pallas_call(functools.partial(finish_kernel, first), in_specs=[ON_VMEM...  4.62 us
    ppermute x3, starting transfers between devices, weight_gradients(): given.append(lax.ppermute(parts[s], 'region', route))  4.59 us
    pallas_call x1, Pallas kernels, score(): pl.pallas_call(functools.partial(score_kernel, pieces), in_specs=[ON_SMEM...  2.36 us
  transfers between devices with their start and end apart: 21, of which 7 were waited for; matrix products, arithmetic and copies ran while one was open for 0% of the time, Pallas kernels for 21%

profile of v2, /device:TPU:8, one launch (start us, length us, event | category | flops | bytes accessed | tf_op | source)
XLA Modules:
  0.0 99.2 jit_solution(12861802243572127811)
XLA Ops:
  0.6 0.1 pad_add_fusion.place
  0.7 0.9 copy-done.1
  1.6 0.7 copy-done.7
  2.3 0.0 copy-start.4
  2.3 10.6 %forward.1 = (bf16[4,512,1024]{2,1,0:T(8,128)(2,1)S(1)}, bf16[1024,1024]{1,0:T(8,128)(2,1)S(1)}, bf16[4,512,1024]{2,1,0:T(8,128)(2,1)S(1)}, bf16[4,512,1024]{2,1...) custom-call(s32[2]{0:T(128)S(1)} %pad_add_fusion.place, ...), custom_call_target="tpu_custom_call" | custom-call | flops 5368709120 | bytes 14680064 | tf_op jit(solution)/shard_map/forward/pallas_call | solution.py:90
  12.9 0.0 copy-start.2
  12.9 1.6 %collective-permute-start = (bf16[5,96,128]{2,1,0:T(8,128)(2,1)S(1)}, bf16[5,96,128]{2,1,0:T(8,128)(2,1)S(1)}, u32[]{:S(2)}, u32[]{:S(2)}) collective-permute-start(bf16[5,96,128]{2,1,0:T(8,128)(2,1)S(1)} %get-tuple-element.52), channel_id=1, source_target_pairs={{24,0},{0,8},{8,16},{16,24},{25,1},{1,9},{9,17},{17,25},{26,2},{2,... | collective-permute-start | bytes 368648 | tf_op jit(solution)/shard_map/ppermute | solution.py:24
  14.5 1.1 %collective-permute-start.1 = (bf16[5,96,128]{2,1,0:T(8,128)(2,1)S(1)}, bf16[5,96,128]{2,1,0:T(8,128)(2,1)S(1)}, u32[]{:S(2)}, u32[]{:S(2)}) collective-permute-start(bf16[5,96,128]{2,1,0:T(8,128)(2,1)S(1)} %get-tuple-element.53), channel_id=1, source_target_pairs={{16,0},{24,8},{0,16},{8,24},{17,1},{25,9},{1,17},{9,25},{18,2},{26... | collective-permute-start | bytes 368648 | tf_op jit(solution)/shard_map/ppermute | solution.py:24
  15.6 1.9 %collective-permute-start.2 = (bf16[5,96,128]{2,1,0:T(8,128)(2,1)S(1)}, bf16[5,96,128]{2,1,0:T(8,128)(2,1)S(1)}, u32[]{:S(2)}, u32[]{:S(2)}) collective-permute-start(bf16[5,96,128]{2,1,0:T(8,128)(2,1)S(1)} %get-tuple-element.54), channel_id=1, source_target_pairs={{8,0},{16,8},{24,16},{0,24},{9,1},{17,9},{25,17},{1,25},{10,2},{18... | collective-permute-start | bytes 368648 | tf_op jit(solution)/shard_map/ppermute | solution.py:24
  17.6 6.0 %collective-permute-done.refs_1_ = bf16[5,96,128]{2,1,0:T(8,128)(2,1)S(1)} collective-permute-done((bf16[5,96,128]{2,1,0:T(8,128)(2,1)S(1)}, bf16[5,96,128]{2,1,0:T(8,128)(2,1)S(1)}, u32[]{:S(2)}, u32[]{:S(2)}) %collective-permute-start) | collective-permute-done | bytes 122912 | tf_op jit(solution)/shard_map/ppermute | solution.py:24
  23.5 1.5 %collective-permute-done.1.refs_2_ = bf16[5,96,128]{2,1,0:T(8,128)(2,1)S(1)} collective-permute-done((bf16[5,96,128]{2,1,0:T(8,128)(2,1)S(1)}, bf16[5,96,128]{2,1,0:T(8,128)(2,1)S(1)}, u32[]{:S(2)}, u32[]{:S(2)}) %collective-permute-start.1) | collective-permute-done | bytes 122912 | tf_op jit(solution)/shard_map/ppermute | solution.py:24
  25.0 1.8 %collective-permute-done.2.refs_3_ = bf16[5,96,128]{2,1,0:T(8,128)(2,1)S(1)} collective-permute-done((bf16[5,96,128]{2,1,0:T(8,128)(2,1)S(1)}, bf16[5,96,128]{2,1,0:T(8,128)(2,1)S(1)}, u32[]{:S(2)}, u32[]{:S(2)}) %collective-permute-start.2) | collective-permute-done | bytes 122912 | tf_op jit(solution)/shard_map/ppermute | solution.py:24
  26.8 2.4 %score.1 = (bf16[1,96,128]{2,1,0:T(8,128)(2,1)S(1)}, bf16[1,96,128]{2,1,0:T(8,128)(2,1)S(1)}, bf16[1,96,128]{2,1,0:T(8,128)(2,1)S(1)}, bf16[1,96,128]{2,1,0:T(8,...) custom-call(s32[2]{0:T(128)S(1)} %pad_add_fusion.place, ...), custom_call_target="tpu_custom_call" | custom-call | flops 40000000 | bytes 1048576 | tf_op jit(solution)/shard_map/score/pallas_call | solution.py:155
  29.2 0.1 collective-permute-start.3
  29.2 1.7 %collective-permute-start.4 = (bf16[1,96,128]{2,1,0:T(8,128)(2,1)S(1)}, bf16[1,96,128]{2,1,0:T(8,128)(2,1)S(1)}, u32[]{:S(2)}, u32[]{:S(2)}) collective-permute-start(bf16[1,96,128]{2,1,0:T(8,128)(2,1)S(1)} %get-tuple-element.57), channel_id=1, source_target_pairs={{16,0},{24,8},{0,16},{8,24},{17,1},{25,9},{1,17},{9,25},{18,2},{26... | collective-permute-start | bytes 73736 | tf_op jit(solution)/shard_map/ppermute | solution.py:24
  30.9 2.8 %collective-permute-start.5 = (bf16[1,96,128]{2,1,0:T(8,128)(2,1)S(1)}, bf16[1,96,128]{2,1,0:T(8,128)(2,1)S(1)}, u32[]{:S(2)}, u32[]{:S(2)}) collective-permute-start(bf16[1,96,128]{2,1,0:T(8,128)(2,1)S(1)} %get-tuple-element.58), channel_id=1, source_target_pairs={{24,0},{0,8},{8,16},{16,24},{25,1},{1,9},{9,17},{17,25},{26,2},{2,... | collective-permute-start | bytes 73736 | tf_op jit(solution)/shard_map/ppermute | solution.py:24
  33.8 1.5 %tiles.1 = (bf16[768,512]{1,0:T(8,128)(2,1)S(1)}, bf16[1024,1024]{1,0:T(8,128)(2,1)S(1)}) custom-call(s32[2]{0:T(128)S(1)} %pad_add_fusion.place, s32[4,3]{1,0:T(4,128)S(1)} %copy-done.4, bf16[4,3,128,128]{3,2,1,0:T(8,128)(2,1)S(1)} %copy-done, bf16[1024,1024]{1,0:T(8,128)(2,1)S(1)} %get-tuple-element.49.w_ref), custom_call_target="tpu_custom_call" | custom-call | flops 4000000 | bytes 2097152 | tf_op jit(solution)/shard_map/tiles/pallas_call | solution.py:187
  35.3 0.1 collective-permute-start.6
  35.4 1.5 %collective-permute-start.7 = (bf16[3,96,128]{2,1,0:T(8,128)(2,1)S(1)}, bf16[3,96,128]{2,1,0:T(8,128)(2,1)S(1)}, u32[]{:S(2)}, u32[]{:S(2)}) collective-permute-start(bf16[3,96,128]{2,1,0:T(8,128)(2,1)S(1)} %get-tuple-element.62), channel_id=1, source_target_pairs={{16,0},{24,8},{0,16},{8,24},{17,1},{25,9},{1,17},{9,25},{18,2},{26... | collective-permute-start | bytes 221192 | tf_op jit(solution)/shard_map/ppermute | solution.py:24
  36.8 2.7 %collective-permute-start.8 = (bf16[3,96,128]{2,1,0:T(8,128)(2,1)S(1)}, bf16[3,96,128]{2,1,0:T(8,128)(2,1)S(1)}, u32[]{:S(2)}, u32[]{:S(2)}) collective-permute-start(bf16[3,96,128]{2,1,0:T(8,128)(2,1)S(1)} %get-tuple-element.63), channel_id=1, source_target_pairs={{24,0},{0,8},{8,16},{16,24},{25,1},{1,9},{9,17},{17,25},{26,2},{2,... | collective-permute-start | bytes 221192 | tf_op jit(solution)/shard_map/ppermute | solution.py:24
  39.6 2.0 %backward.2 = (bf16[1,512,96]{2,1,0:T(8,128)(2,1)S(1)}, bf16[1,512,1024]{2,1,0:T(8,128)(2,1)S(1)}, bf16[1,256,1024]{2,1,0:T(8,128)(2,1)S(1)}, bf16[1,256,1024]{2,1,0:T(8,128)(2,1)S(1)}, bf16[1,256,1024]{2,1,0:T(8,128)(2,1)S(1)}) custom-call(s32[2]{0:T(128)S(1)} %pad_add_fusion.place, bf16[96,1024]{1,0:T(8,128)(2,1)S(1)} %bitcast.7, ...), custom_call_target="tpu_custom_call" | custom-call | flops 1073741824 | bytes 5242880 | tf_op jit(solution)/shard_map/backward/pallas_call | solution.py:229
  41.6 0.1 collective-permute-start.10
  41.7 2.6 %collective-permute-start.11 = (bf16[1,256,1024]{2,1,0:T(8,128)(2,1)S(1)}, bf16[1,256,1024]{2,1,0:T(8,128)(2,1)S(1)}, u32[]{:S(2)}, u32[]{:S(2)}) collective-permute-start(bf16[1,256,1024]{2,1,0:T(8,128)(2,1)S(1)} %get-tuple-element.72), channel_id=1, source_target_pairs={{1,0},{2,1},{3,2},{4,3},{5,4},{6,5},{7,6},{0,7},{9,8},{10,9},{11,1... | collective-permute-start | bytes 1572872 | tf_op jit(solution)/shard_map/ppermute | solution.py:24
  44.3 0.0 collective-permute-done.6.refs_1_
  44.3 0.0 collective-permute-done.7.refs_2_
  44.3 4.5 %backward.3 = (bf16[3,512,96]{2,1,0:T(8,128)(2,1)S(1)}, bf16[3,512,1024]{2,1,0:T(8,128)(2,1)S(1)}, bf16[3,256,1024]{2,1,0:T(8,128)(2,1)S(1)}, bf16[3,256,1024]{2,1,0:T(8,128)(2,1)S(1)}, bf16[3,256,1024]{2,1,0:T(8,128)(2,1)S(1)}) custom-call(s32[2]{0:T(128)S(1)} %pad_add_fusion.place, bf16[96,1024]{1,0:T(8,128)(2,1)S(1)} %bitcast.8, ...), custom_call_target="tpu_custom_call" | custom-call | flops 3221225472 | bytes 5242880 | tf_op jit(solution)/shard_map/backward/pallas_call | solution.py:229
  48.8 0.1 collective-permute-start.19
  48.8 2.6 %collective-permute-start.20 = (bf16[3,256,1024]{2,1,0:T(8,128)(2,1)S(1)}, bf16[3,256,1024]{2,1,0:T(8,128)(2,1)S(1)}, u32[]{:S(2)}, u32[]{:S(2)}) collective-permute-start(bf16[3,256,1024]{2,1,0:T(8,128)(2,1)S(1)} %get-tuple-element.86), channel_id=1, source_target_pairs={{1,0},{2,1},{3,2},{4,3},{5,4},{6,5},{7,6},{0,7},{9,8},{10,9},{11,1... | collective-permute-start | bytes 4718600 | tf_op jit(solution)/shard_map/ppermute | solution.py:24
  51.5 4.9 %weights.3 = (bf16[12,32,1120]{2,1,0:T(8,128)(2,1)S(1)}, bf16[12,32,1120]{2,1,0:T(8,128)(2,1)S(1)}) custom-call(s32[2]{0:T(128)S(1)} %pad_add_fusion.place, bf16[4,512,1024]{2,1,0:T(8,128)(2,1)S(1)} %get-tuple-element.46.x_ref, bf16[4,512,1024]{2,1,0:T(8,128)(2,1)S(1)} %get-tuple-element.47.act_ref, bf16[1,512,1024]{2,1,0:T(8,128)(2,1)S(1)} %get-tuple-element.59.refs_0_, ...), custom_call_target="tpu_custom_call" | custom-call | flops 1000 | bytes 1000 | tf_op jit(solution)/shard_map/weights/pallas_call | solution.py:285
  56.4 0.3 collective-permute-done.11.down_ref
  56.7 1.1 %collective-permute-start.12 = (bf16[12,32,1120]{2,1,0:T(8,128)(2,1)S(1)}, bf16[12,32,1120]{2,1,0:T(8,128)(2,1)S(1)}, u32[]{:S(2)}, u32[]{:S(2)}) collective-permute-start(bf16[12,32,1120]{2,1,0:T(8,128)(2,1)S(1)} %get-tuple-element.74), channel_id=1, source_target_pairs={{0,1},{1,0},{2,3},{3,2},{4,5},{5,4},{6,7},{7,6},{8,9},{9,8},{10,11... | collective-permute-start | bytes 2580488 | tf_op jit(solution)/shard_map/ppermute | solution.py:385
  57.7 2.1 %weights.2 = (bf16[4,32,1120]{2,1,0:T(8,128)(2,1)S(1)}, bf16[4,32,1120]{2,1,0:T(8,128)(2,1)S(1)}) custom-call(s32[2]{0:T(128)S(1)} %pad_add_fusion.place, bf16[4,512,1024]{2,1,0:T(8,128)(2,1)S(1)} %get-tuple-element.46.x_ref, bf16[4,512,1024]{2,1,0:T(8,128)(2,1)S(1)} %get-tuple-element.47.act_ref, bf16[1,512,1024]{2,1,0:T(8,128)(2,1)S(1)} %get-tuple-element.59.refs_0_, ...), custom_call_target="tpu_custom_call" | custom-call | flops 1000 | bytes 1000 | tf_op jit(solution)/shard_map/weights/pallas_call | solution.py:285
  59.9 0.1 collective-permute-start.9
  60.0 0.2 add.5
  60.2 0.1 collective-permute-start.13
  60.3 2.4 %collective-permute-start.14 = (bf16[4,32,1120]{2,1,0:T(8,128)(2,1)S(1)}, bf16[4,32,1120]{2,1,0:T(8,128)(2,1)S(1)}, u32[]{:S(2)}, u32[]{:S(2)}) collective-permute-start(bf16[4,32,1120]{2,1,0:T(8,128)(2,1)S(1)} %get-tuple-element.76), channel_id=1, source_target_pairs={{16,0},{24,8},{0,16},{8,24},{17,1},{25,9},{1,17},{9,25},{18,2},{26... | collective-permute-start | bytes 860168 | tf_op jit(solution)/shard_map/ppermute | solution.py:24
  62.6 1.3 %collective-permute-start.15 = (bf16[4,32,1120]{2,1,0:T(8,128)(2,1)S(1)}, bf16[4,32,1120]{2,1,0:T(8,128)(2,1)S(1)}, u32[]{:S(2)}, u32[]{:S(2)}) collective-permute-start(bf16[4,32,1120]{2,1,0:T(8,128)(2,1)S(1)} %get-tuple-element.77), channel_id=1, source_target_pairs={{8,0},{16,8},{24,16},{0,24},{9,1},{17,9},{25,17},{1,25},{10,2},{18... | collective-permute-start | bytes 860168 | tf_op jit(solution)/shard_map/ppermute | solution.py:24
  63.9 0.1 add.4.refs_0_
  64.0 6.1 %collective-permute-done.13.refs_1_ = bf16[4,32,1120]{2,1,0:T(8,128)(2,1)S(1)} collective-permute-done((bf16[4,32,1120]{2,1,0:T(8,128)(2,1)S(1)}, bf16[4,32,1120]{2,1,0:T(8,128)(2,1)S(1)}, u32[]{:S(2)}, u32[]{:S(2)}) %collective-permute-start.13) | collective-permute-done | bytes 286752 | tf_op jit(solution)/shard_map/ppermute | solution.py:24
  70.1 16.4 %collective-permute-done.14.refs_2_ = bf16[4,32,1120]{2,1,0:T(8,128)(2,1)S(1)} collective-permute-done((bf16[4,32,1120]{2,1,0:T(8,128)(2,1)S(1)}, bf16[4,32,1120]{2,1,0:T(8,128)(2,1)S(1)}, u32[]{:S(2)}, u32[]{:S(2)}) %collective-permute-start.14) | collective-permute-done | bytes 286752 | tf_op jit(solution)/shard_map/ppermute | solution.py:24
  86.4 2.1 %collective-permute-done.15.refs_3_ = bf16[4,32,1120]{2,1,0:T(8,128)(2,1)S(1)} collective-permute-done((bf16[4,32,1120]{2,1,0:T(8,128)(2,1)S(1)}, bf16[4,32,1120]{2,1,0:T(8,128)(2,1)S(1)}, u32[]{:S(2)}, u32[]{:S(2)}) %collective-permute-start.15) | collective-permute-done | bytes 286752 | tf_op jit(solution)/shard_map/ppermute | solution.py:24
  88.5 0.7 split.1
  89.3 2.2 %collective-permute-start.16 = (bf16[1,32,1120]{2,1,0:T(8,128)(2,1)S(1)}, bf16[1,32,1120]{2,1,0:T(8,128)(2,1)S(1)}, u32[]{:S(2)}, u32[]{:S(2)}) collective-permute-start(bf16[1,32,1120]{2,1,0:T(8,128)(2,1)S(1)} %get-tuple-element.79), channel_id=1, source_target_pairs={{0,2},{1,3},{2,4},{3,5},{4,6},{5,7},{6,0},{7,1},{8,10},{9,11},{10,... | collective-permute-start | bytes 215048 | tf_op jit(solution)/shard_map/ppermute | solution.py:393
  91.5 0.5 collective-permute-start.17
  92.0 1.9 %collective-permute-start.18 = (bf16[1,32,1120]{2,1,0:T(8,128)(2,1)S(1)}, bf16[1,32,1120]{2,1,0:T(8,128)(2,1)S(1)}, u32[]{:S(2)}, u32[]{:S(2)}) collective-permute-start(bf16[1,32,1120]{2,1,0:T(8,128)(2,1)S(1)} %get-tuple-element.81), channel_id=1, source_target_pairs={{0,6},{1,7},{2,0},{3,1},{4,2},{5,3},{6,4},{7,5},{8,14},{9,15},{10,... | collective-permute-start | bytes 215048 | tf_op jit(solution)/shard_map/ppermute | solution.py:393
  93.8 1.7 %finish.2.refs_0_ = f32[4,256,1024]{2,1,0:T(8,128)} custom-call(bf16[1,256,1024]{2,1,0:T(8,128)(2,1)S(1)} %get-tuple-element.88.own_ref, bf16[1,256,1024]{2,1,0:T(8,128)(2,1)S(1)} %collective-permute-done.10.up_ref, bf16[1,256,1024]{2,1,0:T(8,128)(2,1)S(1)} %collective-permute-done.11.down_ref, bf16[1024,1024]{1,0:T(8,128)(2,1)S(1)} %get-tuple-element.87.w_ref), custom_call_target="tpu_custom_call" | custom-call | flops 1000 | bytes 1000 | tf_op jit(solution)/shard_map/finish/pallas_call | solution.py:412
  95.6 2.9 %finish.3 = f32[4,256,1024]{2,1,0:T(8,128)} custom-call(bf16[3,256,1024]{2,1,0:T(8,128)(2,1)S(1)} %get-tuple-element.84.own_ref, bf16[3,256,1024]{2,1,0:T(8,128)(2,1)S(1)} %collective-permute-done.19.up_ref, bf16[3,256,1024]{2,1,0:T(8,128)(2,1)S(1)} %collective-permute-done.20.down_ref, ...), custom_call_target="tpu_custom_call", output_to_operand_aliasing={{}: (4, {})} | custom-call | flops 1000 | bytes 1000 | tf_op jit(solution)/shard_map/finish/pallas_call | solution.py:412
  98.5 0.7 total.1
  (24 shorter events, 0.1 us)
Async XLA Ops:
  0.7 0.9 copy-start.1
  1.6 0.7 copy-start.7
  2.3 24.5 %copy-start.3 = (f32[96,512]{1,0:T(8,128)S(1)}, f32[96,512]{1,0:T(8,128)}, u32[]{:S(2)}) copy-start(f32[96,512]{1,0:T(8,128)} %target_ref.1) | copy-start | bytes 589828
  2.3 24.5 %copy-start.5 = (f32[96]{0:T(128)S(1)}, f32[96]{0:T(128)}, u32[]{:S(2)}) copy-start(f32[96]{0:T(128)} %param.13) | copy-start | bytes 1156
  2.3 24.5 %copy-start.6 = (f32[96]{0:T(128)S(1)}, f32[96]{0:T(128)}, u32[]{:S(2)}) copy-start(f32[96]{0:T(128)} %param.15) | copy-start | bytes 1156
  2.3 31.5 %copy-start = (bf16[4,3,128,128]{3,2,1,0:T(8,128)(2,1)S(1)}, bf16[4,3,128,128]{3,2,1,0:T(8,128)(2,1)}, u32[]{:S(2)}) copy-start(bf16[4,3,128,128]{3,2,1,0:T(8,128)(2,1)} %tile_ref.1) | copy-start | bytes 1179652
  2.3 31.4 %copy-start.4 = (s32[4,3]{1,0:T(4,128)S(1)}, s32[4,3]{1,0:T(4,128)}, u32[]{:S(2)}) copy-start(s32[4,3]{1,0:T(4,128)} %index_ref.1) | copy-start | bytes 148
  12.9 26.7 %copy-start.2 = (bf16[1024,96]{0,1:T(8,128)(2,1)S(1)}, bf16[1024,96]{0,1:T(8,128)(2,1)}, u32[]{:S(2)}) copy-start(bf16[1024,96]{0,1:T(8,128)(2,1)} %param.12) | copy-start | bytes 589828
  12.9 10.6 %collective-permute-start = (bf16[5,96,128]{2,1,0:T(8,128)(2,1)S(1)}, bf16[5,96,128]{2,1,0:T(8,128)(2,1)S(1)}, u32[]{:S(2)}, u32[]{:S(2)}) collective-permute-start(bf16[5,96,128]{2,1,0:T(8,128)(2,1)S(1)} %get-tuple-element.52), channel_id=1, source_target_pairs={{24,0},{0,8},{8,16},{16,24},{25,1},{1,9},{9,17},{17,25},{26,2},{2,... | collective-permute-start | bytes 368648 | tf_op jit(solution)/shard_map/ppermute | solution.py:24
  14.5 10.5 %collective-permute-start.1 = (bf16[5,96,128]{2,1,0:T(8,128)(2,1)S(1)}, bf16[5,96,128]{2,1,0:T(8,128)(2,1)S(1)}, u32[]{:S(2)}, u32[]{:S(2)}) collective-permute-start(bf16[5,96,128]{2,1,0:T(8,128)(2,1)S(1)} %get-tuple-element.53), channel_id=1, source_target_pairs={{16,0},{24,8},{0,16},{8,24},{17,1},{25,9},{1,17},{9,25},{18,2},{26... | collective-permute-start | bytes 368648 | tf_op jit(solution)/shard_map/ppermute | solution.py:24
  15.6 11.1 %collective-permute-start.2 = (bf16[5,96,128]{2,1,0:T(8,128)(2,1)S(1)}, bf16[5,96,128]{2,1,0:T(8,128)(2,1)S(1)}, u32[]{:S(2)}, u32[]{:S(2)}) collective-permute-start(bf16[5,96,128]{2,1,0:T(8,128)(2,1)S(1)} %get-tuple-element.54), channel_id=1, source_target_pairs={{8,0},{16,8},{24,16},{0,24},{9,1},{17,9},{25,17},{1,25},{10,2},{18... | collective-permute-start | bytes 368648 | tf_op jit(solution)/shard_map/ppermute | solution.py:24
  29.2 7.7 %collective-permute-start.3 = (bf16[1,96,128]{2,1,0:T(8,128)(2,1)S(1)}, bf16[1,96,128]{2,1,0:T(8,128)(2,1)S(1)}, u32[]{:S(2)}, u32[]{:S(2)}) collective-permute-start(bf16[1,96,128]{2,1,0:T(8,128)(2,1)S(1)} %get-tuple-element.56), channel_id=1, source_target_pairs={{8,0},{16,8},{24,16},{0,24},{9,1},{17,9},{25,17},{1,25},{10,2},{18... | collective-permute-start | bytes 73736 | tf_op jit(solution)/shard_map/ppermute | solution.py:24
  29.2 10.3 %collective-permute-start.4 = (bf16[1,96,128]{2,1,0:T(8,128)(2,1)S(1)}, bf16[1,96,128]{2,1,0:T(8,128)(2,1)S(1)}, u32[]{:S(2)}, u32[]{:S(2)}) collective-permute-start(bf16[1,96,128]{2,1,0:T(8,128)(2,1)S(1)} %get-tuple-element.57), channel_id=1, source_target_pairs={{16,0},{24,8},{0,16},{8,24},{17,1},{25,9},{1,17},{9,25},{18,2},{26... | collective-permute-start | bytes 73736 | tf_op jit(solution)/shard_map/ppermute | solution.py:24
  30.9 8.6 %collective-permute-start.5 = (bf16[1,96,128]{2,1,0:T(8,128)(2,1)S(1)}, bf16[1,96,128]{2,1,0:T(8,128)(2,1)S(1)}, u32[]{:S(2)}, u32[]{:S(2)}) collective-permute-start(bf16[1,96,128]{2,1,0:T(8,128)(2,1)S(1)} %get-tuple-element.58), channel_id=1, source_target_pairs={{24,0},{0,8},{8,16},{16,24},{25,1},{1,9},{9,17},{17,25},{26,2},{2,... | collective-permute-start | bytes 73736 | tf_op jit(solution)/shard_map/ppermute | solution.py:24
  35.3 9.0 %collective-permute-start.6 = (bf16[3,96,128]{2,1,0:T(8,128)(2,1)S(1)}, bf16[3,96,128]{2,1,0:T(8,128)(2,1)S(1)}, u32[]{:S(2)}, u32[]{:S(2)}) collective-permute-start(bf16[3,96,128]{2,1,0:T(8,128)(2,1)S(1)} %get-tuple-element.61), channel_id=1, source_target_pairs={{8,0},{16,8},{24,16},{0,24},{9,1},{17,9},{25,17},{1,25},{10,2},{18... | collective-permute-start | bytes 221192 | tf_op jit(solution)/shard_map/ppermute | solution.py:24
  35.4 8.9 %collective-permute-start.7 = (bf16[3,96,128]{2,1,0:T(8,128)(2,1)S(1)}, bf16[3,96,128]{2,1,0:T(8,128)(2,1)S(1)}, u32[]{:S(2)}, u32[]{:S(2)}) collective-permute-start(bf16[3,96,128]{2,1,0:T(8,128)(2,1)S(1)} %get-tuple-element.62), channel_id=1, source_target_pairs={{16,0},{24,8},{0,16},{8,24},{17,1},{25,9},{1,17},{9,25},{18,2},{26... | collective-permute-start | bytes 221192 | tf_op jit(solution)/shard_map/ppermute | solution.py:24
  36.8 7.5 %collective-permute-start.8 = (bf16[3,96,128]{2,1,0:T(8,128)(2,1)S(1)}, bf16[3,96,128]{2,1,0:T(8,128)(2,1)S(1)}, u32[]{:S(2)}, u32[]{:S(2)}) collective-permute-start(bf16[3,96,128]{2,1,0:T(8,128)(2,1)S(1)} %get-tuple-element.63), channel_id=1, source_target_pairs={{24,0},{0,8},{8,16},{16,24},{25,1},{1,9},{9,17},{17,25},{26,2},{2,... | collective-permute-start | bytes 221192 | tf_op jit(solution)/shard_map/ppermute | solution.py:24
  41.6 14.8 %collective-permute-start.10 = (bf16[1,256,1024]{2,1,0:T(8,128)(2,1)S(1)}, bf16[1,256,1024]{2,1,0:T(8,128)(2,1)S(1)}, u32[]{:S(2)}, u32[]{:S(2)}) collective-permute-start(bf16[1,256,1024]{2,1,0:T(8,128)(2,1)S(1)} %get-tuple-element.71), channel_id=1, source_target_pairs={{7,0},{0,1},{1,2},{2,3},{3,4},{4,5},{5,6},{6,7},{15,8},{8,9},{9,10... | collective-permute-start | bytes 1572872 | tf_op jit(solution)/shard_map/ppermute | solution.py:24
  41.7 15.0 %collective-permute-start.11 = (bf16[1,256,1024]{2,1,0:T(8,128)(2,1)S(1)}, bf16[1,256,1024]{2,1,0:T(8,128)(2,1)S(1)}, u32[]{:S(2)}, u32[]{:S(2)}) collective-permute-start(bf16[1,256,1024]{2,1,0:T(8,128)(2,1)S(1)} %get-tuple-element.72), channel_id=1, source_target_pairs={{1,0},{2,1},{3,2},{4,3},{5,4},{6,5},{7,6},{0,7},{9,8},{10,9},{11,1... | collective-permute-start | bytes 1572872 | tf_op jit(solution)/shard_map/ppermute | solution.py:24
  48.8 46.8 %collective-permute-start.19 = (bf16[3,256,1024]{2,1,0:T(8,128)(2,1)S(1)}, bf16[3,256,1024]{2,1,0:T(8,128)(2,1)S(1)}, u32[]{:S(2)}, u32[]{:S(2)}) collective-permute-start(bf16[3,256,1024]{2,1,0:T(8,128)(2,1)S(1)} %get-tuple-element.85), channel_id=1, source_target_pairs={{7,0},{0,1},{1,2},{2,3},{3,4},{4,5},{5,6},{6,7},{15,8},{8,9},{9,10... | collective-permute-start | bytes 4718600 | tf_op jit(solution)/shard_map/ppermute | solution.py:24
  48.8 46.8 %collective-permute-start.20 = (bf16[3,256,1024]{2,1,0:T(8,128)(2,1)S(1)}, bf16[3,256,1024]{2,1,0:T(8,128)(2,1)S(1)}, u32[]{:S(2)}, u32[]{:S(2)}) collective-permute-start(bf16[3,256,1024]{2,1,0:T(8,128)(2,1)S(1)} %get-tuple-element.86), channel_id=1, source_target_pairs={{1,0},{2,1},{3,2},{4,3},{5,4},{6,5},{7,6},{0,7},{9,8},{10,9},{11,1... | collective-permute-start | bytes 4718600 | tf_op jit(solution)/shard_map/ppermute | solution.py:24
  56.7 3.3 %collective-permute-start.12 = (bf16[12,32,1120]{2,1,0:T(8,128)(2,1)S(1)}, bf16[12,32,1120]{2,1,0:T(8,128)(2,1)S(1)}, u32[]{:S(2)}, u32[]{:S(2)}) collective-permute-start(bf16[12,32,1120]{2,1,0:T(8,128)(2,1)S(1)} %get-tuple-element.74), channel_id=1, source_target_pairs={{0,1},{1,0},{2,3},{3,2},{4,5},{5,4},{6,7},{7,6},{8,9},{9,8},{10,11... | collective-permute-start | bytes 2580488 | tf_op jit(solution)/shard_map/ppermute | solution.py:385
  59.9 2.7 %collective-permute-start.9 = (bf16[4,32,1120]{2,1,0:T(8,128)(2,1)S(1)}, bf16[4,32,1120]{2,1,0:T(8,128)(2,1)S(1)}, u32[]{:S(2)}, u32[]{:S(2)}) collective-permute-start(bf16[4,32,1120]{2,1,0:T(8,128)(2,1)S(1)} %get-tuple-element.68), channel_id=1, source_target_pairs={{0,1},{1,0},{2,3},{3,2},{4,5},{5,4},{6,7},{7,6},{8,9},{9,8},{10,11... | collective-permute-start | bytes 860168 | tf_op jit(solution)/shard_map/ppermute | solution.py:385
  60.2 9.9 %collective-permute-start.13 = (bf16[4,32,1120]{2,1,0:T(8,128)(2,1)S(1)}, bf16[4,32,1120]{2,1,0:T(8,128)(2,1)S(1)}, u32[]{:S(2)}, u32[]{:S(2)}) collective-permute-start(bf16[4,32,1120]{2,1,0:T(8,128)(2,1)S(1)} %get-tuple-element.75), channel_id=1, source_target_pairs={{24,0},{0,8},{8,16},{16,24},{25,1},{1,9},{9,17},{17,25},{26,2},{2,... | collective-permute-start | bytes 860168 | tf_op jit(solution)/shard_map/ppermute | solution.py:24
  60.3 26.1 %collective-permute-start.14 = (bf16[4,32,1120]{2,1,0:T(8,128)(2,1)S(1)}, bf16[4,32,1120]{2,1,0:T(8,128)(2,1)S(1)}, u32[]{:S(2)}, u32[]{:S(2)}) collective-permute-start(bf16[4,32,1120]{2,1,0:T(8,128)(2,1)S(1)} %get-tuple-element.76), channel_id=1, source_target_pairs={{16,0},{24,8},{0,16},{8,24},{17,1},{25,9},{1,17},{9,25},{18,2},{26... | collective-permute-start | bytes 860168 | tf_op jit(solution)/shard_map/ppermute | solution.py:24
  62.6 25.9 %collective-permute-start.15 = (bf16[4,32,1120]{2,1,0:T(8,128)(2,1)S(1)}, bf16[4,32,1120]{2,1,0:T(8,128)(2,1)S(1)}, u32[]{:S(2)}, u32[]{:S(2)}) collective-permute-start(bf16[4,32,1120]{2,1,0:T(8,128)(2,1)S(1)} %get-tuple-element.77), channel_id=1, source_target_pairs={{8,0},{16,8},{24,16},{0,24},{9,1},{17,9},{25,17},{1,25},{10,2},{18... | collective-permute-start | bytes 860168 | tf_op jit(solution)/shard_map/ppermute | solution.py:24
  89.3 9.3 %collective-permute-start.16 = (bf16[1,32,1120]{2,1,0:T(8,128)(2,1)S(1)}, bf16[1,32,1120]{2,1,0:T(8,128)(2,1)S(1)}, u32[]{:S(2)}, u32[]{:S(2)}) collective-permute-start(bf16[1,32,1120]{2,1,0:T(8,128)(2,1)S(1)} %get-tuple-element.79), channel_id=1, source_target_pairs={{0,2},{1,3},{2,4},{3,5},{4,6},{5,7},{6,0},{7,1},{8,10},{9,11},{10,... | collective-permute-start | bytes 215048 | tf_op jit(solution)/shard_map/ppermute | solution.py:393
  91.5 7.0 %collective-permute-start.17 = (bf16[1,32,1120]{2,1,0:T(8,128)(2,1)S(1)}, bf16[1,32,1120]{2,1,0:T(8,128)(2,1)S(1)}, u32[]{:S(2)}, u32[]{:S(2)}) collective-permute-start(bf16[1,32,1120]{2,1,0:T(8,128)(2,1)S(1)} %get-tuple-element.80), channel_id=1, source_target_pairs={{0,4},{1,5},{2,6},{3,7},{4,0},{5,1},{6,2},{7,3},{8,12},{9,13},{10,... | collective-permute-start | bytes 215048 | tf_op jit(solution)/shard_map/ppermute | solution.py:393
  92.0 6.5 %collective-permute-start.18 = (bf16[1,32,1120]{2,1,0:T(8,128)(2,1)S(1)}, bf16[1,32,1120]{2,1,0:T(8,128)(2,1)S(1)}, u32[]{:S(2)}, u32[]{:S(2)}) collective-permute-start(bf16[1,32,1120]{2,1,0:T(8,128)(2,1)S(1)} %get-tuple-element.81), channel_id=1, source_target_pairs={{0,6},{1,7},{2,0},{3,1},{4,2},{5,3},{6,4},{7,5},{8,14},{9,15},{10,... | collective-permute-start | bytes 215048 | tf_op jit(solution)/shard_map/ppermute | solution.py:393

commit v3 on v2

--- a/solution.py
+++ b/solution.py
@@ -45,69 +45,108 @@
     return pl.CostEstimate(flops=int(flops), bytes_accessed=int(moved), transcendentals=0)
 
 
-def forward_kernel(
-    pieces, place, x_hbm, w_hbm, b_ref, wout_ref, x_ref, w_ref, act_ref, slope_ref, *rest
+def cells_forward(turn, place, pieces, x_ref, w_ref, b_ref, wout_ref, act_ref, slope_ref, send_ref):
+    members, cells, width = x_ref.shape
+    length = cells // pieces
+    at = lax.rem(place[0] + turn, pieces) * length
+    x = x_ref[:, pl.ds(pl.multiple_of(at, length), length), :].reshape(members * length, width)
+    each = 2 if members % 2 == 0 else 1
+    base = None
+    for m in range(0, members, each):
+        rows = x[m * length : (m + each) * length]
+        pre = jnp.dot(rows, w_ref[...], preferred_element_type=F32) + b_ref[...]
+        logistic = 0.5 * jnp.tanh(0.5 * pre) + 0.5
+        act = pre * logistic
+        slope = (logistic + act * (1.0 - logistic)).astype(BF16)
+        slope_ref[m : m + each] = slope.reshape(each, length, width)
+        act = act.astype(BF16)
+        act_ref[m : m + each] = act.reshape(each, length, width)
+        line = lax.dot_general(
+            wout_ref[...], act, (((1,), (1,)), ((), ())), preferred_element_type=F32
+        )
+        if m == 0:
+            first = line[:, :length].astype(BF16)
+            send_ref[0] = first
+            base = first.astype(F32)
+        for i in range(each):
+            send_ref[1 + m + i] = (line[:, i * length : (i + 1) * length] - base).astype(BF16)
+
+
+def first_kernel(
+    turn, pieces, place, x_hbm, w_hbm, b_hbm, wout_hbm, x_ref, w_ref, b_ref, wout_ref,
+    act_ref, slope_ref, send_ref, x_sems, sems
 ):
-    sends, line, base, x_sems, w_sem = rest[:pieces], *rest[pieces:]
-    members, cells, _ = x_ref.shape
-    length = sends[0].shape[2]
-    w_copy = pltpu.make_async_copy(w_hbm, w_ref, w_sem)
-    x_copies = [pltpu.make_async_copy(x_hbm.at[m], x_ref.at[m], x_sems.at[m]) for m in range(members)]
-    w_copy.start()
-    x_copies[0].start()
-    w_copy.wait()
+    length = x_ref.shape[1] // pieces
+    x_copies = []
+    for s in range(pieces):
+        at = lax.rem(place[0] + turn + s, pieces) * length
+        cells = pl.ds(pl.multiple_of(at, length), length)
+        x_copies.append(
+            pltpu.make_async_copy(x_hbm.at[:, cells, :], x_ref.at[:, cells, :], x_sems.at[s])
+        )
+    copies = [
+        pltpu.make_async_copy(b_hbm, b_ref, sems.at[0]),
+        pltpu.make_async_copy(w_hbm, w_ref, sems.at[1]),
+        pltpu.make_async_copy(wout_hbm, wout_ref, sems.at[2]),
+    ]
+    for copy in copies[:2] + x_copies[:1] + copies[2:]:
+        copy.start()
+    for copy in copies + x_copies[:1]:
+        copy.wait()
     for copy in x_copies[1:]:
         copy.start()
-    step = cells // 2
-    for m in range(members):
-        x_copies[m].wait()
-        for lo in range(0, cells, step):
-            rows = slice(lo, lo + step)
-            pre = jnp.dot(x_ref[m, rows, :], w_ref[...], preferred_element_type=F32) + b_ref[...]
-            logistic = 0.5 * jnp.tanh(0.5 * pre) + 0.5
-            act = pre * logistic
-            slope_ref[m, rows, :] = (logistic + act * (1.0 - logistic)).astype(BF16)
-            act = act.astype(BF16)
-            act_ref[m, rows, :] = act
-            part = lax.dot_general(
-                wout_ref[...], act, (((1,), (1,)), ((), ())), preferred_element_type=F32
-            )
-            if m == 0:
-                base[:, rows] = part.astype(BF16).astype(F32)
-            line[m, :, rows] = part - base[:, rows]
-    for s in range(pieces):
-        at = lax.rem(place[0] + s, pieces) * length
-        lanes = pl.ds(pl.multiple_of(at, length), length)
-        sends[s][0] = base[:, lanes].astype(BF16)
-        for m in range(members):
-            sends[s][1 + m] = line[m, :, lanes].astype(BF16)
+    cells_forward(turn, place, pieces, x_ref, w_ref, b_ref, wout_ref, act_ref, slope_ref, send_ref)
+    for copy in x_copies[1:]:
+        copy.wait()
+
+
+def later_kernel(turn, pieces, place, x_ref, w_ref, b_ref, wout_ref, act_ref, slope_ref, send_ref):
+    cells_forward(turn, place, pieces, x_ref, w_ref, b_ref, wout_ref, act_ref, slope_ref, send_ref)
 
 
 def forward(grid_input, w_hidden, b_hidden, w_out_t, place, pieces):
     members, cells, width = grid_input.shape
     channels = w_out_t.shape[0]
     length = cells // pieces
-    return pl.pallas_call(
-        functools.partial(forward_kernel, pieces),
-        in_specs=[ON_SMEM, ON_HBM, ON_HBM, ON_VMEM, ON_VMEM],
-        out_specs=[ON_VMEM] * (4 + pieces),
+    rows = pltpu.VMEM((members, length, width), BF16)
+    results = [rows, rows, pltpu.VMEM((members + 1, channels, length), BF16)]
+    turns = far_first(pieces)
+    estimate = cost(1000, 1000)
+    x, w, b, w_out, *one = pl.pallas_call(
+        functools.partial(first_kernel, turns[0], pieces),
+        in_specs=[ON_SMEM] + [ON_HBM] * 4,
+        out_specs=[ON_VMEM] * 7,
         out_shape=[
             pltpu.VMEM(grid_input.shape, BF16),
             pltpu.VMEM(w_hidden.shape, BF16),
-            pltpu.VMEM(grid_input.shape, BF16),
-            pltpu.VMEM(grid_input.shape, BF16),
+            pltpu.VMEM((1, width), F32),
+            pltpu.VMEM(w_out_t.shape, BF16),
         ]
-        + [pltpu.VMEM((members + 1, channels, length), BF16)] * pieces,
-        scratch_shapes=[
-            pltpu.VMEM((members, channels, cells), F32),
-            pltpu.VMEM((channels, cells), F32),
-            pltpu.SemaphoreType.DMA((members,)),
-            pltpu.SemaphoreType.DMA,
-        ],
-        compiler_params=params(),
-        cost_estimate=cost(2 * members * cells * width * (width + 256), 14 << 20),
+        + results,
+        scratch_shapes=[pltpu.SemaphoreType.DMA((pieces,)), pltpu.SemaphoreType.DMA((3,))],
+        compiler_params=params(),
+        cost_estimate=estimate,
         name="forward",
-    )(place, in_hbm(grid_input), in_hbm(w_hidden), b_hidden.reshape(1, width), w_out_t)
+    )(place, in_hbm(grid_input), in_hbm(w_hidden), in_hbm(b_hidden.reshape(1, width)), in_hbm(w_out_t))
+    done = {turns[0]: one}
+    for turn in turns[1:]:
+        b, _ = lax.optimization_barrier((b, one[2]))
+        one = pl.pallas_call(
+            functools.partial(later_kernel, turn, pieces),
+            in_specs=[ON_SMEM] + [ON_VMEM] * 4,
+            out_specs=[ON_VMEM] * 3,
+            out_shape=results,
+            compiler_params=params(),
+            cost_estimate=estimate,
+            name="forward",
+        )(place, x, w, b, w_out)
+        done[turn] = one
+    act, slope, sends = zip(*(done[s] for s in range(pieces)))
+    return x, w, w_out, list(act), list(slope), list(sends)
+
+
+def far_first(pieces):
+    return sorted(range(pieces), key=lambda s: (s == 0, -min(s, pieces - s), s))
 
 
 def score_kernel(pieces, place, target_ref, bias_ref, weight_ref, *refs):
@@ -125,7 +164,7 @@
         own = []
         for s in range(pieces):
             base = given[s][0, rows, :].astype(F32)
-            own += [base + given[s][1 + m, rows, :].astype(F32) for m in range(per)]
+            own += [base + given[s][m, rows, :].astype(F32) for m in range(1, extra)]
         aim = target_ref[rows, pl.ds(start, length)] - bias[rows, :1]
         weight = weights_of[rows, :1]
         spread = [None] * members
@@ -199,23 +238,25 @@
     )(place, block_index, interp_weight, w_hidden)
 
 
-def backward_kernel(first, pieces, place, wout_ref, slope_ref, tiles_ref, *refs):
-    given = refs[:pieces]
-    dpred_ref, dpre_ref, below_ref, own_ref, above_ref = refs[pieces:]
+def backward_kernel(first, pieces, place, wout_ref, tiles_ref, *refs):
+    given, slopes = refs[:pieces], refs[pieces : 2 * pieces]
+    dpred_ref, dpre_ref, below_ref, own_ref, above_ref = refs[2 * pieces :]
     length = given[0].shape[2]
     members, nodes, width = own_ref.shape
     step = 512
     for m in range(members):
         for s in range(pieces):
-            at = lax.rem(place[0] + s, pieces) * length
-            rows = pl.ds(pl.multiple_of(at, length), length)
+            rows = slice(s * length, (s + 1) * length)
             dpred_ref[m, rows, :] = given[s][m].astype(F32).T.astype(BF16)
         for lo in range(0, width, step):
             cols = slice(lo, lo + step)
             dact = jnp.dot(dpred_ref[m], wout_ref[:, cols], preferred_element_type=F32)
-            dpre = (dact * slope_ref[first + m, :, cols].astype(F32)).astype(BF16)
-            dpre_ref[m, :, cols] = dpre
-            terms = jnp.dot(tiles_ref[...], dpre, preferred_element_type=F32)
+            for s in range(pieces):
+                slope = slopes[s][first + m, :, cols].astype(F32)
+                dpre = (dact[s * length : (s + 1) * length] * slope).astype(BF16)
+                at = lax.rem(place[0] + s, pieces) * length
+                dpre_ref[m, pl.ds(pl.multiple_of(at, length), length), cols] = dpre
+            terms = jnp.dot(tiles_ref[...], dpre_ref[m, :, cols], preferred_element_type=F32)
             below_ref[m, :, cols] = terms[:nodes].astype(BF16)
             own_ref[m, :, cols] = terms[nodes : 2 * nodes].astype(BF16)
             above_ref[m, :, cols] = terms[2 * nodes :].astype(BF16)
@@ -223,12 +264,13 @@
 
 def backward(first, members, given, w_out_t, slope, tiles, place):
     pieces = len(given)
-    _, cells, width = slope.shape
+    _, length, width = slope[0].shape
+    cells = length * pieces
     channels = w_out_t.shape[0]
     nodes = tiles.shape[0] // 3
     return pl.pallas_call(
         functools.partial(backward_kernel, first, pieces),
-        in_specs=[ON_SMEM] + [ON_VMEM] * (3 + pieces),
+        in_specs=[ON_SMEM] + [ON_VMEM] * (2 + pieces + len(slope)),
         out_specs=[ON_VMEM] * 5,
         out_shape=[
             pltpu.VMEM((members, cells, channels), BF16),
@@ -240,15 +282,19 @@
         compiler_params=params(),
         cost_estimate=cost(2 * members * cells * width * (256 + 3 * nodes), 5 << 20),
         name="backward",
-    )(place, w_out_t, slope, tiles, *given)
-
-
-def weights_kernel(turns, groups, cores, place, x_ref, act_ref, *refs):
-    parts = (len(refs) - cores) // 2
-    dpre = [(ref, m) for ref in refs[:parts] for m in range(ref.shape[0])]
-    dpred = [(ref, m) for ref in refs[parts : 2 * parts] for m in range(ref.shape[0])]
-    out = refs[2 * parts :]
-    width = dpre[0][0].shape[2]
+    )(place, w_out_t, tiles, *given, *slope)
+
+
+def weights_kernel(turns, groups, cores, counts, place, *refs):
+    split_at, lists = 0, []
+    for count in counts:
+        some = refs[split_at : split_at + count]
+        lists.append([ref.at[m] for ref in some for m in range(ref.shape[0])])
+        split_at += count
+    x, act, dpre, dpred = lists
+    act = [act[m :: len(x)] for m in range(len(x))]
+    out = refs[split_at:]
+    width = dpre[0].shape[1]
     step = width // groups
     count, rows, _ = out[0].shape
     count //= len(turns)
@@ -258,12 +304,16 @@
         at = lax.rem(place[0] + turn, groups) * step
         cols = pl.ds(pl.multiple_of(at, step), step)
         for values, others, wide in (
-            (x_ref, dpre, slice(0, width)),
-            (act_ref, dpred, slice(width, None)),
+            (x, dpre, slice(0, width)),
+            (act, dpred, slice(width, None)),
         ):
             total = None
-            for m, (ref, k) in enumerate(others):
-                part = lax.dot_general(values[m, :, cols], ref[k], across, preferred_element_type=F32)
+            for value, other in zip(values, others):
+                if isinstance(value, list):
+                    value = jnp.concatenate([piece[:, cols] for piece in value], axis=0)
+                else:
+                    value = value[:, cols]
+                part = lax.dot_general(value, other[...], across, preferred_element_type=F32)
                 total = part if total is None else total + part
             total = total.astype(BF16).reshape(count, cores, rows, total.shape[1])
             for b in range(count):
@@ -277,20 +327,20 @@
 
 
 def weights(x, act, dpre, dpred, place, blocks, groups, cores, turns):
-    width = x.shape[2]
+    width = x[0].shape[2]
     columns = width + dpred[0].shape[2]
     rows = width // blocks
     count = len(turns) * blocks // (groups * cores)
-    parts = len(dpre)
-    return pl.pallas_call(
-        functools.partial(weights_kernel, turns, groups, cores),
-        in_specs=[ON_SMEM] + [ON_VMEM] * (2 + 2 * parts),
+    counts = [len(x), len(act), len(dpre), len(dpred)]
+    return pl.pallas_call(
+        functools.partial(weights_kernel, turns, groups, cores, counts),
+        in_specs=[ON_SMEM] + [ON_VMEM] * sum(counts),
         out_specs=[ON_VMEM] * cores,
         out_shape=[pltpu.VMEM((count, rows, columns), BF16)] * cores,
         compiler_params=params(),
         cost_estimate=cost(1000, 1000),
         name="weights",
-    )(place, x, act, *dpre, *dpred)
+    )(place, *x, *act, *dpre, *dpred)
 
 
 def add_kernel(kept_ref, came_ref, *out):
@@ -366,16 +416,16 @@
     )(*given)
 
 
-def weight_gradients(x, act, dpre, dpred, place, after):
+def weight_gradients(x, act, dpre, dpred, place, after, done):
     groups, regions = lax.axis_size("member"), lax.axis_size("region")
-    blocks, width = groups * regions, x.shape[2]
+    blocks, width = groups * regions, x[0].shape[2]
     if regions % 2 or width % (blocks * 16):
         turns = list(range(groups))
         (part,) = weights(x, act, dpre, dpred, place * 0, blocks, groups, 1, turns)
         part = part.reshape(width, -1)
         part = lax.psum_scatter(part, "member", scatter_dimension=0, tiled=True)
         part = lax.psum_scatter(part, "region", scatter_dimension=0, tiled=True).astype(F32)
-        return part[:, :width], part[:, width:]
+        return part[:, :width], part[:, width:], done
     given = [None] * groups
     for turns in turn_sets(groups):
         away, kept = weights(x, act, dpre, dpred, place, blocks, groups, 2, turns)
@@ -385,13 +435,14 @@
         came = lax.ppermute(away, "region", [(i, i ^ 1) for i in range(regions)])
         for s, part in zip(turns, add(kept, came, len(turns))):
             given[s] = shifted(part, "member", s) if s else part
+    given, done = lax.optimization_barrier((given, done))
     chips = regions // 2
     parts = split(given, place, 1, 2, chips)
     given = [parts[0]]
     for s in range(1, chips):
         route = [(i, (i + 2 * s) % regions) for i in range(regions)]
         given.append(lax.ppermute(parts[s], "region", route))
-    return last_total(given, width)
+    return *last_total(given, width), done
 
 
 def finish_kernel(first, own_ref, up_ref, down_ref, w_ref, *refs):
@@ -430,10 +481,13 @@
     per_region = MBLK_REG
     place = jnp.stack([lax.axis_index("member"), lax.axis_index("region")]).astype(jnp.int32)
     w_out_t = w_out.T
-    x, w_hidden, act, slope, *sends = forward(grid_input, w_hidden, b_hidden, w_out_t, place, groups)
+    x, w_hidden, w_out_t, act, slope, sends = forward(
+        grid_input, w_hidden, b_hidden, w_out_t, place, groups
+    )
     tiles, w_hidden_t = tiles_matrix(
         interp_weight, block_index, w_hidden, place, per_region, regions
     )
+    x = [x]
     given = [sends[0]] + [shifted(sends[s], "member", s) for s in range(1, groups)]
     parts = shares(members)
     adjoint = score(given, target, b_out, channel_weight, place, parts)
@@ -442,6 +496,8 @@
     for i, per in enumerate(parts):
         mine = adjoint[i * groups : (i + 1) * groups]
         back = [mine[0]] + [shifted(mine[s], "member", -s) for s in range(1, groups)]
+        if dpred:
+            back, _ = lax.optimization_barrier((back, dpred[-1]))
         one = backward(first, per, back, w_out_t, slope, tiles, place)
         first += per
         dpred.append(one[0])
@@ -449,10 +505,10 @@
         own.append(one[3])
         down.append(shifted(one[2], "region", -1))
         up.append(shifted(one[4], "region", 1))
-    hidden, output = weight_gradients(x, act, dpre, dpred, place, (up[0], down[0]))
-    out = None
-    first = 0
-    for i, per in enumerate(parts):
+    out = finish(0, members, own[0], up[0], down[0], w_hidden_t, None)
+    hidden, output, out = weight_gradients(x, act, dpre, dpred, place, (up[0], down[0]), out)
+    first = parts[0]
+    for i, per in list(enumerate(parts))[1:]:
         out = finish(first, members, own[i], up[i], down[i], w_hidden_t, out)
         first += per
     return hidden, output, out

time: 99.4 us -> 92.3 us (0.929)
  waiting for transfers between devices: 34.1 us -> 24.2 us
  Pallas kernels: 34.2 us -> 36.6 us
  starting transfers between devices: 28.3 us -> 30.2 us
  local copies, waits for them, and re-layouts: 1.64 us -> 0.03 us
    ppermute x16, waiting for transfers between devices: 34 us -> 24.2 us  [shifted(): lax.ppermute(block, axis, [((i - distance) % count, i) for i in range(cou...]
    ppermute x16, starting transfers between devices: 22.6 us -> 24.9 us  [shifted(): lax.ppermute(block, axis, [((i - distance) % count, i) for i in range(cou...]
    unnamed x16 -> x10, local copies, waits for them, and re-layouts: 1.64 us -> 0.03 us
    pallas_call x3 -> x6, Pallas kernels: 17.6 us -> 19.2 us  [the longest x3 7.59 us: forward(): pl.pallas_call(functools.partial(later_kernel, turn, pieces), in_specs=[O...]
  transfers between devices with their start and end apart: 21 -> 21, of which waited for: 7 -> 4; matrix products, arithmetic and copies ran while one was open for 0% -> 0% of each run, Pallas kernels for 21% -> 32%
where the time goes in v3:
time: 92.3 us; the launch traced here: 92.1 us
  Pallas kernels  36.6 us (40%)
  starting transfers between devices  30.2 us (33%)
  waiting for transfers between devices  24.2 us (26%)
    ppermute x16, starting transfers between devices, shifted(): lax.ppermute(block, axis, [((i - distance) % count, i) for i in range(cou...  24.9 us
    ppermute x16, waiting for transfers between devices, shifted(): lax.ppermute(block, axis, [((i - distance) % count, i) for i in range(cou...  24.2 us
    pallas_call x3, Pallas kernels, forward(): pl.pallas_call(functools.partial(later_kernel, turn, pieces), in_specs=[O...  7.59 us
    pallas_call x2, Pallas kernels, backward(): pl.pallas_call(functools.partial(backward_kernel, first, pieces), in_spec...  7.31 us
    pallas_call x2, Pallas kernels, weights(): pl.pallas_call(functools.partial(weights_kernel, turns, groups, cores, co...  7.08 us
    pallas_call x2, Pallas kernels, finish(): pl.pallas_call(functools.partial(finish_kernel, first), in_specs=[ON_VMEM...  4.59 us
    pallas_call x1, Pallas kernels, forward(): pl.pallas_call(functools.partial(first_kernel, turns[0], pieces), in_spec...  4.53 us
    ppermute x3, starting transfers between devices, weight_gradients(): given.append(lax.ppermute(parts[s], 'region', route))  4.5 us
  transfers between devices with their start and end apart: 21, of which 4 were waited for; matrix products, arithmetic and copies ran while one was open for 0% of the time, Pallas kernels for 32%

profile of v3, /device:TPU:8, one launch (start us, length us, event | category | flops | bytes accessed | tf_op | source)
XLA Modules:
  0.0 92.1 jit_solution(4692905480460130390)
XLA Ops:
  0.6 0.1 pad_add_fusion.place
  0.7 4.5 %forward.4 = (bf16[4,512,1024]{2,1,0:T(8,128)(2,1)S(1)}, bf16[1024,1024]{1,0:T(8,128)(2,1)S(1)}, f32[1,1024]{1,0:T(1,128)S(1)}, bf16[96,1024]{1,0:T(8,128)(2,1)S...) custom-call(s32[2]{0:T(128)S(1)} %pad_add_fusion.place, ...), custom_call_target="tpu_custom_call" | custom-call | flops 1000 | bytes 1000 | tf_op jit(solution)/shard_map/forward/pallas_call | solution.py:115
  5.2 2.6 %collective-permute-start.1 = (bf16[5,96,128]{2,1,0:T(8,128)(2,1)S(1)}, bf16[5,96,128]{2,1,0:T(8,128)(2,1)S(1)}, u32[]{:S(2)}, u32[]{:S(2)}) collective-permute-start(bf16[5,96,128]{2,1,0:T(8,128)(2,1)S(1)} %get-tuple-element.69), channel_id=1, source_target_pairs={{16,0},{24,8},{0,16},{8,24},{17,1},{25,9},{1,17},{9,25},{18,2},{26... | collective-permute-start | bytes 368648 | tf_op jit(solution)/shard_map/ppermute | solution.py:24
  7.9 2.5 %forward.5 = (bf16[4,128,1024]{2,1,0:T(8,128)(2,1)S(1)}, bf16[4,128,1024]{2,1,0:T(8,128)(2,1)S(1)}, bf16[5,96,128]{2,1,0:T(8,128)(2,1)S(1)}) custom-call(s32[2]{0:T(128)S(1)} %pad_add_fusion.place, bf16[4,512,1024]{2,1,0:T(8,128)(2,1)S(1)} %get-tuple-element.66.x_ref.refs_0_, bf16[1024,1024]{1,0:T(8,128)(2,1)S(1)} %get-tuple-element.67.w_ref, ...), custom_call_target="tpu_custom_call" | custom-call | flops 1000 | bytes 1000 | tf_op jit(solution)/shard_map/forward/pallas_call | solution.py:134
  10.4 0.1 collective-permute-start
  10.5 2.5 %forward.6 = (bf16[4,128,1024]{2,1,0:T(8,128)(2,1)S(1)}, bf16[4,128,1024]{2,1,0:T(8,128)(2,1)S(1)}, bf16[5,96,128]{2,1,0:T(8,128)(2,1)S(1)}) custom-call(s32[2]{0:T(128)S(1)} %pad_add_fusion.place, bf16[4,512,1024]{2,1,0:T(8,128)(2,1)S(1)} %get-tuple-element.66.x_ref.refs_0_, bf16[1024,1024]{1,0:T(8,128)(2,1)S(1)} %get-tuple-element.67.w_ref, ...), custom_call_target="tpu_custom_call" | custom-call | flops 1000 | bytes 1000 | tf_op jit(solution)/shard_map/forward/pallas_call | solution.py:134
  13.0 0.0 copy-start.1
  13.0 0.0 copy-start.3
  13.1 0.0 copy-start.4
  13.1 0.0 copy-start
  13.1 0.0 copy-start.2
  13.1 2.1 %collective-permute-start.2 = (bf16[5,96,128]{2,1,0:T(8,128)(2,1)S(1)}, bf16[5,96,128]{2,1,0:T(8,128)(2,1)S(1)}, u32[]{:S(2)}, u32[]{:S(2)}) collective-permute-start(bf16[5,96,128]{2,1,0:T(8,128)(2,1)S(1)} %get-tuple-element.74), channel_id=1, source_target_pairs={{8,0},{16,8},{24,16},{0,24},{9,1},{17,9},{25,17},{1,25},{10,2},{18... | collective-permute-start | bytes 368648 | tf_op jit(solution)/shard_map/ppermute | solution.py:24
  15.2 2.5 %forward.7 = (bf16[4,128,1024]{2,1,0:T(8,128)(2,1)S(1)}, bf16[4,128,1024]{2,1,0:T(8,128)(2,1)S(1)}, bf16[5,96,128]{2,1,0:T(8,128)(2,1)S(1)}) custom-call(s32[2]{0:T(128)S(1)} %pad_add_fusion.place, bf16[4,512,1024]{2,1,0:T(8,128)(2,1)S(1)} %get-tuple-element.66.x_ref.refs_0_, bf16[1024,1024]{1,0:T(8,128)(2,1)S(1)} %get-tuple-element.67.w_ref, ...), custom_call_target="tpu_custom_call" | custom-call | flops 1000 | bytes 1000 | tf_op jit(solution)/shard_map/forward/pallas_call | solution.py:134
  17.7 0.0 collective-permute-done.1.refs_2_
  17.7 1.1 %collective-permute-done.2.refs_3_ = bf16[5,96,128]{2,1,0:T(8,128)(2,1)S(1)} collective-permute-done((bf16[5,96,128]{2,1,0:T(8,128)(2,1)S(1)}, bf16[5,96,128]{2,1,0:T(8,128)(2,1)S(1)}, u32[]{:S(2)}, u32[]{:S(2)}) %collective-permute-start.2) | collective-permute-done | bytes 122912 | tf_op jit(solution)/shard_map/ppermute | solution.py:24
  18.8 2.4 %score.1 = (bf16[1,96,128]{2,1,0:T(8,128)(2,1)S(1)}, bf16[1,96,128]{2,1,0:T(8,128)(2,1)S(1)}, bf16[1,96,128]{2,1,0:T(8,128)(2,1)S(1)}, bf16[1,96,128]{2,1,0:T(8,...) custom-call(s32[2]{0:T(128)S(1)} %pad_add_fusion.place, ...), custom_call_target="tpu_custom_call" | custom-call | flops 40000000 | bytes 1048576 | tf_op jit(solution)/shard_map/score/pallas_call | solution.py:194
  21.2 1.5 %collective-permute-start.3 = (bf16[1,96,128]{2,1,0:T(8,128)(2,1)S(1)}, bf16[1,96,128]{2,1,0:T(8,128)(2,1)S(1)}, u32[]{:S(2)}, u32[]{:S(2)}) collective-permute-start(bf16[1,96,128]{2,1,0:T(8,128)(2,1)S(1)} %get-tuple-element.83), channel_id=1, source_target_pairs={{8,0},{16,8},{24,16},{0,24},{9,1},{17,9},{25,17},{1,25},{10,2},{18... | collective-permute-start | bytes 73736 | tf_op jit(solution)/shard_map/ppermute | solution.py:24
  22.7 2.4 %collective-permute-start.4 = (bf16[1,96,128]{2,1,0:T(8,128)(2,1)S(1)}, bf16[1,96,128]{2,1,0:T(8,128)(2,1)S(1)}, u32[]{:S(2)}, u32[]{:S(2)}) collective-permute-start(bf16[1,96,128]{2,1,0:T(8,128)(2,1)S(1)} %get-tuple-element.84), channel_id=1, source_target_pairs={{16,0},{24,8},{0,16},{8,24},{17,1},{25,9},{1,17},{9,25},{18,2},{26... | collective-permute-start | bytes 73736 | tf_op jit(solution)/shard_map/ppermute | solution.py:24
  25.2 2.8 %collective-permute-start.5 = (bf16[1,96,128]{2,1,0:T(8,128)(2,1)S(1)}, bf16[1,96,128]{2,1,0:T(8,128)(2,1)S(1)}, u32[]{:S(2)}, u32[]{:S(2)}) collective-permute-start(bf16[1,96,128]{2,1,0:T(8,128)(2,1)S(1)} %get-tuple-element.85), channel_id=1, source_target_pairs={{24,0},{0,8},{8,16},{16,24},{25,1},{1,9},{9,17},{17,25},{26,2},{2,... | collective-permute-start | bytes 73736 | tf_op jit(solution)/shard_map/ppermute | solution.py:24
  28.0 1.5 %tiles.1 = (bf16[768,512]{1,0:T(8,128)(2,1)S(1)}, bf16[1024,1024]{1,0:T(8,128)(2,1)S(1)}) custom-call(s32[2]{0:T(128)S(1)} %pad_add_fusion.place, s32[4,3]{1,0:T(4,128)S(1)} %copy-done.2, bf16[4,3,128,128]{3,2,1,0:T(8,128)(2,1)S(1)} %copy-done, bf16[1024,1024]{1,0:T(8,128)(2,1)S(1)} %get-tuple-element.67.w_ref), custom_call_target="tpu_custom_call" | custom-call | flops 4000000 | bytes 2097152 | tf_op jit(solution)/shard_map/tiles/pallas_call | solution.py:226
  29.5 0.1 collective-permute-start.6
  29.6 1.5 %collective-permute-start.7 = (bf16[3,96,128]{2,1,0:T(8,128)(2,1)S(1)}, bf16[3,96,128]{2,1,0:T(8,128)(2,1)S(1)}, u32[]{:S(2)}, u32[]{:S(2)}) collective-permute-start(bf16[3,96,128]{2,1,0:T(8,128)(2,1)S(1)} %get-tuple-element.93), channel_id=1, source_target_pairs={{16,0},{24,8},{0,16},{8,24},{17,1},{25,9},{1,17},{9,25},{18,2},{26... | collective-permute-start | bytes 221192 | tf_op jit(solution)/shard_map/ppermute | solution.py:24
  31.0 2.4 %collective-permute-start.8 = (bf16[3,96,128]{2,1,0:T(8,128)(2,1)S(1)}, bf16[3,96,128]{2,1,0:T(8,128)(2,1)S(1)}, u32[]{:S(2)}, u32[]{:S(2)}) collective-permute-start(bf16[3,96,128]{2,1,0:T(8,128)(2,1)S(1)} %get-tuple-element.94), channel_id=1, source_target_pairs={{24,0},{0,8},{8,16},{16,24},{25,1},{1,9},{9,17},{17,25},{26,2},{2,... | collective-permute-start | bytes 221192 | tf_op jit(solution)/shard_map/ppermute | solution.py:24
  33.4 2.2 %backward.2 = (bf16[1,512,96]{2,1,0:T(8,128)(2,1)S(1)}, bf16[1,512,1024]{2,1,0:T(8,128)(2,1)S(1)}, bf16[1,256,1024]{2,1,0:T(8,128)(2,1)S(1)}, bf16[1,256,1024]{2,1,0:T(8,128)(2,1)S(1)}, bf16[1,256,1024]{2,1,0:T(8,128)(2,1)S(1)}) custom-call(s32[2]{0:T(128)S(1)} %pad_add_fusion.place, bf16[96,1024]{1,0:T(8,128)(2,1)S(1)} %get-tuple-element.71.wout_ref, ...), custom_call_target="tpu_custom_call" | custom-call | flops 1073741824 | bytes 5242880 | tf_op jit(solution)/shard_map/backward/pallas_call | solution.py:271
  35.6 0.1 collective-permute-start.10
  35.7 2.6 %collective-permute-start.11 = (bf16[1,256,1024]{2,1,0:T(8,128)(2,1)S(1)}, bf16[1,256,1024]{2,1,0:T(8,128)(2,1)S(1)}, u32[]{:S(2)}, u32[]{:S(2)}) collective-permute-start(bf16[1,256,1024]{2,1,0:T(8,128)(2,1)S(1)} %get-tuple-element.107), channel_id=1, source_target_pairs={{1,0},{2,1},{3,2},{4,3},{5,4},{6,5},{7,6},{0,7},{9,8},{10,9},{11,1... | collective-permute-start | bytes 1572872 | tf_op jit(solution)/shard_map/ppermute | solution.py:24
  38.3 5.1 %backward.3 = (bf16[3,512,96]{2,1,0:T(8,128)(2,1)S(1)}, bf16[3,512,1024]{2,1,0:T(8,128)(2,1)S(1)}, bf16[3,256,1024]{2,1,0:T(8,128)(2,1)S(1)}, bf16[3,256,1024]{2,1,0:T(8,128)(2,1)S(1)}, bf16[3,256,1024]{2,1,0:T(8,128)(2,1)S(1)}) custom-call(s32[2]{0:T(128)S(1)} %pad_add_fusion.place, bf16[96,1024]{1,0:T(8,128)(2,1)S(1)} %get-tuple-element.71.wout_ref, ...), custom_call_target="tpu_custom_call" | custom-call | flops 3221225472 | bytes 5242880 | tf_op jit(solution)/shard_map/backward/pallas_call | solution.py:271
  43.4 0.1 collective-permute-start.19
  43.5 2.6 %collective-permute-start.20 = (bf16[3,256,1024]{2,1,0:T(8,128)(2,1)S(1)}, bf16[3,256,1024]{2,1,0:T(8,128)(2,1)S(1)}, u32[]{:S(2)}, u32[]{:S(2)}) collective-permute-start(bf16[3,256,1024]{2,1,0:T(8,128)(2,1)S(1)} %get-tuple-element.127), channel_id=1, source_target_pairs={{1,0},{2,1},{3,2},{4,3},{5,4},{6,5},{7,6},{0,7},{9,8},{10,9},{11,1... | collective-permute-start | bytes 4718600 | tf_op jit(solution)/shard_map/ppermute | solution.py:24
  46.1 4.9 %weights.3 = (bf16[12,32,1120]{2,1,0:T(8,128)(2,1)S(1)}, bf16[12,32,1120]{2,1,0:T(8,128)(2,1)S(1)}) custom-call(s32[2]{0:T(128)S(1)} %pad_add_fusion.place, bf16[4,512,1024]{2,1,0:T(8,128)(2,1)S(1)} %get-tuple-element.66.x_ref.refs_0_, bf16[4,128,1024]{2,1,0:T(8,128)(2,1)S(1)} %get-tuple-element.76.refs_1_, ...), custom_call_target="tpu_custom_call" | custom-call | flops 1000 | bytes 1000 | tf_op jit(solution)/shard_map/weights/pallas_call | solution.py:335
  51.1 0.7 collective-permute-start.12
  51.8 2.2 %weights.2 = (bf16[4,32,1120]{2,1,0:T(8,128)(2,1)S(1)}, bf16[4,32,1120]{2,1,0:T(8,128)(2,1)S(1)}) custom-call(s32[2]{0:T(128)S(1)} %pad_add_fusion.place, bf16[4,512,1024]{2,1,0:T(8,128)(2,1)S(1)} %get-tuple-element.66.x_ref.refs_0_, bf16[4,128,1024]{2,1,0:T(8,128)(2,1)S(1)} %get-tuple-element.76.refs_1_, ...), custom_call_target="tpu_custom_call" | custom-call | flops 1000 | bytes 1000 | tf_op jit(solution)/shard_map/weights/pallas_call | solution.py:335
  53.9 0.1 collective-permute-start.9
  54.0 0.2 add.5
  54.2 0.2 collective-permute-start.13
  54.5 2.8 %collective-permute-start.14 = (bf16[4,32,1120]{2,1,0:T(8,128)(2,1)S(1)}, bf16[4,32,1120]{2,1,0:T(8,128)(2,1)S(1)}, u32[]{:S(2)}, u32[]{:S(2)}) collective-permute-start(bf16[4,32,1120]{2,1,0:T(8,128)(2,1)S(1)} %get-tuple-element.111), channel_id=1, source_target_pairs={{16,0},{24,8},{0,16},{8,24},{17,1},{25,9},{1,17},{9,25},{18,2},{26... | collective-permute-start | bytes 860168 | tf_op jit(solution)/shard_map/ppermute | solution.py:24
  57.3 1.0 %collective-permute-start.15 = (bf16[4,32,1120]{2,1,0:T(8,128)(2,1)S(1)}, bf16[4,32,1120]{2,1,0:T(8,128)(2,1)S(1)}, u32[]{:S(2)}, u32[]{:S(2)}) collective-permute-start(bf16[4,32,1120]{2,1,0:T(8,128)(2,1)S(1)} %get-tuple-element.112), channel_id=1, source_target_pairs={{8,0},{16,8},{24,16},{0,24},{9,1},{17,9},{25,17},{1,25},{10,2},{18... | collective-permute-start | bytes 860168 | tf_op jit(solution)/shard_map/ppermute | solution.py:24
  58.3 0.1 add.4.refs_0_
  58.4 1.7 %finish.2.refs_0_ = f32[4,256,1024]{2,1,0:T(8,128)} custom-call(bf16[1,256,1024]{2,1,0:T(8,128)(2,1)S(1)} %get-tuple-element.113.own_ref, bf16[1,256,1024]{2,1,0:T(8,128)(2,1)S(1)} %collective-permute-done.10.up_ref, bf16[1,256,1024]{2,1,0:T(8,128)(2,1)S(1)} %collective-permute-done.11.down_ref, bf16[1024,1024]{1,0:T(8,128)(2,1)S(1)} %get-tuple-element.114.w_ref), custom_call_target="tpu_custom_call" | custom-call | flops 1000 | bytes 1000 | tf_op jit(solution)/shard_map/finish/pallas_call | solution.py:463
  60.1 4.0 %collective-permute-done.13.refs_1_ = bf16[4,32,1120]{2,1,0:T(8,128)(2,1)S(1)} collective-permute-done((bf16[4,32,1120]{2,1,0:T(8,128)(2,1)S(1)}, bf16[4,32,1120]{2,1,0:T(8,128)(2,1)S(1)}, u32[]{:S(2)}, u32[]{:S(2)}) %collective-permute-start.13) | collective-permute-done | bytes 286752 | tf_op jit(solution)/shard_map/ppermute | solution.py:24
  64.1 16.4 %collective-permute-done.14.refs_2_ = bf16[4,32,1120]{2,1,0:T(8,128)(2,1)S(1)} collective-permute-done((bf16[4,32,1120]{2,1,0:T(8,128)(2,1)S(1)}, bf16[4,32,1120]{2,1,0:T(8,128)(2,1)S(1)}, u32[]{:S(2)}, u32[]{:S(2)}) %collective-permute-start.14) | collective-permute-done | bytes 286752 | tf_op jit(solution)/shard_map/ppermute | solution.py:24
  80.4 2.8 %collective-permute-done.15.refs_3_ = bf16[4,32,1120]{2,1,0:T(8,128)(2,1)S(1)} collective-permute-done((bf16[4,32,1120]{2,1,0:T(8,128)(2,1)S(1)}, bf16[4,32,1120]{2,1,0:T(8,128)(2,1)S(1)}, u32[]{:S(2)}, u32[]{:S(2)}) %collective-permute-start.15) | collective-permute-done | bytes 286752 | tf_op jit(solution)/shard_map/ppermute | solution.py:24
  83.2 0.7 split.1
  83.9 1.9 %collective-permute-start.16 = (bf16[1,32,1120]{2,1,0:T(8,128)(2,1)S(1)}, bf16[1,32,1120]{2,1,0:T(8,128)(2,1)S(1)}, u32[]{:S(2)}, u32[]{:S(2)}) collective-permute-start(bf16[1,32,1120]{2,1,0:T(8,128)(2,1)S(1)} %get-tuple-element.120), channel_id=1, source_target_pairs={{0,2},{1,3},{2,4},{3,5},{4,6},{5,7},{6,0},{7,1},{8,10},{9,11},{10,... | collective-permute-start | bytes 215048 | tf_op jit(solution)/shard_map/ppermute | solution.py:444
  85.9 0.5 collective-permute-start.17
  86.4 2.0 %collective-permute-start.18 = (bf16[1,32,1120]{2,1,0:T(8,128)(2,1)S(1)}, bf16[1,32,1120]{2,1,0:T(8,128)(2,1)S(1)}, u32[]{:S(2)}, u32[]{:S(2)}) collective-permute-start(bf16[1,32,1120]{2,1,0:T(8,128)(2,1)S(1)} %get-tuple-element.122), channel_id=1, source_target_pairs={{0,6},{1,7},{2,0},{3,1},{4,2},{5,3},{6,4},{7,5},{8,14},{9,15},{10,... | collective-permute-start | bytes 215048 | tf_op jit(solution)/shard_map/ppermute | solution.py:444
  88.4 2.9 %finish.3 = f32[4,256,1024]{2,1,0:T(8,128)} custom-call(bf16[3,256,1024]{2,1,0:T(8,128)(2,1)S(1)} %get-tuple-element.125.own_ref, bf16[3,256,1024]{2,1,0:T(8,128)(2,1)S(1)} %collective-permute-done.19.up_ref, bf16[3,256,1024]{2,1,0:T(8,128)(2,1)S(1)} %collective-permute-done.20.down_ref, ...), custom_call_target="tpu_custom_call", output_to_operand_aliasing={{}: (4, {})} | custom-call | flops 1000 | bytes 1000 | tf_op jit(solution)/shard_map/finish/pallas_call | solution.py:463
  91.4 0.7 total.1
  (21 shorter events, 0.1 us)
Async XLA Ops:
  5.2 12.5 %collective-permute-start.1 = (bf16[5,96,128]{2,1,0:T(8,128)(2,1)S(1)}, bf16[5,96,128]{2,1,0:T(8,128)(2,1)S(1)}, u32[]{:S(2)}, u32[]{:S(2)}) collective-permute-start(bf16[5,96,128]{2,1,0:T(8,128)(2,1)S(1)} %get-tuple-element.69), channel_id=1, source_target_pairs={{16,0},{24,8},{0,16},{8,24},{17,1},{25,9},{1,17},{9,25},{18,2},{26... | collective-permute-start | bytes 368648 | tf_op jit(solution)/shard_map/ppermute | solution.py:24
  10.4 7.3 %collective-permute-start = (bf16[5,96,128]{2,1,0:T(8,128)(2,1)S(1)}, bf16[5,96,128]{2,1,0:T(8,128)(2,1)S(1)}, u32[]{:S(2)}, u32[]{:S(2)}) collective-permute-start(bf16[5,96,128]{2,1,0:T(8,128)(2,1)S(1)} %get-tuple-element.72), channel_id=1, source_target_pairs={{24,0},{0,8},{8,16},{16,24},{25,1},{1,9},{9,17},{17,25},{26,2},{2,... | collective-permute-start | bytes 368648 | tf_op jit(solution)/shard_map/ppermute | solution.py:24
  13.0 5.8 %copy-start.1 = (f32[96,512]{1,0:T(8,128)S(1)}, f32[96,512]{1,0:T(8,128)}, u32[]{:S(2)}) copy-start(f32[96,512]{1,0:T(8,128)} %target_ref.1) | copy-start | bytes 589828
  13.0 5.7 %copy-start.3 = (f32[96]{0:T(128)S(1)}, f32[96]{0:T(128)}, u32[]{:S(2)}) copy-start(f32[96]{0:T(128)} %param.13) | copy-start | bytes 1156
  13.1 5.7 %copy-start.4 = (f32[96]{0:T(128)S(1)}, f32[96]{0:T(128)}, u32[]{:S(2)}) copy-start(f32[96]{0:T(128)} %param.15) | copy-start | bytes 1156
  13.1 14.9 %copy-start = (bf16[4,3,128,128]{3,2,1,0:T(8,128)(2,1)S(1)}, bf16[4,3,128,128]{3,2,1,0:T(8,128)(2,1)}, u32[]{:S(2)}) copy-start(bf16[4,3,128,128]{3,2,1,0:T(8,128)(2,1)} %tile_ref.1) | copy-start | bytes 1179652
  13.1 14.9 %copy-start.2 = (s32[4,3]{1,0:T(4,128)S(1)}, s32[4,3]{1,0:T(4,128)}, u32[]{:S(2)}) copy-start(s32[4,3]{1,0:T(4,128)} %index_ref.1) | copy-start | bytes 148
  13.1 5.7 %collective-permute-start.2 = (bf16[5,96,128]{2,1,0:T(8,128)(2,1)S(1)}, bf16[5,96,128]{2,1,0:T(8,128)(2,1)S(1)}, u32[]{:S(2)}, u32[]{:S(2)}) collective-permute-start(bf16[5,96,128]{2,1,0:T(8,128)(2,1)S(1)} %get-tuple-element.74), channel_id=1, source_target_pairs={{8,0},{16,8},{24,16},{0,24},{9,1},{17,9},{25,17},{1,25},{10,2},{18... | collective-permute-start | bytes 368648 | tf_op jit(solution)/shard_map/ppermute | solution.py:24
  21.2 9.9 %collective-permute-start.3 = (bf16[1,96,128]{2,1,0:T(8,128)(2,1)S(1)}, bf16[1,96,128]{2,1,0:T(8,128)(2,1)S(1)}, u32[]{:S(2)}, u32[]{:S(2)}) collective-permute-start(bf16[1,96,128]{2,1,0:T(8,128)(2,1)S(1)} %get-tuple-element.83), channel_id=1, source_target_pairs={{8,0},{16,8},{24,16},{0,24},{9,1},{17,9},{25,17},{1,25},{10,2},{18... | collective-permute-start | bytes 73736 | tf_op jit(solution)/shard_map/ppermute | solution.py:24
  22.7 10.7 %collective-permute-start.4 = (bf16[1,96,128]{2,1,0:T(8,128)(2,1)S(1)}, bf16[1,96,128]{2,1,0:T(8,128)(2,1)S(1)}, u32[]{:S(2)}, u32[]{:S(2)}) collective-permute-start(bf16[1,96,128]{2,1,0:T(8,128)(2,1)S(1)} %get-tuple-element.84), channel_id=1, source_target_pairs={{16,0},{24,8},{0,16},{8,24},{17,1},{25,9},{1,17},{9,25},{18,2},{26... | collective-permute-start | bytes 73736 | tf_op jit(solution)/shard_map/ppermute | solution.py:24
  25.2 8.2 %collective-permute-start.5 = (bf16[1,96,128]{2,1,0:T(8,128)(2,1)S(1)}, bf16[1,96,128]{2,1,0:T(8,128)(2,1)S(1)}, u32[]{:S(2)}, u32[]{:S(2)}) collective-permute-start(bf16[1,96,128]{2,1,0:T(8,128)(2,1)S(1)} %get-tuple-element.85), channel_id=1, source_target_pairs={{24,0},{0,8},{8,16},{16,24},{25,1},{1,9},{9,17},{17,25},{26,2},{2,... | collective-permute-start | bytes 73736 | tf_op jit(solution)/shard_map/ppermute | solution.py:24
  29.5 8.8 %collective-permute-start.6 = (bf16[3,96,128]{2,1,0:T(8,128)(2,1)S(1)}, bf16[3,96,128]{2,1,0:T(8,128)(2,1)S(1)}, u32[]{:S(2)}, u32[]{:S(2)}) collective-permute-start(bf16[3,96,128]{2,1,0:T(8,128)(2,1)S(1)} %get-tuple-element.92), channel_id=1, source_target_pairs={{8,0},{16,8},{24,16},{0,24},{9,1},{17,9},{25,17},{1,25},{10,2},{18... | collective-permute-start | bytes 221192 | tf_op jit(solution)/shard_map/ppermute | solution.py:24
  29.6 8.7 %collective-permute-start.7 = (bf16[3,96,128]{2,1,0:T(8,128)(2,1)S(1)}, bf16[3,96,128]{2,1,0:T(8,128)(2,1)S(1)}, u32[]{:S(2)}, u32[]{:S(2)}) collective-permute-start(bf16[3,96,128]{2,1,0:T(8,128)(2,1)S(1)} %get-tuple-element.93), channel_id=1, source_target_pairs={{16,0},{24,8},{0,16},{8,24},{17,1},{25,9},{1,17},{9,25},{18,2},{26... | collective-permute-start | bytes 221192 | tf_op jit(solution)/shard_map/ppermute | solution.py:24
  31.0 7.3 %collective-permute-start.8 = (bf16[3,96,128]{2,1,0:T(8,128)(2,1)S(1)}, bf16[3,96,128]{2,1,0:T(8,128)(2,1)S(1)}, u32[]{:S(2)}, u32[]{:S(2)}) collective-permute-start(bf16[3,96,128]{2,1,0:T(8,128)(2,1)S(1)} %get-tuple-element.94), channel_id=1, source_target_pairs={{24,0},{0,8},{8,16},{16,24},{25,1},{1,9},{9,17},{17,25},{26,2},{2,... | collective-permute-start | bytes 221192 | tf_op jit(solution)/shard_map/ppermute | solution.py:24
  35.6 15.4 %collective-permute-start.10 = (bf16[1,256,1024]{2,1,0:T(8,128)(2,1)S(1)}, bf16[1,256,1024]{2,1,0:T(8,128)(2,1)S(1)}, u32[]{:S(2)}, u32[]{:S(2)}) collective-permute-start(bf16[1,256,1024]{2,1,0:T(8,128)(2,1)S(1)} %get-tuple-element.106), channel_id=1, source_target_pairs={{7,0},{0,1},{1,2},{2,3},{3,4},{4,5},{5,6},{6,7},{15,8},{8,9},{9,10... | collective-permute-start | bytes 1572872 | tf_op jit(solution)/shard_map/ppermute | solution.py:24
  35.7 15.4 %collective-permute-start.11 = (bf16[1,256,1024]{2,1,0:T(8,128)(2,1)S(1)}, bf16[1,256,1024]{2,1,0:T(8,128)(2,1)S(1)}, u32[]{:S(2)}, u32[]{:S(2)}) collective-permute-start(bf16[1,256,1024]{2,1,0:T(8,128)(2,1)S(1)} %get-tuple-element.107), channel_id=1, source_target_pairs={{1,0},{2,1},{3,2},{4,3},{5,4},{6,5},{7,6},{0,7},{9,8},{10,9},{11,1... | collective-permute-start | bytes 1572872 | tf_op jit(solution)/shard_map/ppermute | solution.py:24
  43.4 45.0 %collective-permute-start.19 = (bf16[3,256,1024]{2,1,0:T(8,128)(2,1)S(1)}, bf16[3,256,1024]{2,1,0:T(8,128)(2,1)S(1)}, u32[]{:S(2)}, u32[]{:S(2)}) collective-permute-start(bf16[3,256,1024]{2,1,0:T(8,128)(2,1)S(1)} %get-tuple-element.126), channel_id=1, source_target_pairs={{7,0},{0,1},{1,2},{2,3},{3,4},{4,5},{5,6},{6,7},{15,8},{8,9},{9,10... | collective-permute-start | bytes 4718600 | tf_op jit(solution)/shard_map/ppermute | solution.py:24
  43.5 45.0 %collective-permute-start.20 = (bf16[3,256,1024]{2,1,0:T(8,128)(2,1)S(1)}, bf16[3,256,1024]{2,1,0:T(8,128)(2,1)S(1)}, u32[]{:S(2)}, u32[]{:S(2)}) collective-permute-start(bf16[3,256,1024]{2,1,0:T(8,128)(2,1)S(1)} %get-tuple-element.127), channel_id=1, source_target_pairs={{1,0},{2,1},{3,2},{4,3},{5,4},{6,5},{7,6},{0,7},{9,8},{10,9},{11,1... | collective-permute-start | bytes 4718600 | tf_op jit(solution)/shard_map/ppermute | solution.py:24
  51.1 2.9 %collective-permute-start.12 = (bf16[12,32,1120]{2,1,0:T(8,128)(2,1)S(1)}, bf16[12,32,1120]{2,1,0:T(8,128)(2,1)S(1)}, u32[]{:S(2)}, u32[]{:S(2)}) collective-permute-start(bf16[12,32,1120]{2,1,0:T(8,128)(2,1)S(1)} %get-tuple-element.109), channel_id=1, source_target_pairs={{0,1},{1,0},{2,3},{3,2},{4,5},{5,4},{6,7},{7,6},{8,9},{9,8},{10,11... | collective-permute-start | bytes 2580488 | tf_op jit(solution)/shard_map/ppermute | solution.py:435
  53.9 3.4 %collective-permute-start.9 = (bf16[4,32,1120]{2,1,0:T(8,128)(2,1)S(1)}, bf16[4,32,1120]{2,1,0:T(8,128)(2,1)S(1)}, u32[]{:S(2)}, u32[]{:S(2)}) collective-permute-start(bf16[4,32,1120]{2,1,0:T(8,128)(2,1)S(1)} %get-tuple-element.103), channel_id=1, source_target_pairs={{0,1},{1,0},{2,3},{3,2},{4,5},{5,4},{6,7},{7,6},{8,9},{9,8},{10,11... | collective-permute-start | bytes 860168 | tf_op jit(solution)/shard_map/ppermute | solution.py:435
  54.2 9.9 %collective-permute-start.13 = (bf16[4,32,1120]{2,1,0:T(8,128)(2,1)S(1)}, bf16[4,32,1120]{2,1,0:T(8,128)(2,1)S(1)}, u32[]{:S(2)}, u32[]{:S(2)}) collective-permute-start(bf16[4,32,1120]{2,1,0:T(8,128)(2,1)S(1)} %get-tuple-element.110), channel_id=1, source_target_pairs={{24,0},{0,8},{8,16},{16,24},{25,1},{1,9},{9,17},{17,25},{26,2},{2,... | collective-permute-start | bytes 860168 | tf_op jit(solution)/shard_map/ppermute | solution.py:24
  54.5 26.0 %collective-permute-start.14 = (bf16[4,32,1120]{2,1,0:T(8,128)(2,1)S(1)}, bf16[4,32,1120]{2,1,0:T(8,128)(2,1)S(1)}, u32[]{:S(2)}, u32[]{:S(2)}) collective-permute-start(bf16[4,32,1120]{2,1,0:T(8,128)(2,1)S(1)} %get-tuple-element.111), channel_id=1, source_target_pairs={{16,0},{24,8},{0,16},{8,24},{17,1},{25,9},{1,17},{9,25},{18,2},{26... | collective-permute-start | bytes 860168 | tf_op jit(solution)/shard_map/ppermute | solution.py:24
  57.3 25.9 %collective-permute-start.15 = (bf16[4,32,1120]{2,1,0:T(8,128)(2,1)S(1)}, bf16[4,32,1120]{2,1,0:T(8,128)(2,1)S(1)}, u32[]{:S(2)}, u32[]{:S(2)}) collective-permute-start(bf16[4,32,1120]{2,1,0:T(8,128)(2,1)S(1)} %get-tuple-element.112), channel_id=1, source_target_pairs={{8,0},{16,8},{24,16},{0,24},{9,1},{17,9},{25,17},{1,25},{10,2},{18... | collective-permute-start | bytes 860168 | tf_op jit(solution)/shard_map/ppermute | solution.py:24
  83.9 7.4 %collective-permute-start.16 = (bf16[1,32,1120]{2,1,0:T(8,128)(2,1)S(1)}, bf16[1,32,1120]{2,1,0:T(8,128)(2,1)S(1)}, u32[]{:S(2)}, u32[]{:S(2)}) collective-permute-start(bf16[1,32,1120]{2,1,0:T(8,128)(2,1)S(1)} %get-tuple-element.120), channel_id=1, source_target_pairs={{0,2},{1,3},{2,4},{3,5},{4,6},{5,7},{6,0},{7,1},{8,10},{9,11},{10,... | collective-permute-start | bytes 215048 | tf_op jit(solution)/shard_map/ppermute | solution.py:444
  85.9 5.5 %collective-permute-start.17 = (bf16[1,32,1120]{2,1,0:T(8,128)(2,1)S(1)}, bf16[1,32,1120]{2,1,0:T(8,128)(2,1)S(1)}, u32[]{:S(2)}, u32[]{:S(2)}) collective-permute-start(bf16[1,32,1120]{2,1,0:T(8,128)(2,1)S(1)} %get-tuple-element.121), channel_id=1, source_target_pairs={{0,4},{1,5},{2,6},{3,7},{4,0},{5,1},{6,2},{7,3},{8,12},{9,13},{10,... | collective-permute-start | bytes 215048 | tf_op jit(solution)/shard_map/ppermute | solution.py:444
  86.4 5.0 %collective-permute-start.18 = (bf16[1,32,1120]{2,1,0:T(8,128)(2,1)S(1)}, bf16[1,32,1120]{2,1,0:T(8,128)(2,1)S(1)}, u32[]{:S(2)}, u32[]{:S(2)}) collective-permute-start(bf16[1,32,1120]{2,1,0:T(8,128)(2,1)S(1)} %get-tuple-element.122), channel_id=1, source_target_pairs={{0,6},{1,7},{2,0},{3,1},{4,2},{5,3},{6,4},{7,5},{8,14},{9,15},{10,... | collective-permute-start | bytes 215048 | tf_op jit(solution)/shard_map/ppermute | solution.py:444

commit v4 on v3

--- a/solution.py
+++ b/solution.py
@@ -167,20 +167,26 @@
             own += [base + given[s][m, rows, :].astype(F32) for m in range(1, extra)]
         aim = target_ref[rows, pl.ds(start, length)] - bias[rows, :1]
         weight = weights_of[rows, :1]
-        spread = [None] * members
+        halves = []
+        for half in (slice(0, 8), slice(8, 16)):
+            mine = [value[half] for value in own]
+            spread = [None] * members
+            for j in range(members):
+                for k in range(j + 1, members):
+                    slope = smooth_slope(mine[j] - mine[k])
+                    spread[j] = slope if spread[j] is None else spread[j] + slope
+                    spread[k] = -slope if spread[k] is None else spread[k] - slope
+            skill = [smooth_slope(value - aim[half]) * (1.0 / members) for value in mine]
+            halves.append(
+                [weight[half] * (a - (2.0 * kappa) * b) for a, b in zip(skill, spread)]
+            )
         for j in range(members):
-            for k in range(j + 1, members):
-                slope = smooth_slope(own[j] - own[k])
-                spread[j] = slope if spread[j] is None else spread[j] + slope
-                spread[k] = -slope if spread[k] is None else spread[k] - slope
-        for j in range(members):
-            skill = smooth_slope(own[j] - aim) * (1.0 / members)
-            value = weight * (skill - (2.0 * kappa) * spread[j])
             part = j % per
             at = j // per
             while part >= out[at].shape[0]:
                 part -= out[at].shape[0]
                 at += pieces
+            value = jnp.concatenate([half[j] for half in halves], axis=0)
             out[at][part, rows, :] = value.astype(BF16)
         return carry
 
@@ -203,7 +209,7 @@
     )(place, target, b_out.reshape(1, channels), channel_weight.reshape(1, channels), *given)
 
 
-def tiles_kernel(per_region, regions, place, index_ref, tile_ref, w_ref, out_ref, w_t_ref, total):
+def tiles_kernel(per_region, regions, place, index_ref, tile_ref, w_ref, out_ref, own_ref, w_t_ref, total):
     blocks, sources, cells, nodes = tile_ref.shape
     total[...] = jnp.zeros_like(total)
     for b in range(blocks):
@@ -213,8 +219,9 @@
             slot = relative * per_region + lax.rem(number, per_region)
             total[slot, b] += tile_ref[b, k].astype(F32).T
     for s in range(total.shape[0]):
+        ref, to = (own_ref, s - per_region) if s // per_region == 1 else (out_ref, s if s < per_region else s - per_region)
         for b in range(blocks):
-            out_ref[s * nodes : (s + 1) * nodes, b * cells : (b + 1) * cells] = total[s, b].astype(BF16)
+            ref[to * nodes : (to + 1) * nodes, b * cells : (b + 1) * cells] = total[s, b].astype(BF16)
     step = 256
     for lo in range(0, w_ref.shape[0], step):
         w_t_ref[:, lo : lo + step] = w_ref[lo : lo + step, :].T
@@ -226,9 +233,10 @@
     return pl.pallas_call(
         functools.partial(tiles_kernel, per_region, regions),
         in_specs=[ON_SMEM, ON_SMEM, ON_VMEM, ON_VMEM],
-        out_specs=[ON_VMEM] * 2,
+        out_specs=[ON_VMEM] * 3,
         out_shape=[
-            pltpu.VMEM((slots * nodes, blocks * cells), BF16),
+            pltpu.VMEM((2 * per_region * nodes, blocks * cells), BF16),
+            pltpu.VMEM((per_region * nodes, blocks * cells), BF16),
             pltpu.VMEM(w_hidden.shape, BF16),
         ],
         scratch_shapes=[pltpu.VMEM((slots, blocks, nodes, cells), F32)],
@@ -240,9 +248,9 @@
 
 def backward_kernel(first, pieces, place, wout_ref, tiles_ref, *refs):
     given, slopes = refs[:pieces], refs[pieces : 2 * pieces]
-    dpred_ref, dpre_ref, below_ref, own_ref, above_ref = refs[2 * pieces :]
+    dpred_ref, dpre_ref, below_ref, above_ref = refs[2 * pieces :]
     length = given[0].shape[2]
-    members, nodes, width = own_ref.shape
+    members, nodes, width = below_ref.shape
     step = 512
     for m in range(members):
         for s in range(pieces):
@@ -258,8 +266,7 @@
                 dpre_ref[m, pl.ds(pl.multiple_of(at, length), length), cols] = dpre
             terms = jnp.dot(tiles_ref[...], dpre_ref[m, :, cols], preferred_element_type=F32)
             below_ref[m, :, cols] = terms[:nodes].astype(BF16)
-            own_ref[m, :, cols] = terms[nodes : 2 * nodes].astype(BF16)
-            above_ref[m, :, cols] = terms[2 * nodes :].astype(BF16)
+            above_ref[m, :, cols] = terms[nodes:].astype(BF16)
 
 
 def backward(first, members, given, w_out_t, slope, tiles, place):
@@ -267,17 +274,16 @@
     _, length, width = slope[0].shape
     cells = length * pieces
     channels = w_out_t.shape[0]
-    nodes = tiles.shape[0] // 3
+    nodes = tiles.shape[0] // 2
     return pl.pallas_call(
         functools.partial(backward_kernel, first, pieces),
         in_specs=[ON_SMEM] + [ON_VMEM] * (2 + pieces + len(slope)),
-        out_specs=[ON_VMEM] * 5,
+        out_specs=[ON_VMEM] * 4,
         out_shape=[
             pltpu.VMEM((members, cells, channels), BF16),
             pltpu.VMEM((members, cells, width), BF16),
             pltpu.VMEM((members, nodes, width), BF16),
             pltpu.VMEM((members, nodes, width), BF16),
-            pltpu.VMEM((members, nodes, width), BF16),
         ],
         compiler_params=params(),
         cost_estimate=cost(2 * members * cells * width * (256 + 3 * nodes), 5 << 20),
@@ -285,35 +291,58 @@
     )(place, w_out_t, tiles, *given, *slope)
 
 
+def own_kernel(tiles_ref, dpre_ref, out_ref):
+    for m in range(dpre_ref.shape[0]):
+        out_ref[m] = jnp.dot(tiles_ref[...], dpre_ref[m], preferred_element_type=F32)
+
+
+def own_terms(tiles, dpre):
+    members, cells, width = dpre.shape
+    return pl.pallas_call(
+        own_kernel,
+        in_specs=[ON_VMEM] * 2,
+        out_specs=ON_VMEM,
+        out_shape=pltpu.VMEM((members, tiles.shape[0], width), F32),
+        compiler_params=params(),
+        cost_estimate=cost(1000, 1000),
+        name="own",
+    )(tiles, dpre)
+
+
 def weights_kernel(turns, groups, cores, counts, place, *refs):
     split_at, lists = 0, []
     for count in counts:
-        some = refs[split_at : split_at + count]
-        lists.append([ref.at[m] for ref in some for m in range(ref.shape[0])])
+        lists.append(refs[split_at : split_at + count])
         split_at += count
-    x, act, dpre, dpred = lists
-    act = [act[m :: len(x)] for m in range(len(x))]
+    (x,), acts, dpre, dpred = lists
     out = refs[split_at:]
-    width = dpre[0].shape[1]
+    width = dpre[0].shape[2]
     step = width // groups
     count, rows, _ = out[0].shape
     count //= len(turns)
     across = (((0,), (0,)), ((), ()))
     mine = lax.rem(place[1], cores)
     for i, turn in enumerate(turns):
-        at = lax.rem(place[0] + turn, groups) * step
+        other = lax.rem(place[0] + turn, groups) if cores == 1 else place[0] ^ turn
+        at = other * step
         cols = pl.ds(pl.multiple_of(at, step), step)
-        for values, others, wide in (
-            (x, dpre, slice(0, width)),
-            (act, dpred, slice(width, None)),
+        for ours, others, wide in (
+            ([x], dpre, slice(0, width)),
+            (acts, dpred, slice(width, None)),
         ):
             total = None
-            for value, other in zip(values, others):
-                if isinstance(value, list):
-                    value = jnp.concatenate([piece[:, cols] for piece in value], axis=0)
-                else:
-                    value = value[:, cols]
-                part = lax.dot_general(value, other[...], across, preferred_element_type=F32)
+            first = 0
+            for other in others:
+                here, cells, columns = other.shape
+                value = [ref[first : first + here, :, cols] for ref in ours]
+                value = (jnp.concatenate(value, axis=1) if len(value) > 1 else value[0])
+                first += here
+                part = lax.dot_general(
+                    value.reshape(here * cells, step),
+                    other[...].reshape(here * cells, columns),
+                    across,
+                    preferred_element_type=F32,
+                )
                 total = part if total is None else total + part
             total = total.astype(BF16).reshape(count, cores, rows, total.shape[1])
             for b in range(count):
@@ -343,50 +372,85 @@
     )(place, *x, *act, *dpre, *dpred)
 
 
-def add_kernel(kept_ref, came_ref, *out):
-    count = out[0].shape[0]
-    for s, ref in enumerate(out):
-        for i in range(count):
-            at = s * count + i
-            ref[i] = (kept_ref[at].astype(F32) + came_ref[at].astype(F32)).astype(BF16)
-
-
-def add(kept, came, parts):
-    blocks, rows, columns = kept.shape
+def plus(left, right):
+    return (left.astype(F32) + right.astype(F32)).astype(BF16)
+
+
+def add_kernel(kept_ref, came_ref, out):
+    for i in range(out.shape[0]):
+        out[i] = plus(kept_ref[i], came_ref[i])
+
+
+def add(kept, came):
     return pl.pallas_call(
         add_kernel,
         in_specs=[ON_VMEM] * 2,
-        out_specs=[ON_VMEM] * parts,
-        out_shape=[pltpu.VMEM((blocks // parts, rows, columns), BF16)] * parts,
+        out_specs=ON_VMEM,
+        out_shape=pltpu.VMEM(kept.shape, BF16),
         compiler_params=params(),
         cost_estimate=cost(1000, 1000),
         name="add",
     )(kept, came)
 
 
-def split_kernel(which, unit, parts, place, *refs):
-    given, out = refs[:-parts], refs[-parts:]
-    count = out[0].shape[0]
-    mine = lax.rem(place[which] // unit, parts)
+def outer_kernel(kept_ref, came_ref, near_ref, far_ref, near_kept, far_kept):
+    chips = kept_ref.shape[0] // 3
+    half = chips // 2
+    for c in range(chips):
+        one, two, three = (
+            plus(kept_ref[t * chips + c], came_ref[t * chips + c]) for t in range(3)
+        )
+        if c < half:
+            near_ref[c], near_ref[half + c], near_kept[c] = one, three, two
+        else:
+            far_ref[c - half], far_ref[c], far_kept[c - half] = two, three, one
+
+
+def inner_kernel(near_kept, near_came, far_kept, far_came, near_ref, far_ref):
+    half = near_ref.shape[0]
+    for c in range(half):
+        near_ref[c] = plus(near_kept[c], near_came[half + c])
+        far_ref[c] = plus(far_kept[c], far_came[half + c])
+
+
+def paired(kernel, given, counts):
+    _, rows, columns = given[0].shape
+    return pl.pallas_call(
+        kernel,
+        in_specs=[ON_VMEM] * len(given),
+        out_specs=[ON_VMEM] * len(counts),
+        out_shape=[pltpu.VMEM((count, rows, columns), BF16) for count in counts],
+        compiler_params=params(),
+        cost_estimate=cost(1000, 1000),
+        name="pairs",
+    )(*given)
+
+
+def chips_kernel(parts, place, own, near, far, near_last, far_last, *out):
+    half = near_last.shape[0]
+    mine = lax.rem(place[1] // 2, parts)
+    total = []
+    for c in range(parts):
+        pair = (near, near_last) if c < half else (far, far_last)
+        total.append(sum((ref[c % half].astype(F32) for ref in pair), own[c].astype(F32)).astype(BF16))
     for s in range(parts):
-        first = lax.rem(mine + s, parts) * count
-        for i in range(count):
-            total = given[0][first + i].astype(F32)
-            for ref in given[1:]:
-                total = total + ref[first + i].astype(F32)
-            out[s][i] = total.astype(BF16)
-
-
-def split(given, place, which, unit, parts):
-    blocks, rows, columns = given[0].shape
-    return pl.pallas_call(
-        functools.partial(split_kernel, which, unit, parts),
+        to = lax.rem(mine + s, parts)
+        value = total[0]
+        for c in range(1, parts):
+            value = jnp.where(to == c, total[c], value)
+        out[s][0] = value
+
+
+def by_chip(given, place, parts):
+    _, rows, columns = given[0].shape
+    return pl.pallas_call(
+        functools.partial(chips_kernel, parts),
         in_specs=[ON_SMEM] + [ON_VMEM] * len(given),
         out_specs=[ON_VMEM] * parts,
-        out_shape=[pltpu.VMEM((blocks // parts, rows, columns), BF16)] * parts,
+        out_shape=[pltpu.VMEM((1, rows, columns), BF16)] * parts,
         compiler_params=params(),
         cost_estimate=cost(1000, 1000),
-        name="split",
+        name="chips",
     )(place, *given)
 
 
@@ -416,28 +480,33 @@
     )(*given)
 
 
-def weight_gradients(x, act, dpre, dpred, place, after, done):
+def weight_gradients(x, act, dpre, dpred, place, after, meanwhile):
     groups, regions = lax.axis_size("member"), lax.axis_size("region")
     blocks, width = groups * regions, x[0].shape[2]
-    if regions % 2 or width % (blocks * 16):
+    chips = regions // 2
+    if groups != 4 or regions % 4 or width % (blocks * 16):
         turns = list(range(groups))
         (part,) = weights(x, act, dpre, dpred, place * 0, blocks, groups, 1, turns)
         part = part.reshape(width, -1)
         part = lax.psum_scatter(part, "member", scatter_dimension=0, tiled=True)
         part = lax.psum_scatter(part, "region", scatter_dimension=0, tiled=True).astype(F32)
-        return part[:, :width], part[:, width:], done
-    given = [None] * groups
-    for turns in turn_sets(groups):
-        away, kept = weights(x, act, dpre, dpred, place, blocks, groups, 2, turns)
-        if after is not None:
-            (away, kept), _ = lax.optimization_barrier(((away, kept), after))
-            after = None
-        came = lax.ppermute(away, "region", [(i, i ^ 1) for i in range(regions)])
-        for s, part in zip(turns, add(kept, came, len(turns))):
-            given[s] = shifted(part, "member", s) if s else part
+        return part[:, :width], part[:, width:], meanwhile(dpre)
+    away, kept = weights(x, act, dpre, dpred, place, blocks, groups, 2, [1, 2, 3])
+    (away, kept), _ = lax.optimization_barrier(((away, kept), after))
+    came = exchanged(away, "region", 1)
+    half = chips // 2
+    near, far, near_kept, far_kept = paired(outer_kernel, (kept, came), (chips, chips, half, half))
+    away, kept = weights(x, act, dpre, dpred, place, blocks, groups, 2, [0])
+    own = add(kept, exchanged(away, "region", 1))
+    near, far = exchanged(near, "member", 1), exchanged(far, "member", 2)
+    dpre, _ = lax.optimization_barrier((dpre, own))
+    done = meanwhile(dpre)
+    near_last, far_last = paired(inner_kernel, (near_kept, near, far_kept, far), (half, half))
+    near_last = exchanged(near_last, "member", 2)
+    far_last = exchanged(far_last, "member", 1)
+    given = (own, near, far, near_last, far_last)
     given, done = lax.optimization_barrier((given, done))
-    chips = regions // 2
-    parts = split(given, place, 1, 2, chips)
+    parts = by_chip(given, place, chips)
     given = [parts[0]]
     for s in range(1, chips):
         route = [(i, (i + 2 * s) % regions) for i in range(regions)]
@@ -484,38 +553,42 @@
     x, w_hidden, w_out_t, act, slope, sends = forward(
         grid_input, w_hidden, b_hidden, w_out_t, place, groups
     )
-    tiles, w_hidden_t = tiles_matrix(
+    tiles, own_tiles, w_hidden_t = tiles_matrix(
         interp_weight, block_index, w_hidden, place, per_region, regions
     )
     x = [x]
     given = [sends[0]] + [shifted(sends[s], "member", s) for s in range(1, groups)]
+    given, tiles = lax.optimization_barrier((given, tiles))
     parts = shares(members)
     adjoint = score(given, target, b_out, channel_weight, place, parts)
-    dpred, dpre, own, up, down = [], [], [], [], []
+    dpred, dpre, up, down = [], [], [], []
     first = 0
     for i, per in enumerate(parts):
         mine = adjoint[i * groups : (i + 1) * groups]
         back = [mine[0]] + [shifted(mine[s], "member", -s) for s in range(1, groups)]
         if dpred:
             back, _ = lax.optimization_barrier((back, dpred[-1]))
+        if dpred:
+            back, _ = lax.optimization_barrier((back, dpred[-1]))
         one = backward(first, per, back, w_out_t, slope, tiles, place)
         first += per
         dpred.append(one[0])
         dpre.append(one[1])
-        own.append(one[3])
         down.append(shifted(one[2], "region", -1))
-        up.append(shifted(one[4], "region", 1))
-    out = finish(0, members, own[0], up[0], down[0], w_hidden_t, None)
-    hidden, output, out = weight_gradients(x, act, dpre, dpred, place, (up[0], down[0]), out)
+        up.append(shifted(one[3], "region", 1))
+
+    def meanwhile(dpre):
+        own = [own_terms(own_tiles, part) for part in dpre]
+        return own, finish(0, members, own[0], up[0], down[0], w_hidden_t, None)
+
+    hidden, output, (own, out) = weight_gradients(
+        x, act, dpre, dpred, place, (up[0], down[0]), meanwhile
+    )
     first = parts[0]
     for i, per in list(enumerate(parts))[1:]:
         out = finish(first, members, own[i], up[i], down[i], w_hidden_t, out)
         first += per
     return hidden, output, out
-
-
-def turn_sets(groups):
-    return [list(range(groups - 1, 0, -1)), [0]]
 
 
 def shares(members):

time: 92.3 us -> 88.2 us (0.956)
  the two profiles are of different devices: /device:TPU:8 before, /device:TPU:3 now
where the time goes in v4:
time: 88.2 us; the launch traced here: 88 us
  Pallas kernels  37.1 us (42%)
  starting transfers between devices  28.4 us (32%)
  waiting for transfers between devices  21.5 us (24%)
  between operations  0.93 us (1%)
    ppermute x13, starting transfers between devices, shifted(): lax.ppermute(block, axis, [((i - distance) % count, i) for i in range(cou...  19.5 us
    ppermute x6, waiting for transfers between devices, exchanged(): return lax.ppermute(block, axis, [(i, i ^ bit) for i in range(count)])  12.3 us
    ppermute x13, waiting for transfers between devices, shifted(): lax.ppermute(block, axis, [((i - distance) % count, i) for i in range(cou...  9.2 us
    pallas_call x3, Pallas kernels, forward(): pl.pallas_call(functools.partial(later_kernel, turn, pieces), in_specs=[O...  7.59 us
    ppermute x6, starting transfers between devices, exchanged(): return lax.ppermute(block, axis, [(i, i ^ bit) for i in range(count)])  7.18 us
    pallas_call x2, Pallas kernels, weights(): pl.pallas_call(functools.partial(weights_kernel, turns, groups, cores, co...  7.08 us
    pallas_call x2, Pallas kernels, backward(): pl.pallas_call(functools.partial(backward_kernel, first, pieces), in_spec...  6.17 us
    pallas_call x2, Pallas kernels, finish(): pl.pallas_call(functools.partial(finish_kernel, first), in_specs=[ON_VMEM...  4.67 us
  transfers between devices with their start and end apart: 22, of which 7 were waited for; matrix products, arithmetic and copies ran while one was open for 0% of the time, Pallas kernels for 34%

profile of v4, /device:TPU:3, one launch (start us, length us, event | category | flops | bytes accessed | tf_op | source)
XLA Modules:
  0.0 88.0 jit_solution(8542482741886975800)
XLA Ops:
  0.6 0.1 pad_add_fusion.place
  0.7 4.5 %forward.4 = (bf16[4,512,1024]{2,1,0:T(8,128)(2,1)S(1)}, bf16[1024,1024]{1,0:T(8,128)(2,1)S(1)}, f32[1,1024]{1,0:T(1,128)S(1)}, bf16[96,1024]{1,0:T(8,128)(2,1)S...) custom-call(s32[2]{0:T(128)S(1)} %pad_add_fusion.place, ...), custom_call_target="tpu_custom_call" | custom-call | flops 1000 | bytes 1000 | tf_op jit(solution)/shard_map/forward/pallas_call | solution.py:115
  5.2 2.4 %collective-permute-start.1 = (bf16[5,96,128]{2,1,0:T(8,128)(2,1)S(1)}, bf16[5,96,128]{2,1,0:T(8,128)(2,1)S(1)}, u32[]{:S(2)}, u32[]{:S(2)}) collective-permute-start(bf16[5,96,128]{2,1,0:T(8,128)(2,1)S(1)} %get-tuple-element.84), channel_id=1, source_target_pairs={{16,0},{24,8},{0,16},{8,24},{17,1},{25,9},{1,17},{9,25},{18,2},{26... | collective-permute-start | bytes 368648 | tf_op jit(solution)/shard_map/ppermute | solution.py:24
  7.6 2.5 %forward.5 = (bf16[4,128,1024]{2,1,0:T(8,128)(2,1)S(1)}, bf16[4,128,1024]{2,1,0:T(8,128)(2,1)S(1)}, bf16[5,96,128]{2,1,0:T(8,128)(2,1)S(1)}) custom-call(s32[2]{0:T(128)S(1)} %pad_add_fusion.place, bf16[4,512,1024]{2,1,0:T(8,128)(2,1)S(1)} %get-tuple-element.81.x_ref.refs_0_, bf16[1024,1024]{1,0:T(8,128)(2,1)S(1)} %get-tuple-element.82.w_ref, ...), custom_call_target="tpu_custom_call" | custom-call | flops 1000 | bytes 1000 | tf_op jit(solution)/shard_map/forward/pallas_call | solution.py:134
  10.2 1.3 %collective-permute-start = (bf16[5,96,128]{2,1,0:T(8,128)(2,1)S(1)}, bf16[5,96,128]{2,1,0:T(8,128)(2,1)S(1)}, u32[]{:S(2)}, u32[]{:S(2)}) collective-permute-start(bf16[5,96,128]{2,1,0:T(8,128)(2,1)S(1)} %get-tuple-element.87), channel_id=1, source_target_pairs={{24,0},{0,8},{8,16},{16,24},{25,1},{1,9},{9,17},{17,25},{26,2},{2,... | collective-permute-start | bytes 368648 | tf_op jit(solution)/shard_map/ppermute | solution.py:24
  11.5 2.5 %forward.6 = (bf16[4,128,1024]{2,1,0:T(8,128)(2,1)S(1)}, bf16[4,128,1024]{2,1,0:T(8,128)(2,1)S(1)}, bf16[5,96,128]{2,1,0:T(8,128)(2,1)S(1)}) custom-call(s32[2]{0:T(128)S(1)} %pad_add_fusion.place, bf16[4,512,1024]{2,1,0:T(8,128)(2,1)S(1)} %get-tuple-element.81.x_ref.refs_0_, bf16[1024,1024]{1,0:T(8,128)(2,1)S(1)} %get-tuple-element.82.w_ref, ...), custom_call_target="tpu_custom_call" | custom-call | flops 1000 | bytes 1000 | tf_op jit(solution)/shard_map/forward/pallas_call | solution.py:134
  14.0 0.0 copy-start
  14.0 0.0 copy-start.2
  14.1 2.0 %collective-permute-start.2 = (bf16[5,96,128]{2,1,0:T(8,128)(2,1)S(1)}, bf16[5,96,128]{2,1,0:T(8,128)(2,1)S(1)}, u32[]{:S(2)}, u32[]{:S(2)}) collective-permute-start(bf16[5,96,128]{2,1,0:T(8,128)(2,1)S(1)} %get-tuple-element.89), channel_id=1, source_target_pairs={{8,0},{16,8},{24,16},{0,24},{9,1},{17,9},{25,17},{1,25},{10,2},{18... | collective-permute-start | bytes 368648 | tf_op jit(solution)/shard_map/ppermute | solution.py:24
  16.1 2.5 %forward.7 = (bf16[4,128,1024]{2,1,0:T(8,128)(2,1)S(1)}, bf16[4,128,1024]{2,1,0:T(8,128)(2,1)S(1)}, bf16[5,96,128]{2,1,0:T(8,128)(2,1)S(1)}) custom-call(s32[2]{0:T(128)S(1)} %pad_add_fusion.place, bf16[4,512,1024]{2,1,0:T(8,128)(2,1)S(1)} %get-tuple-element.81.x_ref.refs_0_, bf16[1024,1024]{1,0:T(8,128)(2,1)S(1)} %get-tuple-element.82.w_ref, ...), custom_call_target="tpu_custom_call" | custom-call | flops 1000 | bytes 1000 | tf_op jit(solution)/shard_map/forward/pallas_call | solution.py:134
  18.6 0.0 copy-start.1
  18.7 1.5 %tiles.1 = (bf16[512,512]{1,0:T(8,128)(2,1)S(1)}, bf16[256,512]{1,0:T(8,128)(2,1)S(1)}, bf16[1024,1024]{1,0:T(8,128)(2,1)S(1)}) custom-call(s32[2]{0:T(128)S(1)} %pad_add_fusion.place, s32[4,3]{1,0:T(4,128)S(1)} %copy-done.2, bf16[4,3,128,128]{3,2,1,0:T(8,128)(2,1)S(1)} %copy-done, bf16[1024,1024]{1,0:T(8,128)(2,1)S(1)} %get-tuple-element.82.w_ref), custom_call_target="tpu_custom_call" | custom-call | flops 4000000 | bytes 2097152 | tf_op jit(solution)/shard_map/tiles/pallas_call | solution.py:233
  20.2 2.4 %score.1 = (bf16[1,96,128]{2,1,0:T(8,128)(2,1)S(1)}, bf16[1,96,128]{2,1,0:T(8,128)(2,1)S(1)}, bf16[1,96,128]{2,1,0:T(8,128)(2,1)S(1)}, bf16[1,96,128]{2,1,0:T(8,...) custom-call(s32[2]{0:T(128)S(1)} %pad_add_fusion.place, ...), custom_call_target="tpu_custom_call" | custom-call | flops 40000000 | bytes 1048576 | tf_op jit(solution)/shard_map/score/pallas_call | solution.py:200
  22.6 1.4 %collective-permute-start.3 = (bf16[1,96,128]{2,1,0:T(8,128)(2,1)S(1)}, bf16[1,96,128]{2,1,0:T(8,128)(2,1)S(1)}, u32[]{:S(2)}, u32[]{:S(2)}) collective-permute-start(bf16[1,96,128]{2,1,0:T(8,128)(2,1)S(1)} %get-tuple-element.103), channel_id=1, source_target_pairs={{8,0},{16,8},{24,16},{0,24},{9,1},{17,9},{25,17},{1,25},{10,2},{18... | collective-permute-start | bytes 73736 | tf_op jit(solution)/shard_map/ppermute | solution.py:24
  24.0 0.4 collective-permute-start.5
  24.4 2.9 %collective-permute-start.6 = (bf16[3,96,128]{2,1,0:T(8,128)(2,1)S(1)}, bf16[3,96,128]{2,1,0:T(8,128)(2,1)S(1)}, u32[]{:S(2)}, u32[]{:S(2)}) collective-permute-start(bf16[3,96,128]{2,1,0:T(8,128)(2,1)S(1)} %get-tuple-element.112), channel_id=1, source_target_pairs={{8,0},{16,8},{24,16},{0,24},{9,1},{17,9},{25,17},{1,25},{10,2},{18... | collective-permute-start | bytes 221192 | tf_op jit(solution)/shard_map/ppermute | solution.py:24
  27.3 0.6 collective-permute-start.7
  27.9 0.1 collective-permute-start.8
  28.0 0.6 collective-permute-done.5.refs_3_
  28.6 1.9 %backward.2 = (bf16[1,512,96]{2,1,0:T(8,128)(2,1)S(1)}, bf16[1,512,1024]{2,1,0:T(8,128)(2,1)S(1)}, bf16[1,256,1024]{2,1,0:T(8,128)(2,1)S(1)}, bf16[1,256,1024]{2,1,0:T(8,128)(2,1)S(1)}) custom-call(s32[2]{0:T(128)S(1)} %pad_add_fusion.place, bf16[96,1024]{1,0:T(8,128)(2,1)S(1)} %get-tuple-element.86.wout_ref, ...), custom_call_target="tpu_custom_call" | custom-call | flops 1073741824 | bytes 5242880 | tf_op jit(solution)/shard_map/backward/pallas_call | solution.py:278
  30.5 5.0 %collective-permute-start.10 = (bf16[1,256,1024]{2,1,0:T(8,128)(2,1)S(1)}, bf16[1,256,1024]{2,1,0:T(8,128)(2,1)S(1)}, u32[]{:S(2)}, u32[]{:S(2)}) collective-permute-start(bf16[1,256,1024]{2,1,0:T(8,128)(2,1)S(1)} %get-tuple-element.130), channel_id=1, source_target_pairs={{7,0},{0,1},{1,2},{2,3},{3,4},{4,5},{5,6},{6,7},{15,8},{8,9},{9,10... | collective-permute-start | bytes 1572872 | tf_op jit(solution)/shard_map/ppermute | solution.py:24
  35.6 4.3 %backward.3 = (bf16[3,512,96]{2,1,0:T(8,128)(2,1)S(1)}, bf16[3,512,1024]{2,1,0:T(8,128)(2,1)S(1)}, bf16[3,256,1024]{2,1,0:T(8,128)(2,1)S(1)}, bf16[3,256,1024]{2,1,0:T(8,128)(2,1)S(1)}) custom-call(s32[2]{0:T(128)S(1)} %pad_add_fusion.place, bf16[96,1024]{1,0:T(8,128)(2,1)S(1)} %get-tuple-element.86.wout_ref, ...), custom_call_target="tpu_custom_call" | custom-call | flops 3221225472 | bytes 5242880 | tf_op jit(solution)/shard_map/backward/pallas_call | solution.py:278
  39.9 3.3 %collective-permute-start.20 = (bf16[3,256,1024]{2,1,0:T(8,128)(2,1)S(1)}, bf16[3,256,1024]{2,1,0:T(8,128)(2,1)S(1)}, u32[]{:S(2)}, u32[]{:S(2)}) collective-permute-start(bf16[3,256,1024]{2,1,0:T(8,128)(2,1)S(1)} %get-tuple-element.156), channel_id=1, source_target_pairs={{7,0},{0,1},{1,2},{2,3},{3,4},{4,5},{5,6},{6,7},{15,8},{8,9},{9,10... | collective-permute-start | bytes 4718600 | tf_op jit(solution)/shard_map/ppermute | solution.py:24
  43.2 5.0 %weights.3 = (bf16[12,32,1120]{2,1,0:T(8,128)(2,1)S(1)}, bf16[12,32,1120]{2,1,0:T(8,128)(2,1)S(1)}) custom-call(s32[2]{0:T(128)S(1)} %pad_add_fusion.place, bf16[4,512,1024]{2,1,0:T(8,128)(2,1)S(1)} %get-tuple-element.81.x_ref.refs_0_, bf16[4,128,1024]{2,1,0:T(8,128)(2,1)S(1)} %get-tuple-element.91.refs_1_, ...), custom_call_target="tpu_custom_call" | custom-call | flops 1000 | bytes 1000 | tf_op jit(solution)/shard_map/weights/pallas_call | solution.py:364
  48.2 2.6 %collective-permute-done.11.down_ref = bf16[1,256,1024]{2,1,0:T(8,128)(2,1)S(1)} collective-permute-done((bf16[1,256,1024]{2,1,0:T(8,128)(2,1)S(1)}, bf16[1,256,1024]{2,1,0:T(8,128)(2,1)S(1)}, u32[]{:S(2)}, u32[]{:S(2)}) %collective-permute-start.11) | collective-permute-done | bytes 524320 | tf_op jit(solution)/shard_map/ppermute | solution.py:24
  50.8 2.4 %collective-permute-done.12.came_ref = bf16[12,32,1120]{2,1,0:T(8,128)(2,1)S(1)} collective-permute-done((bf16[12,32,1120]{2,1,0:T(8,128)(2,1)S(1)}, bf16[12,32,1120]{2,1,0:T(8,128)(2,1)S(1)}, u32[]{:S(2)}, u32[]{:S(2)}) %collective-permute-start.12) | collective-permute-done | bytes 860192 | tf_op jit(solution)/shard_map/ppermute | solution.py:29
  53.2 0.2 pairs.2
  53.4 1.3 %collective-permute-start.13 = (bf16[4,32,1120]{2,1,0:T(8,128)(2,1)S(1)}, bf16[4,32,1120]{2,1,0:T(8,128)(2,1)S(1)}, u32[]{:S(2)}, u32[]{:S(2)}) collective-permute-start(bf16[4,32,1120]{2,1,0:T(8,128)(2,1)S(1)} %get-tuple-element.134), channel_id=1, source_target_pairs={{0,8},{8,0},{16,24},{24,16},{1,9},{9,1},{17,25},{25,17},{2,10},{10... | collective-permute-start | bytes 860168 | tf_op jit(solution)/shard_map/ppermute | solution.py:29
  54.7 1.7 %collective-permute-start.14 = (bf16[4,32,1120]{2,1,0:T(8,128)(2,1)S(1)}, bf16[4,32,1120]{2,1,0:T(8,128)(2,1)S(1)}, u32[]{:S(2)}, u32[]{:S(2)}) collective-permute-start(bf16[4,32,1120]{2,1,0:T(8,128)(2,1)S(1)} %get-tuple-element.135), channel_id=1, source_target_pairs={{0,16},{8,24},{16,0},{24,8},{1,17},{9,25},{17,1},{25,9},{2,18},{10... | collective-permute-start | bytes 860168 | tf_op jit(solution)/shard_map/ppermute | solution.py:29
  56.5 2.1 %weights.2 = (bf16[4,32,1120]{2,1,0:T(8,128)(2,1)S(1)}, bf16[4,32,1120]{2,1,0:T(8,128)(2,1)S(1)}) custom-call(s32[2]{0:T(128)S(1)} %pad_add_fusion.place, bf16[4,512,1024]{2,1,0:T(8,128)(2,1)S(1)} %get-tuple-element.81.x_ref.refs_0_, bf16[4,128,1024]{2,1,0:T(8,128)(2,1)S(1)} %get-tuple-element.91.refs_1_, ...), custom_call_target="tpu_custom_call" | custom-call | flops 1000 | bytes 1000 | tf_op jit(solution)/shard_map/weights/pallas_call | solution.py:364
  58.6 0.8 collective-permute-start.9
  59.4 8.0 %collective-permute-done.13.near_came.near = bf16[4,32,1120]{2,1,0:T(8,128)(2,1)S(1)} collective-permute-done((bf16[4,32,1120]{2,1,0:T(8,128)(2,1)S(1)}, bf16[4,32,1120]{2,1,0:T(8,128)(2,1)S(1)}, u32[]{:S(2)}, u32[]{:S(2)}) %collective-permute-start.13) | collective-permute-done | bytes 286752 | tf_op jit(solution)/shard_map/ppermute | solution.py:29
  67.4 0.1 pairs.3
  67.5 3.1 %collective-permute-start.15 = (bf16[2,32,1120]{2,1,0:T(8,128)(2,1)S(1)}, bf16[2,32,1120]{2,1,0:T(8,128)(2,1)S(1)}, u32[]{:S(2)}, u32[]{:S(2)}) collective-permute-start(bf16[2,32,1120]{2,1,0:T(8,128)(2,1)S(1)} %get-tuple-element.138), channel_id=1, source_target_pairs={{0,16},{8,24},{16,0},{24,8},{1,17},{9,25},{17,1},{25,9},{2,18},{10... | collective-permute-start | bytes 430088 | tf_op jit(solution)/shard_map/ppermute | solution.py:29
  70.6 0.2 collective-permute-start.16
  70.8 0.1 add.3.own
  70.9 0.4 own.2.own_ref
  71.3 1.0 %own.3.own_ref = f32[3,256,1024]{2,1,0:T(8,128)S(1)} custom-call(bf16[256,512]{1,0:T(8,128)(2,1)S(1)} %get-tuple-element.140.tiles_ref, bf16[3,512,1024]{2,1,0:T(8,128)(2,1)S(1)} %get-tuple-element.142.refs_6_.dpre_ref), custom_call_target="tpu_custom_call" | custom-call | flops 1000 | bytes 1000 | tf_op jit(solution)/shard_map/own/pallas_call | solution.py:301
  72.4 1.7 %finish.2.refs_0_ = f32[4,256,1024]{2,1,0:T(8,128)} custom-call(f32[1,256,1024]{2,1,0:T(8,128)S(1)} %own.2.own_ref, bf16[1,256,1024]{2,1,0:T(8,128)(2,1)S(1)} %collective-permute-done.10.up_ref, bf16[1,256,1024]{2,1,0:T(8,128)(2,1)S(1)} %collective-permute-done.11.down_ref, bf16[1024,1024]{1,0:T(8,128)(2,1)S(1)} %get-tuple-element.143.w_ref), custom_call_target="tpu_custom_call" | custom-call | flops 1000 | bytes 1000 | tf_op jit(solution)/shard_map/finish/pallas_call | solution.py:532
  74.1 1.8 %collective-permute-done.16.far_last = bf16[2,32,1120]{2,1,0:T(8,128)(2,1)S(1)} collective-permute-done((bf16[2,32,1120]{2,1,0:T(8,128)(2,1)S(1)}, bf16[2,32,1120]{2,1,0:T(8,128)(2,1)S(1)}, u32[]{:S(2)}, u32[]{:S(2)}) %collective-permute-start.16) | collective-permute-done | bytes 143392 | tf_op jit(solution)/shard_map/ppermute | solution.py:29
  76.0 0.7 chips.1
  76.7 0.7 collective-permute-start.17
  77.3 0.1 collective-permute-start.18
  77.5 0.9 %collective-permute-start.19 = (bf16[1,32,1120]{2,1,0:T(8,128)(2,1)S(1)}, bf16[1,32,1120]{2,1,0:T(8,128)(2,1)S(1)}, u32[]{:S(2)}, u32[]{:S(2)}) collective-permute-start(bf16[1,32,1120]{2,1,0:T(8,128)(2,1)S(1)} %get-tuple-element.152), channel_id=1, source_target_pairs={{0,6},{1,7},{2,0},{3,1},{4,2},{5,3},{6,4},{7,5},{8,14},{9,15},{10,... | collective-permute-start | bytes 215048 | tf_op jit(solution)/shard_map/ppermute | solution.py:513
  78.4 1.8 %collective-permute-done.20.up_ref = bf16[3,256,1024]{2,1,0:T(8,128)(2,1)S(1)} collective-permute-done((bf16[3,256,1024]{2,1,0:T(8,128)(2,1)S(1)}, bf16[3,256,1024]{2,1,0:T(8,128)(2,1)S(1)}, u32[]{:S(2)}, u32[]{:S(2)}) %collective-permute-start.20) | collective-permute-done | bytes 1572896 | tf_op jit(solution)/shard_map/ppermute | solution.py:24
  80.2 4.2 %collective-permute-done.21.down_ref = bf16[3,256,1024]{2,1,0:T(8,128)(2,1)S(1)} collective-permute-done((bf16[3,256,1024]{2,1,0:T(8,128)(2,1)S(1)}, bf16[3,256,1024]{2,1,0:T(8,128)(2,1)S(1)}, u32[]{:S(2)}, u32[]{:S(2)}) %collective-permute-start.21) | collective-permute-done | bytes 1572896 | tf_op jit(solution)/shard_map/ppermute | solution.py:24
  84.4 2.9 %finish.3 = f32[4,256,1024]{2,1,0:T(8,128)} custom-call(f32[3,256,1024]{2,1,0:T(8,128)S(1)} %own.3.own_ref, bf16[3,256,1024]{2,1,0:T(8,128)(2,1)S(1)} %collective-permute-done.20.up_ref, bf16[3,256,1024]{2,1,0:T(8,128)(2,1)S(1)} %collective-permute-done.21.down_ref, bf16[1024,1024]{1,0:T(8,128)(2,1)S(1)} %get-tuple-element.143.w_ref, ...), custom_call_target="tpu_custom_call", output_to_operand_aliasing={{}: (4, {})} | custom-call | flops 1000 | bytes 1000 | tf_op jit(solution)/shard_map/finish/pallas_call | solution.py:532
  87.3 0.7 total.1
  (26 shorter events, 0.1 us)
Async XLA Ops:
  5.2 14.9 %collective-permute-start.1 = (bf16[5,96,128]{2,1,0:T(8,128)(2,1)S(1)}, bf16[5,96,128]{2,1,0:T(8,128)(2,1)S(1)}, u32[]{:S(2)}, u32[]{:S(2)}) collective-permute-start(bf16[5,96,128]{2,1,0:T(8,128)(2,1)S(1)} %get-tuple-element.84), channel_id=1, source_target_pairs={{16,0},{24,8},{0,16},{8,24},{17,1},{25,9},{1,17},{9,25},{18,2},{26... | collective-permute-start | bytes 368648 | tf_op jit(solution)/shard_map/ppermute | solution.py:24
  10.2 10.0 %collective-permute-start = (bf16[5,96,128]{2,1,0:T(8,128)(2,1)S(1)}, bf16[5,96,128]{2,1,0:T(8,128)(2,1)S(1)}, u32[]{:S(2)}, u32[]{:S(2)}) collective-permute-start(bf16[5,96,128]{2,1,0:T(8,128)(2,1)S(1)} %get-tuple-element.87), channel_id=1, source_target_pairs={{24,0},{0,8},{8,16},{16,24},{25,1},{1,9},{9,17},{17,25},{26,2},{2,... | collective-permute-start | bytes 368648 | tf_op jit(solution)/shard_map/ppermute | solution.py:24
  14.0 4.6 %copy-start = (bf16[4,3,128,128]{3,2,1,0:T(8,128)(2,1)S(1)}, bf16[4,3,128,128]{3,2,1,0:T(8,128)(2,1)}, u32[]{:S(2)}) copy-start(bf16[4,3,128,128]{3,2,1,0:T(8,128)(2,1)} %tile_ref.1) | copy-start | bytes 1179652
  14.0 4.6 %copy-start.2 = (s32[4,3]{1,0:T(4,128)S(1)}, s32[4,3]{1,0:T(4,128)}, u32[]{:S(2)}) copy-start(s32[4,3]{1,0:T(4,128)} %index_ref.1) | copy-start | bytes 148
  14.1 6.2 %collective-permute-start.2 = (bf16[5,96,128]{2,1,0:T(8,128)(2,1)S(1)}, bf16[5,96,128]{2,1,0:T(8,128)(2,1)S(1)}, u32[]{:S(2)}, u32[]{:S(2)}) collective-permute-start(bf16[5,96,128]{2,1,0:T(8,128)(2,1)S(1)} %get-tuple-element.89), channel_id=1, source_target_pairs={{8,0},{16,8},{24,16},{0,24},{9,1},{17,9},{25,17},{1,25},{10,2},{18... | collective-permute-start | bytes 368648 | tf_op jit(solution)/shard_map/ppermute | solution.py:24
  18.6 1.6 %copy-start.1 = (f32[96,512]{1,0:T(8,128)S(1)}, f32[96,512]{1,0:T(8,128)}, u32[]{:S(2)}) copy-start(f32[96,512]{1,0:T(8,128)} %target_ref.1) | copy-start | bytes 589828
  18.7 1.6 %copy-start.3 = (f32[96]{0:T(128)S(1)}, f32[96]{0:T(128)}, u32[]{:S(2)}) copy-start(f32[96]{0:T(128)} %param.13) | copy-start | bytes 1156
  18.7 1.6 %copy-start.4 = (f32[96]{0:T(128)S(1)}, f32[96]{0:T(128)}, u32[]{:S(2)}) copy-start(f32[96]{0:T(128)} %param.15) | copy-start | bytes 1156
  22.6 5.3 %collective-permute-start.3 = (bf16[1,96,128]{2,1,0:T(8,128)(2,1)S(1)}, bf16[1,96,128]{2,1,0:T(8,128)(2,1)S(1)}, u32[]{:S(2)}, u32[]{:S(2)}) collective-permute-start(bf16[1,96,128]{2,1,0:T(8,128)(2,1)S(1)} %get-tuple-element.103), channel_id=1, source_target_pairs={{8,0},{16,8},{24,16},{0,24},{9,1},{17,9},{25,17},{1,25},{10,2},{18... | collective-permute-start | bytes 73736 | tf_op jit(solution)/shard_map/ppermute | solution.py:24
  24.0 3.9 %collective-permute-start.4 = (bf16[1,96,128]{2,1,0:T(8,128)(2,1)S(1)}, bf16[1,96,128]{2,1,0:T(8,128)(2,1)S(1)}, u32[]{:S(2)}, u32[]{:S(2)}) collective-permute-start(bf16[1,96,128]{2,1,0:T(8,128)(2,1)S(1)} %get-tuple-element.104), channel_id=1, source_target_pairs={{16,0},{24,8},{0,16},{8,24},{17,1},{25,9},{1,17},{9,25},{18,2},{26... | collective-permute-start | bytes 73736 | tf_op jit(solution)/shard_map/ppermute | solution.py:24
  24.0 4.6 %collective-permute-start.5 = (bf16[1,96,128]{2,1,0:T(8,128)(2,1)S(1)}, bf16[1,96,128]{2,1,0:T(8,128)(2,1)S(1)}, u32[]{:S(2)}, u32[]{:S(2)}) collective-permute-start(bf16[1,96,128]{2,1,0:T(8,128)(2,1)S(1)} %get-tuple-element.105), channel_id=1, source_target_pairs={{24,0},{0,8},{8,16},{16,24},{25,1},{1,9},{9,17},{17,25},{26,2},{2,... | collective-permute-start | bytes 73736 | tf_op jit(solution)/shard_map/ppermute | solution.py:24
  24.4 11.2 %collective-permute-start.6 = (bf16[3,96,128]{2,1,0:T(8,128)(2,1)S(1)}, bf16[3,96,128]{2,1,0:T(8,128)(2,1)S(1)}, u32[]{:S(2)}, u32[]{:S(2)}) collective-permute-start(bf16[3,96,128]{2,1,0:T(8,128)(2,1)S(1)} %get-tuple-element.112), channel_id=1, source_target_pairs={{8,0},{16,8},{24,16},{0,24},{9,1},{17,9},{25,17},{1,25},{10,2},{18... | collective-permute-start | bytes 221192 | tf_op jit(solution)/shard_map/ppermute | solution.py:24
  27.3 8.3 %collective-permute-start.7 = (bf16[3,96,128]{2,1,0:T(8,128)(2,1)S(1)}, bf16[3,96,128]{2,1,0:T(8,128)(2,1)S(1)}, u32[]{:S(2)}, u32[]{:S(2)}) collective-permute-start(bf16[3,96,128]{2,1,0:T(8,128)(2,1)S(1)} %get-tuple-element.113), channel_id=1, source_target_pairs={{16,0},{24,8},{0,16},{8,24},{17,1},{25,9},{1,17},{9,25},{18,2},{26... | collective-permute-start | bytes 221192 | tf_op jit(solution)/shard_map/ppermute | solution.py:24
  27.9 7.7 %collective-permute-start.8 = (bf16[3,96,128]{2,1,0:T(8,128)(2,1)S(1)}, bf16[3,96,128]{2,1,0:T(8,128)(2,1)S(1)}, u32[]{:S(2)}, u32[]{:S(2)}) collective-permute-start(bf16[3,96,128]{2,1,0:T(8,128)(2,1)S(1)} %get-tuple-element.114), channel_id=1, source_target_pairs={{24,0},{0,8},{8,16},{16,24},{25,1},{1,9},{9,17},{17,25},{26,2},{2,... | collective-permute-start | bytes 221192 | tf_op jit(solution)/shard_map/ppermute | solution.py:24
  30.5 17.6 %collective-permute-start.10 = (bf16[1,256,1024]{2,1,0:T(8,128)(2,1)S(1)}, bf16[1,256,1024]{2,1,0:T(8,128)(2,1)S(1)}, u32[]{:S(2)}, u32[]{:S(2)}) collective-permute-start(bf16[1,256,1024]{2,1,0:T(8,128)(2,1)S(1)} %get-tuple-element.130), channel_id=1, source_target_pairs={{7,0},{0,1},{1,2},{2,3},{3,4},{4,5},{5,6},{6,7},{15,8},{8,9},{9,10... | collective-permute-start | bytes 1572872 | tf_op jit(solution)/shard_map/ppermute | solution.py:24
  35.6 15.2 %collective-permute-start.11 = (bf16[1,256,1024]{2,1,0:T(8,128)(2,1)S(1)}, bf16[1,256,1024]{2,1,0:T(8,128)(2,1)S(1)}, u32[]{:S(2)}, u32[]{:S(2)}) collective-permute-start(bf16[1,256,1024]{2,1,0:T(8,128)(2,1)S(1)} %get-tuple-element.131), channel_id=1, source_target_pairs={{1,0},{2,1},{3,2},{4,3},{5,4},{6,5},{7,6},{0,7},{9,8},{10,9},{11,1... | collective-permute-start | bytes 1572872 | tf_op jit(solution)/shard_map/ppermute | solution.py:24
  39.9 40.4 %collective-permute-start.20 = (bf16[3,256,1024]{2,1,0:T(8,128)(2,1)S(1)}, bf16[3,256,1024]{2,1,0:T(8,128)(2,1)S(1)}, u32[]{:S(2)}, u32[]{:S(2)}) collective-permute-start(bf16[3,256,1024]{2,1,0:T(8,128)(2,1)S(1)} %get-tuple-element.156), channel_id=1, source_target_pairs={{7,0},{0,1},{1,2},{2,3},{3,4},{4,5},{5,6},{6,7},{15,8},{8,9},{9,10... | collective-permute-start | bytes 4718600 | tf_op jit(solution)/shard_map/ppermute | solution.py:24
  43.2 41.2 %collective-permute-start.21 = (bf16[3,256,1024]{2,1,0:T(8,128)(2,1)S(1)}, bf16[3,256,1024]{2,1,0:T(8,128)(2,1)S(1)}, u32[]{:S(2)}, u32[]{:S(2)}) collective-permute-start(bf16[3,256,1024]{2,1,0:T(8,128)(2,1)S(1)} %get-tuple-element.157), channel_id=1, source_target_pairs={{1,0},{2,1},{3,2},{4,3},{5,4},{6,5},{7,6},{0,7},{9,8},{10,9},{11,1... | collective-permute-start | bytes 4718600 | tf_op jit(solution)/shard_map/ppermute | solution.py:24
  50.8 2.4 %collective-permute-start.12 = (bf16[12,32,1120]{2,1,0:T(8,128)(2,1)S(1)}, bf16[12,32,1120]{2,1,0:T(8,128)(2,1)S(1)}, u32[]{:S(2)}, u32[]{:S(2)}) collective-permute-start(bf16[12,32,1120]{2,1,0:T(8,128)(2,1)S(1)} %get-tuple-element.133), channel_id=1, source_target_pairs={{0,1},{1,0},{2,3},{3,2},{4,5},{5,4},{6,7},{7,6},{8,9},{9,8},{10,11... | collective-permute-start | bytes 2580488 | tf_op jit(solution)/shard_map/ppermute | solution.py:29
  53.4 14.0 %collective-permute-start.13 = (bf16[4,32,1120]{2,1,0:T(8,128)(2,1)S(1)}, bf16[4,32,1120]{2,1,0:T(8,128)(2,1)S(1)}, u32[]{:S(2)}, u32[]{:S(2)}) collective-permute-start(bf16[4,32,1120]{2,1,0:T(8,128)(2,1)S(1)} %get-tuple-element.134), channel_id=1, source_target_pairs={{0,8},{8,0},{16,24},{24,16},{1,9},{9,1},{17,25},{25,17},{2,10},{10... | collective-permute-start | bytes 860168 | tf_op jit(solution)/shard_map/ppermute | solution.py:29
  54.7 12.7 %collective-permute-start.14 = (bf16[4,32,1120]{2,1,0:T(8,128)(2,1)S(1)}, bf16[4,32,1120]{2,1,0:T(8,128)(2,1)S(1)}, u32[]{:S(2)}, u32[]{:S(2)}) collective-permute-start(bf16[4,32,1120]{2,1,0:T(8,128)(2,1)S(1)} %get-tuple-element.135), channel_id=1, source_target_pairs={{0,16},{8,24},{16,0},{24,8},{1,17},{9,25},{17,1},{25,9},{2,18},{10... | collective-permute-start | bytes 860168 | tf_op jit(solution)/shard_map/ppermute | solution.py:29
  58.6 12.2 %collective-permute-start.9 = (bf16[4,32,1120]{2,1,0:T(8,128)(2,1)S(1)}, bf16[4,32,1120]{2,1,0:T(8,128)(2,1)S(1)}, u32[]{:S(2)}, u32[]{:S(2)}) collective-permute-start(bf16[4,32,1120]{2,1,0:T(8,128)(2,1)S(1)} %get-tuple-element.127), channel_id=1, source_target_pairs={{0,1},{1,0},{2,3},{3,2},{4,5},{5,4},{6,7},{7,6},{8,9},{9,8},{10,11... | collective-permute-start | bytes 860168 | tf_op jit(solution)/shard_map/ppermute | solution.py:29
  67.5 6.6 %collective-permute-start.15 = (bf16[2,32,1120]{2,1,0:T(8,128)(2,1)S(1)}, bf16[2,32,1120]{2,1,0:T(8,128)(2,1)S(1)}, u32[]{:S(2)}, u32[]{:S(2)}) collective-permute-start(bf16[2,32,1120]{2,1,0:T(8,128)(2,1)S(1)} %get-tuple-element.138), channel_id=1, source_target_pairs={{0,16},{8,24},{16,0},{24,8},{1,17},{9,25},{17,1},{25,9},{2,18},{10... | collective-permute-start | bytes 430088 | tf_op jit(solution)/shard_map/ppermute | solution.py:29
  70.6 5.4 %collective-permute-start.16 = (bf16[2,32,1120]{2,1,0:T(8,128)(2,1)S(1)}, bf16[2,32,1120]{2,1,0:T(8,128)(2,1)S(1)}, u32[]{:S(2)}, u32[]{:S(2)}) collective-permute-start(bf16[2,32,1120]{2,1,0:T(8,128)(2,1)S(1)} %get-tuple-element.139), channel_id=1, source_target_pairs={{0,8},{8,0},{16,24},{24,16},{1,9},{9,1},{17,25},{25,17},{2,10},{10... | collective-permute-start | bytes 430088 | tf_op jit(solution)/shard_map/ppermute | solution.py:29
  76.7 10.6 %collective-permute-start.17 = (bf16[1,32,1120]{2,1,0:T(8,128)(2,1)S(1)}, bf16[1,32,1120]{2,1,0:T(8,128)(2,1)S(1)}, u32[]{:S(2)}, u32[]{:S(2)}) collective-permute-start(bf16[1,32,1120]{2,1,0:T(8,128)(2,1)S(1)} %get-tuple-element.150), channel_id=1, source_target_pairs={{0,2},{1,3},{2,4},{3,5},{4,6},{5,7},{6,0},{7,1},{8,10},{9,11},{10,... | collective-permute-start | bytes 215048 | tf_op jit(solution)/shard_map/ppermute | solution.py:513
  77.3 10.0 %collective-permute-start.18 = (bf16[1,32,1120]{2,1,0:T(8,128)(2,1)S(1)}, bf16[1,32,1120]{2,1,0:T(8,128)(2,1)S(1)}, u32[]{:S(2)}, u32[]{:S(2)}) collective-permute-start(bf16[1,32,1120]{2,1,0:T(8,128)(2,1)S(1)} %get-tuple-element.151), channel_id=1, source_target_pairs={{0,4},{1,5},{2,6},{3,7},{4,0},{5,1},{6,2},{7,3},{8,12},{9,13},{10,... | collective-permute-start | bytes 215048 | tf_op jit(solution)/shard_map/ppermute | solution.py:513
  77.5 9.9 %collective-permute-start.19 = (bf16[1,32,1120]{2,1,0:T(8,128)(2,1)S(1)}, bf16[1,32,1120]{2,1,0:T(8,128)(2,1)S(1)}, u32[]{:S(2)}, u32[]{:S(2)}) collective-permute-start(bf16[1,32,1120]{2,1,0:T(8,128)(2,1)S(1)} %get-tuple-element.152), channel_id=1, source_target_pairs={{0,6},{1,7},{2,0},{3,1},{4,2},{5,3},{6,4},{7,5},{8,14},{9,15},{10,... | collective-permute-start | bytes 215048 | tf_op jit(solution)/shard_map/ppermute | solution.py:513

commit v5 on v4

--- a/solution.py
+++ b/solution.py
@@ -45,31 +45,40 @@
     return pl.CostEstimate(flops=int(flops), bytes_accessed=int(moved), transcendentals=0)
 
 
-def cells_forward(turn, place, pieces, x_ref, w_ref, b_ref, wout_ref, act_ref, slope_ref, send_ref):
+def cells_forward(
+    turn, place, pieces, x_ref, w_ref, b_ref, wout_ref, act_ref, slope_ref, send_ref, ready
+):
     members, cells, width = x_ref.shape
     length = cells // pieces
     at = lax.rem(place[0] + turn, pieces) * length
-    x = x_ref[:, pl.ds(pl.multiple_of(at, length), length), :].reshape(members * length, width)
+    cells = pl.ds(pl.multiple_of(at, length), length)
     each = 2 if members % 2 == 0 else 1
-    base = None
-    for m in range(0, members, each):
-        rows = x[m * length : (m + each) * length]
-        pre = jnp.dot(rows, w_ref[...], preferred_element_type=F32) + b_ref[...]
-        logistic = 0.5 * jnp.tanh(0.5 * pre) + 0.5
-        act = pre * logistic
-        slope = (logistic + act * (1.0 - logistic)).astype(BF16)
-        slope_ref[m : m + each] = slope.reshape(each, length, width)
-        act = act.astype(BF16)
-        act_ref[m : m + each] = act.reshape(each, length, width)
-        line = lax.dot_general(
-            wout_ref[...], act, (((1,), (1,)), ((), ())), preferred_element_type=F32
-        )
-        if m == 0:
-            first = line[:, :length].astype(BF16)
-            send_ref[0] = first
-            base = first.astype(F32)
+    starts = range(0, members, each)
+    lines = dict.fromkeys(starts)
+    step = width // len(ready)
+    for part, wait in enumerate(ready):
+        wait()
+        cols = slice(part * step, (part + 1) * step)
+        for m in starts:
+            rows = x_ref[m : m + each, cells, :].reshape(each * length, width)
+            pre = jnp.dot(rows, w_ref[:, cols], preferred_element_type=F32) + b_ref[:, cols]
+            logistic = 0.5 * jnp.tanh(0.5 * pre) + 0.5
+            act = pre * logistic
+            slope = (logistic + act * (1.0 - logistic)).astype(BF16)
+            slope_ref[m : m + each, :, cols] = slope.reshape(each, length, step)
+            act = act.astype(BF16)
+            act_ref[m : m + each, :, cols] = act.reshape(each, length, step)
+            line = lax.dot_general(
+                wout_ref[:, cols], act, (((1,), (1,)), ((), ())), preferred_element_type=F32
+            )
+            lines[m] = line if lines[m] is None else lines[m] + line
+    first = lines[0][:, :length].astype(BF16)
+    send_ref[0] = first
+    base = first.astype(F32)
+    for m in starts:
         for i in range(each):
-            send_ref[1 + m + i] = (line[:, i * length : (i + 1) * length] - base).astype(BF16)
+            line = lines[m][:, i * length : (i + 1) * length]
+            send_ref[1 + m + i] = (line - base).astype(BF16)
 
 
 def first_kernel(
@@ -84,24 +93,41 @@
         x_copies.append(
             pltpu.make_async_copy(x_hbm.at[:, cells, :], x_ref.at[:, cells, :], x_sems.at[s])
         )
-    copies = [
+    half = w_ref.shape[1] // 2
+    w_copies = []
+    for i in range(2):
+        cols = slice(i * half, (i + 1) * half)
+        w_copies.append(pltpu.make_async_copy(w_hbm.at[:, cols], w_ref.at[:, cols], sems.at[2 + i]))
+    small = [
         pltpu.make_async_copy(b_hbm, b_ref, sems.at[0]),
-        pltpu.make_async_copy(w_hbm, w_ref, sems.at[1]),
-        pltpu.make_async_copy(wout_hbm, wout_ref, sems.at[2]),
+        pltpu.make_async_copy(wout_hbm, wout_ref, sems.at[1]),
     ]
-    for copy in copies[:2] + x_copies[:1] + copies[2:]:
+    early = small + w_copies[:1] + x_copies[:1]
+    for copy in early + w_copies[1:]:
         copy.start()
-    for copy in copies + x_copies[:1]:
-        copy.wait()
-    for copy in x_copies[1:]:
-        copy.start()
-    cells_forward(turn, place, pieces, x_ref, w_ref, b_ref, wout_ref, act_ref, slope_ref, send_ref)
+
+    def first_half():
+        for copy in early:
+            copy.wait()
+        for copy in x_copies[1:]:
+            copy.start()
+
+    def second_half():
+        w_copies[1].wait()
+
+    cells_forward(
+        turn, place, pieces, x_ref, w_ref, b_ref, wout_ref, act_ref, slope_ref, send_ref,
+        [first_half, second_half],
+    )
     for copy in x_copies[1:]:
         copy.wait()
 
 
 def later_kernel(turn, pieces, place, x_ref, w_ref, b_ref, wout_ref, act_ref, slope_ref, send_ref):
-    cells_forward(turn, place, pieces, x_ref, w_ref, b_ref, wout_ref, act_ref, slope_ref, send_ref)
+    cells_forward(
+        turn, place, pieces, x_ref, w_ref, b_ref, wout_ref, act_ref, slope_ref, send_ref,
+        [lambda: None],
+    )
 
 
 def forward(grid_input, w_hidden, b_hidden, w_out_t, place, pieces):
@@ -123,7 +149,7 @@
             pltpu.VMEM(w_out_t.shape, BF16),
         ]
         + results,
-        scratch_shapes=[pltpu.SemaphoreType.DMA((pieces,)), pltpu.SemaphoreType.DMA((3,))],
+        scratch_shapes=[pltpu.SemaphoreType.DMA((pieces,)), pltpu.SemaphoreType.DMA((4,))],
         compiler_params=params(),
         cost_estimate=estimate,
         name="forward",

time: 88.2 us -> 88.9 us (level)
  transfers between devices with their start and end apart: 22 -> 22, of which waited for: 7 -> 7; matrix products, arithmetic and copies ran while one was open for 0% -> 0% of each run, Pallas kernels for 34% -> 33%
where the time goes in v5:
time: 88.9 us; the launch traced here: 88.7 us
  Pallas kernels  37.7 us (42%)
  starting transfers between devices  28.4 us (32%)
  waiting for transfers between devices  21.5 us (24%)
  between operations  0.93 us (1%)
    ppermute x13, starting transfers between devices, shifted(): lax.ppermute(block, axis, [((i - distance) % count, i) for i in range(cou...  19.5 us
    ppermute x6, waiting for transfers between devices, exchanged(): return lax.ppermute(block, axis, [(i, i ^ bit) for i in range(count)])  12.3 us
    ppermute x13, waiting for transfers between devices, shifted(): lax.ppermute(block, axis, [((i - distance) % count, i) for i in range(cou...  9.19 us
    pallas_call x3, Pallas kernels, forward(): pl.pallas_call(functools.partial(later_kernel, turn, pieces), in_specs=[O...  7.6 us
    ppermute x6, starting transfers between devices, exchanged(): return lax.ppermute(block, axis, [(i, i ^ bit) for i in range(count)])  7.2 us
    pallas_call x2, Pallas kernels, weights(): pl.pallas_call(functools.partial(weights_kernel, turns, groups, cores, co...  7.08 us
    pallas_call x2, Pallas kernels, backward(): pl.pallas_call(functools.partial(backward_kernel, first, pieces), in_spec...  6.16 us
    pallas_call x1, Pallas kernels, forward(): pl.pallas_call(functools.partial(first_kernel, turns[0], pieces), in_spec...  5.18 us
  transfers between devices with their start and end apart: 22, of which 7 were waited for; matrix products, arithmetic and copies ran while one was open for 0% of the time, Pallas kernels for 33%

profile of v5, /device:TPU:3, one launch (start us, length us, event | category | flops | bytes accessed | tf_op | source)
XLA Modules:
  0.0 88.7 jit_solution(17383193168286764159)
XLA Ops:
  0.6 0.1 pad_add_fusion.place
  0.7 5.2 %forward.4 = (bf16[4,512,1024]{2,1,0:T(8,128)(2,1)S(1)}, bf16[1024,1024]{1,0:T(8,128)(2,1)S(1)}, f32[1,1024]{1,0:T(1,128)S(1)}, bf16[96,1024]{1,0:T(8,128)(2,1)S...) custom-call(s32[2]{0:T(128)S(1)} %pad_add_fusion.place, ...), custom_call_target="tpu_custom_call" | custom-call | flops 1000 | bytes 1000 | tf_op jit(solution)/shard_map/forward/pallas_call | solution.py:141
  5.9 2.4 %collective-permute-start.1 = (bf16[5,96,128]{2,1,0:T(8,128)(2,1)S(1)}, bf16[5,96,128]{2,1,0:T(8,128)(2,1)S(1)}, u32[]{:S(2)}, u32[]{:S(2)}) collective-permute-start(bf16[5,96,128]{2,1,0:T(8,128)(2,1)S(1)} %get-tuple-element.84), channel_id=1, source_target_pairs={{16,0},{24,8},{0,16},{8,24},{17,1},{25,9},{1,17},{9,25},{18,2},{26... | collective-permute-start | bytes 368648 | tf_op jit(solution)/shard_map/ppermute | solution.py:24
  8.3 2.5 %forward.5 = (bf16[4,128,1024]{2,1,0:T(8,128)(2,1)S(1)}, bf16[4,128,1024]{2,1,0:T(8,128)(2,1)S(1)}, bf16[5,96,128]{2,1,0:T(8,128)(2,1)S(1)}) custom-call(s32[2]{0:T(128)S(1)} %pad_add_fusion.place, bf16[4,512,1024]{2,1,0:T(8,128)(2,1)S(1)} %get-tuple-element.81.x_ref.refs_0_, bf16[1024,1024]{1,0:T(8,128)(2,1)S(1)} %get-tuple-element.82.w_ref, ...), custom_call_target="tpu_custom_call" | custom-call | flops 1000 | bytes 1000 | tf_op jit(solution)/shard_map/forward/pallas_call | solution.py:160
  10.8 1.4 %collective-permute-start = (bf16[5,96,128]{2,1,0:T(8,128)(2,1)S(1)}, bf16[5,96,128]{2,1,0:T(8,128)(2,1)S(1)}, u32[]{:S(2)}, u32[]{:S(2)}) collective-permute-start(bf16[5,96,128]{2,1,0:T(8,128)(2,1)S(1)} %get-tuple-element.87), channel_id=1, source_target_pairs={{24,0},{0,8},{8,16},{16,24},{25,1},{1,9},{9,17},{17,25},{26,2},{2,... | collective-permute-start | bytes 368648 | tf_op jit(solution)/shard_map/ppermute | solution.py:24
  12.2 2.5 %forward.6 = (bf16[4,128,1024]{2,1,0:T(8,128)(2,1)S(1)}, bf16[4,128,1024]{2,1,0:T(8,128)(2,1)S(1)}, bf16[5,96,128]{2,1,0:T(8,128)(2,1)S(1)}) custom-call(s32[2]{0:T(128)S(1)} %pad_add_fusion.place, bf16[4,512,1024]{2,1,0:T(8,128)(2,1)S(1)} %get-tuple-element.81.x_ref.refs_0_, bf16[1024,1024]{1,0:T(8,128)(2,1)S(1)} %get-tuple-element.82.w_ref, ...), custom_call_target="tpu_custom_call" | custom-call | flops 1000 | bytes 1000 | tf_op jit(solution)/shard_map/forward/pallas_call | solution.py:160
  14.7 0.0 copy-start
  14.7 0.0 copy-start.2
  14.7 2.0 %collective-permute-start.2 = (bf16[5,96,128]{2,1,0:T(8,128)(2,1)S(1)}, bf16[5,96,128]{2,1,0:T(8,128)(2,1)S(1)}, u32[]{:S(2)}, u32[]{:S(2)}) collective-permute-start(bf16[5,96,128]{2,1,0:T(8,128)(2,1)S(1)} %get-tuple-element.89), channel_id=1, source_target_pairs={{8,0},{16,8},{24,16},{0,24},{9,1},{17,9},{25,17},{1,25},{10,2},{18... | collective-permute-start | bytes 368648 | tf_op jit(solution)/shard_map/ppermute | solution.py:24
  16.7 2.5 %forward.7 = (bf16[4,128,1024]{2,1,0:T(8,128)(2,1)S(1)}, bf16[4,128,1024]{2,1,0:T(8,128)(2,1)S(1)}, bf16[5,96,128]{2,1,0:T(8,128)(2,1)S(1)}) custom-call(s32[2]{0:T(128)S(1)} %pad_add_fusion.place, bf16[4,512,1024]{2,1,0:T(8,128)(2,1)S(1)} %get-tuple-element.81.x_ref.refs_0_, bf16[1024,1024]{1,0:T(8,128)(2,1)S(1)} %get-tuple-element.82.w_ref, ...), custom_call_target="tpu_custom_call" | custom-call | flops 1000 | bytes 1000 | tf_op jit(solution)/shard_map/forward/pallas_call | solution.py:160
  19.3 0.0 copy-start.1
  19.3 1.5 %tiles.1 = (bf16[512,512]{1,0:T(8,128)(2,1)S(1)}, bf16[256,512]{1,0:T(8,128)(2,1)S(1)}, bf16[1024,1024]{1,0:T(8,128)(2,1)S(1)}) custom-call(s32[2]{0:T(128)S(1)} %pad_add_fusion.place, s32[4,3]{1,0:T(4,128)S(1)} %copy-done.2, bf16[4,3,128,128]{3,2,1,0:T(8,128)(2,1)S(1)} %copy-done, bf16[1024,1024]{1,0:T(8,128)(2,1)S(1)} %get-tuple-element.82.w_ref), custom_call_target="tpu_custom_call" | custom-call | flops 4000000 | bytes 2097152 | tf_op jit(solution)/shard_map/tiles/pallas_call | solution.py:259
  20.9 2.4 %score.1 = (bf16[1,96,128]{2,1,0:T(8,128)(2,1)S(1)}, bf16[1,96,128]{2,1,0:T(8,128)(2,1)S(1)}, bf16[1,96,128]{2,1,0:T(8,128)(2,1)S(1)}, bf16[1,96,128]{2,1,0:T(8,...) custom-call(s32[2]{0:T(128)S(1)} %pad_add_fusion.place, ...), custom_call_target="tpu_custom_call" | custom-call | flops 40000000 | bytes 1048576 | tf_op jit(solution)/shard_map/score/pallas_call | solution.py:226
  23.3 1.4 %collective-permute-start.3 = (bf16[1,96,128]{2,1,0:T(8,128)(2,1)S(1)}, bf16[1,96,128]{2,1,0:T(8,128)(2,1)S(1)}, u32[]{:S(2)}, u32[]{:S(2)}) collective-permute-start(bf16[1,96,128]{2,1,0:T(8,128)(2,1)S(1)} %get-tuple-element.103), channel_id=1, source_target_pairs={{8,0},{16,8},{24,16},{0,24},{9,1},{17,9},{25,17},{1,25},{10,2},{18... | collective-permute-start | bytes 73736 | tf_op jit(solution)/shard_map/ppermute | solution.py:24
  24.7 0.4 collective-permute-start.5
  25.0 2.9 %collective-permute-start.6 = (bf16[3,96,128]{2,1,0:T(8,128)(2,1)S(1)}, bf16[3,96,128]{2,1,0:T(8,128)(2,1)S(1)}, u32[]{:S(2)}, u32[]{:S(2)}) collective-permute-start(bf16[3,96,128]{2,1,0:T(8,128)(2,1)S(1)} %get-tuple-element.112), channel_id=1, source_target_pairs={{8,0},{16,8},{24,16},{0,24},{9,1},{17,9},{25,17},{1,25},{10,2},{18... | collective-permute-start | bytes 221192 | tf_op jit(solution)/shard_map/ppermute | solution.py:24
  28.0 0.6 collective-permute-start.7
  28.5 0.1 collective-permute-start.8
  28.6 0.6 collective-permute-done.5.refs_3_
  29.3 1.9 %backward.2 = (bf16[1,512,96]{2,1,0:T(8,128)(2,1)S(1)}, bf16[1,512,1024]{2,1,0:T(8,128)(2,1)S(1)}, bf16[1,256,1024]{2,1,0:T(8,128)(2,1)S(1)}, bf16[1,256,1024]{2,1,0:T(8,128)(2,1)S(1)}) custom-call(s32[2]{0:T(128)S(1)} %pad_add_fusion.place, bf16[96,1024]{1,0:T(8,128)(2,1)S(1)} %get-tuple-element.86.wout_ref, ...), custom_call_target="tpu_custom_call" | custom-call | flops 1073741824 | bytes 5242880 | tf_op jit(solution)/shard_map/backward/pallas_call | solution.py:304
  31.2 5.0 %collective-permute-start.10 = (bf16[1,256,1024]{2,1,0:T(8,128)(2,1)S(1)}, bf16[1,256,1024]{2,1,0:T(8,128)(2,1)S(1)}, u32[]{:S(2)}, u32[]{:S(2)}) collective-permute-start(bf16[1,256,1024]{2,1,0:T(8,128)(2,1)S(1)} %get-tuple-element.130), channel_id=1, source_target_pairs={{7,0},{0,1},{1,2},{2,3},{3,4},{4,5},{5,6},{6,7},{15,8},{8,9},{9,10... | collective-permute-start | bytes 1572872 | tf_op jit(solution)/shard_map/ppermute | solution.py:24
  36.2 4.2 %backward.3 = (bf16[3,512,96]{2,1,0:T(8,128)(2,1)S(1)}, bf16[3,512,1024]{2,1,0:T(8,128)(2,1)S(1)}, bf16[3,256,1024]{2,1,0:T(8,128)(2,1)S(1)}, bf16[3,256,1024]{2,1,0:T(8,128)(2,1)S(1)}) custom-call(s32[2]{0:T(128)S(1)} %pad_add_fusion.place, bf16[96,1024]{1,0:T(8,128)(2,1)S(1)} %get-tuple-element.86.wout_ref, ...), custom_call_target="tpu_custom_call" | custom-call | flops 3221225472 | bytes 5242880 | tf_op jit(solution)/shard_map/backward/pallas_call | solution.py:304
  40.5 3.4 %collective-permute-start.20 = (bf16[3,256,1024]{2,1,0:T(8,128)(2,1)S(1)}, bf16[3,256,1024]{2,1,0:T(8,128)(2,1)S(1)}, u32[]{:S(2)}, u32[]{:S(2)}) collective-permute-start(bf16[3,256,1024]{2,1,0:T(8,128)(2,1)S(1)} %get-tuple-element.156), channel_id=1, source_target_pairs={{7,0},{0,1},{1,2},{2,3},{3,4},{4,5},{5,6},{6,7},{15,8},{8,9},{9,10... | collective-permute-start | bytes 4718600 | tf_op jit(solution)/shard_map/ppermute | solution.py:24
  43.9 5.0 %weights.3 = (bf16[12,32,1120]{2,1,0:T(8,128)(2,1)S(1)}, bf16[12,32,1120]{2,1,0:T(8,128)(2,1)S(1)}) custom-call(s32[2]{0:T(128)S(1)} %pad_add_fusion.place, bf16[4,512,1024]{2,1,0:T(8,128)(2,1)S(1)} %get-tuple-element.81.x_ref.refs_0_, bf16[4,128,1024]{2,1,0:T(8,128)(2,1)S(1)} %get-tuple-element.91.refs_1_, ...), custom_call_target="tpu_custom_call" | custom-call | flops 1000 | bytes 1000 | tf_op jit(solution)/shard_map/weights/pallas_call | solution.py:390
  48.8 2.6 %collective-permute-done.11.down_ref = bf16[1,256,1024]{2,1,0:T(8,128)(2,1)S(1)} collective-permute-done((bf16[1,256,1024]{2,1,0:T(8,128)(2,1)S(1)}, bf16[1,256,1024]{2,1,0:T(8,128)(2,1)S(1)}, u32[]{:S(2)}, u32[]{:S(2)}) %collective-permute-start.11) | collective-permute-done | bytes 524320 | tf_op jit(solution)/shard_map/ppermute | solution.py:24
  51.4 2.4 %collective-permute-done.12.came_ref = bf16[12,32,1120]{2,1,0:T(8,128)(2,1)S(1)} collective-permute-done((bf16[12,32,1120]{2,1,0:T(8,128)(2,1)S(1)}, bf16[12,32,1120]{2,1,0:T(8,128)(2,1)S(1)}, u32[]{:S(2)}, u32[]{:S(2)}) %collective-permute-start.12) | collective-permute-done | bytes 860192 | tf_op jit(solution)/shard_map/ppermute | solution.py:29
  53.8 0.2 pairs.2
  54.0 1.3 %collective-permute-start.13 = (bf16[4,32,1120]{2,1,0:T(8,128)(2,1)S(1)}, bf16[4,32,1120]{2,1,0:T(8,128)(2,1)S(1)}, u32[]{:S(2)}, u32[]{:S(2)}) collective-permute-start(bf16[4,32,1120]{2,1,0:T(8,128)(2,1)S(1)} %get-tuple-element.134), channel_id=1, source_target_pairs={{0,8},{8,0},{16,24},{24,16},{1,9},{9,1},{17,25},{25,17},{2,10},{10... | collective-permute-start | bytes 860168 | tf_op jit(solution)/shard_map/ppermute | solution.py:29
  55.4 1.7 %collective-permute-start.14 = (bf16[4,32,1120]{2,1,0:T(8,128)(2,1)S(1)}, bf16[4,32,1120]{2,1,0:T(8,128)(2,1)S(1)}, u32[]{:S(2)}, u32[]{:S(2)}) collective-permute-start(bf16[4,32,1120]{2,1,0:T(8,128)(2,1)S(1)} %get-tuple-element.135), channel_id=1, source_target_pairs={{0,16},{8,24},{16,0},{24,8},{1,17},{9,25},{17,1},{25,9},{2,18},{10... | collective-permute-start | bytes 860168 | tf_op jit(solution)/shard_map/ppermute | solution.py:29
  57.1 2.1 %weights.2 = (bf16[4,32,1120]{2,1,0:T(8,128)(2,1)S(1)}, bf16[4,32,1120]{2,1,0:T(8,128)(2,1)S(1)}) custom-call(s32[2]{0:T(128)S(1)} %pad_add_fusion.place, bf16[4,512,1024]{2,1,0:T(8,128)(2,1)S(1)} %get-tuple-element.81.x_ref.refs_0_, bf16[4,128,1024]{2,1,0:T(8,128)(2,1)S(1)} %get-tuple-element.91.refs_1_, ...), custom_call_target="tpu_custom_call" | custom-call | flops 1000 | bytes 1000 | tf_op jit(solution)/shard_map/weights/pallas_call | solution.py:390
  59.2 0.8 collective-permute-start.9
  60.0 8.0 %collective-permute-done.13.near_came.near = bf16[4,32,1120]{2,1,0:T(8,128)(2,1)S(1)} collective-permute-done((bf16[4,32,1120]{2,1,0:T(8,128)(2,1)S(1)}, bf16[4,32,1120]{2,1,0:T(8,128)(2,1)S(1)}, u32[]{:S(2)}, u32[]{:S(2)}) %collective-permute-start.13) | collective-permute-done | bytes 286752 | tf_op jit(solution)/shard_map/ppermute | solution.py:29
  68.0 0.1 pairs.3
  68.1 3.1 %collective-permute-start.15 = (bf16[2,32,1120]{2,1,0:T(8,128)(2,1)S(1)}, bf16[2,32,1120]{2,1,0:T(8,128)(2,1)S(1)}, u32[]{:S(2)}, u32[]{:S(2)}) collective-permute-start(bf16[2,32,1120]{2,1,0:T(8,128)(2,1)S(1)} %get-tuple-element.138), channel_id=1, source_target_pairs={{0,16},{8,24},{16,0},{24,8},{1,17},{9,25},{17,1},{25,9},{2,18},{10... | collective-permute-start | bytes 430088 | tf_op jit(solution)/shard_map/ppermute | solution.py:29
  71.3 0.2 collective-permute-start.16
  71.5 0.1 add.3.own
  71.5 0.4 own.2.own_ref
  72.0 1.0 %own.3.own_ref = f32[3,256,1024]{2,1,0:T(8,128)S(1)} custom-call(bf16[256,512]{1,0:T(8,128)(2,1)S(1)} %get-tuple-element.140.tiles_ref, bf16[3,512,1024]{2,1,0:T(8,128)(2,1)S(1)} %get-tuple-element.142.refs_6_.dpre_ref), custom_call_target="tpu_custom_call" | custom-call | flops 1000 | bytes 1000 | tf_op jit(solution)/shard_map/own/pallas_call | solution.py:327
  73.0 1.7 %finish.2.refs_0_ = f32[4,256,1024]{2,1,0:T(8,128)} custom-call(f32[1,256,1024]{2,1,0:T(8,128)S(1)} %own.2.own_ref, bf16[1,256,1024]{2,1,0:T(8,128)(2,1)S(1)} %collective-permute-done.10.up_ref, bf16[1,256,1024]{2,1,0:T(8,128)(2,1)S(1)} %collective-permute-done.11.down_ref, bf16[1024,1024]{1,0:T(8,128)(2,1)S(1)} %get-tuple-element.143.w_ref), custom_call_target="tpu_custom_call" | custom-call | flops 1000 | bytes 1000 | tf_op jit(solution)/shard_map/finish/pallas_call | solution.py:558
  74.8 1.8 %collective-permute-done.16.far_last = bf16[2,32,1120]{2,1,0:T(8,128)(2,1)S(1)} collective-permute-done((bf16[2,32,1120]{2,1,0:T(8,128)(2,1)S(1)}, bf16[2,32,1120]{2,1,0:T(8,128)(2,1)S(1)}, u32[]{:S(2)}, u32[]{:S(2)}) %collective-permute-start.16) | collective-permute-done | bytes 143392 | tf_op jit(solution)/shard_map/ppermute | solution.py:29
  76.6 0.7 chips.1
  77.3 0.7 collective-permute-start.17
  78.0 0.1 collective-permute-start.18
  78.1 1.0 %collective-permute-start.19 = (bf16[1,32,1120]{2,1,0:T(8,128)(2,1)S(1)}, bf16[1,32,1120]{2,1,0:T(8,128)(2,1)S(1)}, u32[]{:S(2)}, u32[]{:S(2)}) collective-permute-start(bf16[1,32,1120]{2,1,0:T(8,128)(2,1)S(1)} %get-tuple-element.152), channel_id=1, source_target_pairs={{0,6},{1,7},{2,0},{3,1},{4,2},{5,3},{6,4},{7,5},{8,14},{9,15},{10,... | collective-permute-start | bytes 215048 | tf_op jit(solution)/shard_map/ppermute | solution.py:539
  79.1 1.8 %collective-permute-done.20.up_ref = bf16[3,256,1024]{2,1,0:T(8,128)(2,1)S(1)} collective-permute-done((bf16[3,256,1024]{2,1,0:T(8,128)(2,1)S(1)}, bf16[3,256,1024]{2,1,0:T(8,128)(2,1)S(1)}, u32[]{:S(2)}, u32[]{:S(2)}) %collective-permute-start.20) | collective-permute-done | bytes 1572896 | tf_op jit(solution)/shard_map/ppermute | solution.py:24
  80.9 4.2 %collective-permute-done.21.down_ref = bf16[3,256,1024]{2,1,0:T(8,128)(2,1)S(1)} collective-permute-done((bf16[3,256,1024]{2,1,0:T(8,128)(2,1)S(1)}, bf16[3,256,1024]{2,1,0:T(8,128)(2,1)S(1)}, u32[]{:S(2)}, u32[]{:S(2)}) %collective-permute-start.21) | collective-permute-done | bytes 1572896 | tf_op jit(solution)/shard_map/ppermute | solution.py:24
  85.0 2.9 %finish.3 = f32[4,256,1024]{2,1,0:T(8,128)} custom-call(f32[3,256,1024]{2,1,0:T(8,128)S(1)} %own.3.own_ref, bf16[3,256,1024]{2,1,0:T(8,128)(2,1)S(1)} %collective-permute-done.20.up_ref, bf16[3,256,1024]{2,1,0:T(8,128)(2,1)S(1)} %collective-permute-done.21.down_ref, bf16[1024,1024]{1,0:T(8,128)(2,1)S(1)} %get-tuple-element.143.w_ref, ...), custom_call_target="tpu_custom_call", output_to_operand_aliasing={{}: (4, {})} | custom-call | flops 1000 | bytes 1000 | tf_op jit(solution)/shard_map/finish/pallas_call | solution.py:558
  88.0 0.7 total.1
  (26 shorter events, 0.1 us)
Async XLA Ops:
  5.9 14.9 %collective-permute-start.1 = (bf16[5,96,128]{2,1,0:T(8,128)(2,1)S(1)}, bf16[5,96,128]{2,1,0:T(8,128)(2,1)S(1)}, u32[]{:S(2)}, u32[]{:S(2)}) collective-permute-start(bf16[5,96,128]{2,1,0:T(8,128)(2,1)S(1)} %get-tuple-element.84), channel_id=1, source_target_pairs={{16,0},{24,8},{0,16},{8,24},{17,1},{25,9},{1,17},{9,25},{18,2},{26... | collective-permute-start | bytes 368648 | tf_op jit(solution)/shard_map/ppermute | solution.py:24
  10.8 10.0 %collective-permute-start = (bf16[5,96,128]{2,1,0:T(8,128)(2,1)S(1)}, bf16[5,96,128]{2,1,0:T(8,128)(2,1)S(1)}, u32[]{:S(2)}, u32[]{:S(2)}) collective-permute-start(bf16[5,96,128]{2,1,0:T(8,128)(2,1)S(1)} %get-tuple-element.87), channel_id=1, source_target_pairs={{24,0},{0,8},{8,16},{16,24},{25,1},{1,9},{9,17},{17,25},{26,2},{2,... | collective-permute-start | bytes 368648 | tf_op jit(solution)/shard_map/ppermute | solution.py:24
  14.7 4.6 %copy-start = (bf16[4,3,128,128]{3,2,1,0:T(8,128)(2,1)S(1)}, bf16[4,3,128,128]{3,2,1,0:T(8,128)(2,1)}, u32[]{:S(2)}) copy-start(bf16[4,3,128,128]{3,2,1,0:T(8,128)(2,1)} %tile_ref.1) | copy-start | bytes 1179652
  14.7 4.6 %copy-start.2 = (s32[4,3]{1,0:T(4,128)S(1)}, s32[4,3]{1,0:T(4,128)}, u32[]{:S(2)}) copy-start(s32[4,3]{1,0:T(4,128)} %index_ref.1) | copy-start | bytes 148
  14.7 6.1 %collective-permute-start.2 = (bf16[5,96,128]{2,1,0:T(8,128)(2,1)S(1)}, bf16[5,96,128]{2,1,0:T(8,128)(2,1)S(1)}, u32[]{:S(2)}, u32[]{:S(2)}) collective-permute-start(bf16[5,96,128]{2,1,0:T(8,128)(2,1)S(1)} %get-tuple-element.89), channel_id=1, source_target_pairs={{8,0},{16,8},{24,16},{0,24},{9,1},{17,9},{25,17},{1,25},{10,2},{18... | collective-permute-start | bytes 368648 | tf_op jit(solution)/shard_map/ppermute | solution.py:24
  19.3 1.6 %copy-start.1 = (f32[96,512]{1,0:T(8,128)S(1)}, f32[96,512]{1,0:T(8,128)}, u32[]{:S(2)}) copy-start(f32[96,512]{1,0:T(8,128)} %target_ref.1) | copy-start | bytes 589828
  19.3 1.6 %copy-start.3 = (f32[96]{0:T(128)S(1)}, f32[96]{0:T(128)}, u32[]{:S(2)}) copy-start(f32[96]{0:T(128)} %param.13) | copy-start | bytes 1156
  19.3 1.6 %copy-start.4 = (f32[96]{0:T(128)S(1)}, f32[96]{0:T(128)}, u32[]{:S(2)}) copy-start(f32[96]{0:T(128)} %param.15) | copy-start | bytes 1156
  23.3 5.3 %collective-permute-start.3 = (bf16[1,96,128]{2,1,0:T(8,128)(2,1)S(1)}, bf16[1,96,128]{2,1,0:T(8,128)(2,1)S(1)}, u32[]{:S(2)}, u32[]{:S(2)}) collective-permute-start(bf16[1,96,128]{2,1,0:T(8,128)(2,1)S(1)} %get-tuple-element.103), channel_id=1, source_target_pairs={{8,0},{16,8},{24,16},{0,24},{9,1},{17,9},{25,17},{1,25},{10,2},{18... | collective-permute-start | bytes 73736 | tf_op jit(solution)/shard_map/ppermute | solution.py:24
  24.7 3.9 %collective-permute-start.4 = (bf16[1,96,128]{2,1,0:T(8,128)(2,1)S(1)}, bf16[1,96,128]{2,1,0:T(8,128)(2,1)S(1)}, u32[]{:S(2)}, u32[]{:S(2)}) collective-permute-start(bf16[1,96,128]{2,1,0:T(8,128)(2,1)S(1)} %get-tuple-element.104), channel_id=1, source_target_pairs={{16,0},{24,8},{0,16},{8,24},{17,1},{25,9},{1,17},{9,25},{18,2},{26... | collective-permute-start | bytes 73736 | tf_op jit(solution)/shard_map/ppermute | solution.py:24
  24.7 4.6 %collective-permute-start.5 = (bf16[1,96,128]{2,1,0:T(8,128)(2,1)S(1)}, bf16[1,96,128]{2,1,0:T(8,128)(2,1)S(1)}, u32[]{:S(2)}, u32[]{:S(2)}) collective-permute-start(bf16[1,96,128]{2,1,0:T(8,128)(2,1)S(1)} %get-tuple-element.105), channel_id=1, source_target_pairs={{24,0},{0,8},{8,16},{16,24},{25,1},{1,9},{9,17},{17,25},{26,2},{2,... | collective-permute-start | bytes 73736 | tf_op jit(solution)/shard_map/ppermute | solution.py:24
  25.0 11.2 %collective-permute-start.6 = (bf16[3,96,128]{2,1,0:T(8,128)(2,1)S(1)}, bf16[3,96,128]{2,1,0:T(8,128)(2,1)S(1)}, u32[]{:S(2)}, u32[]{:S(2)}) collective-permute-start(bf16[3,96,128]{2,1,0:T(8,128)(2,1)S(1)} %get-tuple-element.112), channel_id=1, source_target_pairs={{8,0},{16,8},{24,16},{0,24},{9,1},{17,9},{25,17},{1,25},{10,2},{18... | collective-permute-start | bytes 221192 | tf_op jit(solution)/shard_map/ppermute | solution.py:24
  28.0 8.3 %collective-permute-start.7 = (bf16[3,96,128]{2,1,0:T(8,128)(2,1)S(1)}, bf16[3,96,128]{2,1,0:T(8,128)(2,1)S(1)}, u32[]{:S(2)}, u32[]{:S(2)}) collective-permute-start(bf16[3,96,128]{2,1,0:T(8,128)(2,1)S(1)} %get-tuple-element.113), channel_id=1, source_target_pairs={{16,0},{24,8},{0,16},{8,24},{17,1},{25,9},{1,17},{9,25},{18,2},{26... | collective-permute-start | bytes 221192 | tf_op jit(solution)/shard_map/ppermute | solution.py:24
  28.5 7.7 %collective-permute-start.8 = (bf16[3,96,128]{2,1,0:T(8,128)(2,1)S(1)}, bf16[3,96,128]{2,1,0:T(8,128)(2,1)S(1)}, u32[]{:S(2)}, u32[]{:S(2)}) collective-permute-start(bf16[3,96,128]{2,1,0:T(8,128)(2,1)S(1)} %get-tuple-element.114), channel_id=1, source_target_pairs={{24,0},{0,8},{8,16},{16,24},{25,1},{1,9},{9,17},{17,25},{26,2},{2,... | collective-permute-start | bytes 221192 | tf_op jit(solution)/shard_map/ppermute | solution.py:24
  31.2 17.6 %collective-permute-start.10 = (bf16[1,256,1024]{2,1,0:T(8,128)(2,1)S(1)}, bf16[1,256,1024]{2,1,0:T(8,128)(2,1)S(1)}, u32[]{:S(2)}, u32[]{:S(2)}) collective-permute-start(bf16[1,256,1024]{2,1,0:T(8,128)(2,1)S(1)} %get-tuple-element.130), channel_id=1, source_target_pairs={{7,0},{0,1},{1,2},{2,3},{3,4},{4,5},{5,6},{6,7},{15,8},{8,9},{9,10... | collective-permute-start | bytes 1572872 | tf_op jit(solution)/shard_map/ppermute | solution.py:24
  36.2 15.2 %collective-permute-start.11 = (bf16[1,256,1024]{2,1,0:T(8,128)(2,1)S(1)}, bf16[1,256,1024]{2,1,0:T(8,128)(2,1)S(1)}, u32[]{:S(2)}, u32[]{:S(2)}) collective-permute-start(bf16[1,256,1024]{2,1,0:T(8,128)(2,1)S(1)} %get-tuple-element.131), channel_id=1, source_target_pairs={{1,0},{2,1},{3,2},{4,3},{5,4},{6,5},{7,6},{0,7},{9,8},{10,9},{11,1... | collective-permute-start | bytes 1572872 | tf_op jit(solution)/shard_map/ppermute | solution.py:24
  40.5 40.4 %collective-permute-start.20 = (bf16[3,256,1024]{2,1,0:T(8,128)(2,1)S(1)}, bf16[3,256,1024]{2,1,0:T(8,128)(2,1)S(1)}, u32[]{:S(2)}, u32[]{:S(2)}) collective-permute-start(bf16[3,256,1024]{2,1,0:T(8,128)(2,1)S(1)} %get-tuple-element.156), channel_id=1, source_target_pairs={{7,0},{0,1},{1,2},{2,3},{3,4},{4,5},{5,6},{6,7},{15,8},{8,9},{9,10... | collective-permute-start | bytes 4718600 | tf_op jit(solution)/shard_map/ppermute | solution.py:24
  43.9 41.2 %collective-permute-start.21 = (bf16[3,256,1024]{2,1,0:T(8,128)(2,1)S(1)}, bf16[3,256,1024]{2,1,0:T(8,128)(2,1)S(1)}, u32[]{:S(2)}, u32[]{:S(2)}) collective-permute-start(bf16[3,256,1024]{2,1,0:T(8,128)(2,1)S(1)} %get-tuple-element.157), channel_id=1, source_target_pairs={{1,0},{2,1},{3,2},{4,3},{5,4},{6,5},{7,6},{0,7},{9,8},{10,9},{11,1... | collective-permute-start | bytes 4718600 | tf_op jit(solution)/shard_map/ppermute | solution.py:24
  51.4 2.4 %collective-permute-start.12 = (bf16[12,32,1120]{2,1,0:T(8,128)(2,1)S(1)}, bf16[12,32,1120]{2,1,0:T(8,128)(2,1)S(1)}, u32[]{:S(2)}, u32[]{:S(2)}) collective-permute-start(bf16[12,32,1120]{2,1,0:T(8,128)(2,1)S(1)} %get-tuple-element.133), channel_id=1, source_target_pairs={{0,1},{1,0},{2,3},{3,2},{4,5},{5,4},{6,7},{7,6},{8,9},{9,8},{10,11... | collective-permute-start | bytes 2580488 | tf_op jit(solution)/shard_map/ppermute | solution.py:29
  54.0 14.0 %collective-permute-start.13 = (bf16[4,32,1120]{2,1,0:T(8,128)(2,1)S(1)}, bf16[4,32,1120]{2,1,0:T(8,128)(2,1)S(1)}, u32[]{:S(2)}, u32[]{:S(2)}) collective-permute-start(bf16[4,32,1120]{2,1,0:T(8,128)(2,1)S(1)} %get-tuple-element.134), channel_id=1, source_target_pairs={{0,8},{8,0},{16,24},{24,16},{1,9},{9,1},{17,25},{25,17},{2,10},{10... | collective-permute-start | bytes 860168 | tf_op jit(solution)/shard_map/ppermute | solution.py:29
  55.4 12.7 %collective-permute-start.14 = (bf16[4,32,1120]{2,1,0:T(8,128)(2,1)S(1)}, bf16[4,32,1120]{2,1,0:T(8,128)(2,1)S(1)}, u32[]{:S(2)}, u32[]{:S(2)}) collective-permute-start(bf16[4,32,1120]{2,1,0:T(8,128)(2,1)S(1)} %get-tuple-element.135), channel_id=1, source_target_pairs={{0,16},{8,24},{16,0},{24,8},{1,17},{9,25},{17,1},{25,9},{2,18},{10... | collective-permute-start | bytes 860168 | tf_op jit(solution)/shard_map/ppermute | solution.py:29
  59.2 12.2 %collective-permute-start.9 = (bf16[4,32,1120]{2,1,0:T(8,128)(2,1)S(1)}, bf16[4,32,1120]{2,1,0:T(8,128)(2,1)S(1)}, u32[]{:S(2)}, u32[]{:S(2)}) collective-permute-start(bf16[4,32,1120]{2,1,0:T(8,128)(2,1)S(1)} %get-tuple-element.127), channel_id=1, source_target_pairs={{0,1},{1,0},{2,3},{3,2},{4,5},{5,4},{6,7},{7,6},{8,9},{9,8},{10,11... | collective-permute-start | bytes 860168 | tf_op jit(solution)/shard_map/ppermute | solution.py:29
  68.1 6.7 %collective-permute-start.15 = (bf16[2,32,1120]{2,1,0:T(8,128)(2,1)S(1)}, bf16[2,32,1120]{2,1,0:T(8,128)(2,1)S(1)}, u32[]{:S(2)}, u32[]{:S(2)}) collective-permute-start(bf16[2,32,1120]{2,1,0:T(8,128)(2,1)S(1)} %get-tuple-element.138), channel_id=1, source_target_pairs={{0,16},{8,24},{16,0},{24,8},{1,17},{9,25},{17,1},{25,9},{2,18},{10... | collective-permute-start | bytes 430088 | tf_op jit(solution)/shard_map/ppermute | solution.py:29
  71.3 5.4 %collective-permute-start.16 = (bf16[2,32,1120]{2,1,0:T(8,128)(2,1)S(1)}, bf16[2,32,1120]{2,1,0:T(8,128)(2,1)S(1)}, u32[]{:S(2)}, u32[]{:S(2)}) collective-permute-start(bf16[2,32,1120]{2,1,0:T(8,128)(2,1)S(1)} %get-tuple-element.139), channel_id=1, source_target_pairs={{0,8},{8,0},{16,24},{24,16},{1,9},{9,1},{17,25},{25,17},{2,10},{10... | collective-permute-start | bytes 430088 | tf_op jit(solution)/shard_map/ppermute | solution.py:29
  77.3 10.6 %collective-permute-start.17 = (bf16[1,32,1120]{2,1,0:T(8,128)(2,1)S(1)}, bf16[1,32,1120]{2,1,0:T(8,128)(2,1)S(1)}, u32[]{:S(2)}, u32[]{:S(2)}) collective-permute-start(bf16[1,32,1120]{2,1,0:T(8,128)(2,1)S(1)} %get-tuple-element.150), channel_id=1, source_target_pairs={{0,2},{1,3},{2,4},{3,5},{4,6},{5,7},{6,0},{7,1},{8,10},{9,11},{10,... | collective-permute-start | bytes 215048 | tf_op jit(solution)/shard_map/ppermute | solution.py:539
  78.0 10.0 %collective-permute-start.18 = (bf16[1,32,1120]{2,1,0:T(8,128)(2,1)S(1)}, bf16[1,32,1120]{2,1,0:T(8,128)(2,1)S(1)}, u32[]{:S(2)}, u32[]{:S(2)}) collective-permute-start(bf16[1,32,1120]{2,1,0:T(8,128)(2,1)S(1)} %get-tuple-element.151), channel_id=1, source_target_pairs={{0,4},{1,5},{2,6},{3,7},{4,0},{5,1},{6,2},{7,3},{8,12},{9,13},{10,... | collective-permute-start | bytes 215048 | tf_op jit(solution)/shard_map/ppermute | solution.py:539
  78.1 9.9 %collective-permute-start.19 = (bf16[1,32,1120]{2,1,0:T(8,128)(2,1)S(1)}, bf16[1,32,1120]{2,1,0:T(8,128)(2,1)S(1)}, u32[]{:S(2)}, u32[]{:S(2)}) collective-permute-start(bf16[1,32,1120]{2,1,0:T(8,128)(2,1)S(1)} %get-tuple-element.152), channel_id=1, source_target_pairs={{0,6},{1,7},{2,0},{3,1},{4,2},{5,3},{6,4},{7,5},{8,14},{9,15},{10,... | collective-permute-start | bytes 215048 | tf_op jit(solution)/shard_map/ppermute | solution.py:539
